TPU v7x, 32 devices: a whole 2x2x4 slice. The times are simulated.
32 devices in a mesh: dp: 8 (over z, x), section: 4 (over y, core).
Axes of the slice: x: 2, y: 2, z: 4, core: 2. Of those that a mesh axis runs over, the one named last changes fastest.
Arguments:
- inputs: bfloat16 [32, 248, 768], P('dp'), may hold values from -6 to 6
- out_grad: bfloat16 [32, 248, 768], P('dp'), may hold values from -6 to 6
- segment_ids: int32 [32, 248], P('dp'), may hold values from 0 to 3, never falling along the last dimension, each value on 1 to 124 neighbouring positions
- cls_index: int32 [32], P('dp'), may hold values from 0 to 247
- qkv_master: float32 [4, 768, 2304], P('section', 'dp'), may hold values from -0.21875 to 0.21875
- proj_master: float32 [4, 768, 768], P('section', 'dp'), may hold values from -0.875 to 0.875
- up_master: float32 [4, 768, 3072], P('section', 'dp'), may hold values from -0.21875 to 0.21875
- down_master: float32 [4, 3072, 768], P('section', 'dp'), may hold values from -0.109375 to 0.109375
- small_master: float32 [4, 9216], P('section', 'dp'), may hold values from -0.4 to 1.4, as said below
- qkv_first: float32 [4, 768, 2304], P('section', 'dp'), may hold values from -0.0012207031 to 0.0012207031
- proj_first: float32 [4, 768, 768], P('section', 'dp'), may hold values from -0.0012207031 to 0.0012207031
- up_first: float32 [4, 768, 3072], P('section', 'dp'), may hold values from -0.0012207031 to 0.0012207031
- down_first: float32 [4, 3072, 768], P('section', 'dp'), may hold values from -0.0012207031 to 0.0012207031
- small_first: float32 [4, 9216], P('section', 'dp'), may hold values from -0.0024414062 to 0.0024414062
- qkv_second: float32 [4, 768, 2304], P('section', 'dp'), may hold values from 3.5275338e-08 to 1.4110135e-07
- proj_second: float32 [4, 768, 768], P('section', 'dp'), may hold values from 3.5275338e-08 to 1.4110135e-07
- up_second: float32 [4, 768, 3072], P('section', 'dp'), may hold values from 3.5275338e-08 to 1.4110135e-07
- down_second: float32 [4, 3072, 768], P('section', 'dp'), may hold values from 3.5275338e-08 to 1.4110135e-07
- small_second: float32 [4, 9216], P('section', 'dp'), may hold values from 1.4110135e-07 to 5.644054e-07
Outputs:
- acts: bfloat16 [4, 32, 248, 768], P('section', 'dp')
- input_grads: bfloat16 [4, 32, 248, 768], P('section', 'dp')
- grad_norm: float32 [1], replicated
- qkv_grad: float32 [4, 768, 2304], P('section', 'dp')
- qkv_master_new: float32 [4, 768, 2304], P('section', 'dp')
- qkv_first_new: float32 [4, 768, 2304], P('section', 'dp')
- qkv_second_new: float32 [4, 768, 2304], P('section', 'dp')
- proj_grad: float32 [4, 768, 768], P('section', 'dp')
- proj_master_new: float32 [4, 768, 768], P('section', 'dp')
- proj_first_new: float32 [4, 768, 768], P('section', 'dp')
- proj_second_new: float32 [4, 768, 768], P('section', 'dp')
- up_grad: float32 [4, 768, 3072], P('section', 'dp')
- up_master_new: float32 [4, 768, 3072], P('section', 'dp')
- up_first_new: float32 [4, 768, 3072], P('section', 'dp')
- up_second_new: float32 [4, 768, 3072], P('section', 'dp')
- down_grad: float32 [4, 3072, 768], P('section', 'dp')
- down_master_new: float32 [4, 3072, 768], P('section', 'dp')
- down_first_new: float32 [4, 3072, 768], P('section', 'dp')
- down_second_new: float32 [4, 3072, 768], P('section', 'dp')
- small_grad: float32 [4, 9216], P('section', 'dp')
- small_master_new: float32 [4, 9216], P('section', 'dp')
- small_first_new: float32 [4, 9216], P('section', 'dp')
- small_second_new: float32 [4, 9216], P('section', 'dp')
Inputs may be any that keep to these rules, and one draw needn't show every extreme that they name: `segment_ids`: clip numbers never fall along a sequence; each clip covers 1 to 124 patches, and one covers exactly 124. `small_master`: gains lie near one, biases near zero.
All inputs are finite; a program needn't handle non-finite values.
Results may differ from a plain program's by a relative error of at most 0.018.
Values may be sent and summed in bfloat16 or wider, within the bound.
A program may use at most 768 MiB of HBM per device.

v0:
```python
from functools import partial

import jax
import jax.numpy as jnp
from jax import lax
from jax.sharding import PartitionSpec as P

HEADS = 12
MICRO = 4
STEP = 3


norm_eps = 1e-06
masked_score = -1e30
learn_rate = 0.05
small_rate = 0.3
decay_rate = 0.05
adam_eps = 1e-08


def from_behind(value, axis, by):
    length = lax.axis_size(axis)
    pairs = [(i, i + by) for i in range(length) if 0 <= i + by < length]
    return lax.ppermute(value, axis, pairs)


def layer_norm(values):
    center = values - jnp.mean(values, axis=-1, keepdims=True)
    spread = jnp.mean(center * center, axis=-1, keepdims=True)
    return center * lax.rsqrt(spread + norm_eps)


def norm_affine(values, gain, shift):
    return layer_norm(values) * gain + shift


def split_small(small, width, hidden_width, slices):
    share = width // slices
    stacked = small.reshape(slices, small.shape[0] // slices)
    pieces = [stacked[:, place * share : (place + 1) * share].reshape(width) for place in range(8)]
    pieces.append(stacked[:, 8 * share :].reshape(hidden_width))
    return pieces


def join_small(pieces, slices):
    sliced = [piece.reshape(slices, piece.shape[0] // slices) for piece in pieces]
    return jnp.concatenate(sliced, axis=1).reshape(-1)


def allowed_pairs(segment_ids, cls_rows):
    length = segment_ids.shape[1]
    places = lax.broadcasted_iota(jnp.int32, (1, length), 1)
    is_cls = places == cls_rows[:, None]
    same = segment_ids[:, :, None] == segment_ids[:, None, :]
    allowed = same | is_cls[:, :, None] | is_cls[:, None, :]
    return allowed[:, None, :, :]


def masked_scores(query, keys, allowed):
    scale = query.shape[-1] ** (-0.5)
    scores = jnp.einsum("nqhd,nkhd->nhqk", query, keys, preferred_element_type=jnp.float32) * scale
    return jnp.where(allowed, scores, masked_score)


def layer_forward(inputs, segment_ids, cls_rows, weights, slices):
    w_qkv, w_proj, w_up, w_down, small = weights
    count, length, width = inputs.shape
    hidden_width = w_up.shape[1]
    head_size = width // HEADS
    parts = split_small(small.astype(jnp.float32), width, hidden_width, slices)
    flat = inputs.reshape(count * length, width).astype(jnp.float32)
    normed = norm_affine(flat, parts[0], parts[1]).astype(jnp.bfloat16)
    mixed = jnp.dot(normed, w_qkv, preferred_element_type=jnp.float32)
    query = (mixed[:, :width] + parts[2]).astype(jnp.bfloat16)
    keys = mixed[:, width : 2 * width].astype(jnp.bfloat16)
    values = (mixed[:, 2 * width :] + parts[3]).astype(jnp.bfloat16)
    shape_heads = (count, length, HEADS, head_size)
    allowed = allowed_pairs(segment_ids, cls_rows)
    scores = masked_scores(query.reshape(shape_heads), keys.reshape(shape_heads), allowed)
    peak = jnp.max(scores, axis=-1, keepdims=True)
    raised = jnp.exp(scores - peak)
    summed = jnp.sum(raised, axis=-1, keepdims=True)
    soft_weights = (raised / summed).astype(jnp.bfloat16)
    logsum = peak + jnp.log(summed)
    attended = jnp.einsum(
        "nhqk,nkhd->nqhd",
        soft_weights,
        values.reshape(shape_heads),
        preferred_element_type=jnp.float32,
    )
    attended = attended.reshape(count * length, width).astype(jnp.bfloat16)
    hidden = flat + jnp.dot(attended, w_proj, preferred_element_type=jnp.float32) + parts[4]
    normed_two = norm_affine(hidden, parts[5], parts[6]).astype(jnp.bfloat16)
    inner = jnp.dot(normed_two, w_up, preferred_element_type=jnp.float32) + parts[8]
    active = jax.nn.gelu(inner, approximate=False).astype(jnp.bfloat16)
    output = hidden + jnp.dot(active, w_down, preferred_element_type=jnp.float32) + parts[7]
    kept = (flat, normed, query, keys, values, logsum, attended, hidden, normed_two, inner, active)
    return (output.astype(jnp.bfloat16), kept)


def layer_backward(grad_out, kept, segment_ids, cls_rows, weights, slices):
    w_qkv, w_proj, w_up, w_down, small = weights
    flat, normed, query, keys, values, logsum, attended, hidden, normed_two, inner, active = kept
    count, length = segment_ids.shape
    width = flat.shape[1]
    hidden_width = w_up.shape[1]
    head_size = width // HEADS
    parts = split_small(small.astype(jnp.float32), width, hidden_width, slices)
    grad_low = grad_out.astype(jnp.bfloat16)
    grad_active = jnp.einsum("rd,fd->rf", grad_low, w_down, preferred_element_type=jnp.float32)
    gelu_value, gelu_back = jax.vjp(partial(jax.nn.gelu, approximate=False), inner)
    grad_inner = gelu_back(grad_active)[0].astype(jnp.bfloat16)
    grad_normed_two = jnp.einsum("rf,df->rd", grad_inner, w_up, preferred_element_type=jnp.float32)
    norm_value, norm_back = jax.vjp(norm_affine, hidden, parts[5], parts[6])
    grad_hidden_part, grad_gain_two, grad_shift_two = norm_back(grad_normed_two)
    grad_hidden = grad_out + grad_hidden_part
    grad_branch = grad_hidden.astype(jnp.bfloat16)
    grad_attended = jnp.einsum(
        "rd,ed->re", grad_branch, w_proj, preferred_element_type=jnp.float32
    ).astype(jnp.bfloat16)
    shape_heads = (count, length, HEADS, head_size)
    query_heads = query.reshape(shape_heads)
    key_heads = keys.reshape(shape_heads)
    value_heads = values.reshape(shape_heads)
    grad_heads = grad_attended.reshape(shape_heads)
    scores = masked_scores(query_heads, key_heads, allowed_pairs(segment_ids, cls_rows))
    probs = jnp.exp(scores - logsum)
    grad_values = jnp.einsum(
        "nhqk,nqhd->nkhd",
        probs.astype(jnp.bfloat16),
        grad_heads,
        preferred_element_type=jnp.float32,
    )
    grad_probs = jnp.einsum(
        "nqhd,nkhd->nhqk", grad_heads, value_heads, preferred_element_type=jnp.float32
    )
    grad_scores = (
        probs * (grad_probs - jnp.sum(probs * grad_probs, axis=-1, keepdims=True))
    ).astype(jnp.bfloat16)
    scale = head_size ** (-0.5)
    grad_query = (
        jnp.einsum("nhqk,nkhd->nqhd", grad_scores, key_heads, preferred_element_type=jnp.float32)
        * scale
    )
    grad_keys = (
        jnp.einsum("nhqk,nqhd->nkhd", grad_scores, query_heads, preferred_element_type=jnp.float32)
        * scale
    )
    total_rows = count * length
    grad_mixed = jnp.concatenate(
        [
            grad_query.reshape(total_rows, width),
            grad_keys.reshape(total_rows, width),
            grad_values.reshape(total_rows, width),
        ],
        axis=1,
    ).astype(jnp.bfloat16)
    grad_normed = jnp.einsum("re,de->rd", grad_mixed, w_qkv, preferred_element_type=jnp.float32)
    norm_value_one, norm_back_one = jax.vjp(norm_affine, flat, parts[0], parts[1])
    grad_flat_part, grad_gain_one, grad_shift_one = norm_back_one(grad_normed)
    grad_input = (grad_hidden + grad_flat_part).astype(jnp.bfloat16)
    mixed_sums = jnp.sum(grad_mixed.astype(jnp.float32), axis=0)
    small_grad = join_small(
        [
            grad_gain_one,
            grad_shift_one,
            mixed_sums[:width],
            mixed_sums[2 * width :],
            jnp.sum(grad_branch.astype(jnp.float32), axis=0),
            grad_gain_two,
            grad_shift_two,
            jnp.sum(grad_low.astype(jnp.float32), axis=0),
            jnp.sum(grad_inner.astype(jnp.float32), axis=0),
        ],
        slices,
    )
    rows_kept = (
        normed,
        grad_mixed,
        attended,
        grad_branch,
        normed_two,
        grad_inner,
        grad_low,
        active,
    )
    return (grad_input, small_grad, rows_kept)


def weight_grads(rows_kept):
    normed, grad_mixed, attended, grad_branch, normed_two, grad_inner, grad_low, active = rows_kept
    return (
        jnp.einsum("rd,re->de", normed, grad_mixed, preferred_element_type=jnp.float32),
        jnp.einsum("rd,re->de", attended, grad_branch, preferred_element_type=jnp.float32),
        jnp.einsum("rd,rf->df", normed_two, grad_inner, preferred_element_type=jnp.float32),
        jnp.einsum("rf,rd->fd", active, grad_low, preferred_element_type=jnp.float32),
    )


def skip_like(function):

    def skipped(*operands):
        return jax.tree.map(jnp.zeros_like, function(*operands))

    return skipped


def store_slot(store, value, position, valid):
    old = lax.dynamic_index_in_dim(store, position, 0, keepdims=False)
    return lax.dynamic_update_index_in_dim(store, jnp.where(valid, value, old), position, 0)


def empty_store(value):
    return jnp.zeros((MICRO,) + value.shape, value.dtype)


def per_device(
    inputs,
    out_grad,
    segment_ids,
    cls_index,
    qkv_master,
    proj_master,
    up_master,
    down_master,
    small_master,
    qkv_first,
    proj_first,
    up_first,
    down_first,
    small_first,
    qkv_second,
    proj_second,
    up_second,
    down_second,
    small_second,
):
    masters = (qkv_master, proj_master, up_master, down_master, small_master)
    firsts = (qkv_first, proj_first, up_first, down_first, small_first)
    seconds = (qkv_second, proj_second, up_second, down_second, small_second)
    gathered = (
        lax.all_gather(qkv_master.astype(jnp.bfloat16), "dp", axis=1, tiled=True),
        lax.all_gather(proj_master.astype(jnp.bfloat16), "dp", axis=1, tiled=True),
        lax.all_gather(up_master.astype(jnp.bfloat16), "dp", axis=1, tiled=True),
        lax.all_gather(down_master.astype(jnp.bfloat16), "dp", axis=1, tiled=True),
        lax.all_gather(small_master.astype(jnp.bfloat16), "dp", axis=1, tiled=True),
    )
    weights = tuple((piece[0] for piece in gathered))
    slices = lax.axis_size("dp")
    sections = lax.axis_size("section")
    section = lax.axis_index("section")
    seq_dev, length, width = inputs.shape
    per_batch = seq_dev // MICRO
    rows = per_batch * length
    ticks = MICRO + sections - 1

    def batch_slice(array, position):
        return lax.dynamic_slice_in_dim(array, position * per_batch, per_batch, 0)

    def forward_run(current, segs, classes):
        output, kept = layer_forward(current, segs, classes, weights, slices)
        return (output, kept)

    def backward_run(grad_now, kept_now, segs, classes):
        grad_input, small_grad, rows_kept = layer_backward(
            grad_now, kept_now, segs, classes, weights, slices
        )
        return (grad_input, small_grad, weight_grads(rows_kept))

    incoming = jnp.zeros((per_batch, length, width), jnp.bfloat16)
    out_store = jnp.zeros((MICRO, rows, width), jnp.bfloat16)
    kept_store = None
    for tick in range(ticks):
        batch = tick - section
        valid = (batch >= 0) & (batch < MICRO)
        position = jnp.clip(batch, 0, MICRO - 1)
        current = jnp.where(section == 0, batch_slice(inputs, position), incoming)
        segs = batch_slice(segment_ids, position)
        classes = batch_slice(cls_index, position)
        output, kept = lax.cond(valid, forward_run, skip_like(forward_run), current, segs, classes)
        if kept_store is None:
            kept_store = jax.tree.map(empty_store, kept)
        out_store = store_slot(out_store, output, position, valid)
        kept_store = jax.tree.map(
            partial(store_slot, position=position, valid=valid), kept_store, kept
        )
        if tick + 1 < ticks:
            incoming = from_behind(output.reshape(per_batch, length, width), "section", 1)
    back_incoming = jnp.zeros((rows, width), jnp.bfloat16)
    grad_store = jnp.zeros((MICRO, rows, width), jnp.bfloat16)
    small_total = jnp.zeros((weights[4].shape[0],), jnp.float32)
    matrix_totals = tuple((jnp.zeros(piece.shape, jnp.float32) for piece in weights[:4]))
    for tick in range(ticks):
        batch = tick - (sections - 1 - section)
        valid = (batch >= 0) & (batch < MICRO)
        position = jnp.clip(batch, 0, MICRO - 1)
        own_grad = batch_slice(out_grad, position).reshape(rows, width)
        grad_now = jnp.where(section == sections - 1, own_grad, back_incoming).astype(jnp.float32)
        kept_now = jax.tree.map(
            lambda stored: lax.dynamic_index_in_dim(stored, position, 0, keepdims=False), kept_store
        )
        segs = batch_slice(segment_ids, position)
        classes = batch_slice(cls_index, position)
        grad_input, small_grad, extra = lax.cond(
            valid, backward_run, skip_like(backward_run), grad_now, kept_now, segs, classes
        )
        small_total = small_total + small_grad
        matrix_totals = tuple((total + term for total, term in zip(matrix_totals, extra)))
        grad_store = store_slot(grad_store, grad_input, position, valid)
        if tick + 1 < ticks:
            back_incoming = from_behind(grad_input, "section", -1)
    shards = (
        lax.psum_scatter(matrix_totals[0][None], "dp", scatter_dimension=1, tiled=True),
        lax.psum_scatter(matrix_totals[1][None], "dp", scatter_dimension=1, tiled=True),
        lax.psum_scatter(matrix_totals[2][None], "dp", scatter_dimension=1, tiled=True),
        lax.psum_scatter(matrix_totals[3][None], "dp", scatter_dimension=1, tiled=True),
        lax.psum_scatter(small_total[None], "dp", scatter_dimension=1, tiled=True),
    )
    shards = tuple(shards)
    squares = jnp.sum(jnp.stack([jnp.sum(shard * shard) for shard in shards]))
    total = lax.psum(squares, ("dp", "section"))
    grad_norm = jnp.sqrt(total)
    factor = 1.0 / jnp.maximum(grad_norm, 1.0)
    first_fix = 1.0 - 0.5**STEP
    second_fix = 1.0 - 0.5**STEP
    results = []
    for kind in range(5):
        grad = shards[kind] * factor
        first = 0.5 * firsts[kind] + 0.5 * grad
        second = 0.5 * seconds[kind] + 0.5 * grad * grad
        update = first / first_fix / (jnp.sqrt(second / second_fix) + adam_eps)
        rate = small_rate
        if kind < 4:
            update = update + decay_rate * masters[kind]
            rate = learn_rate
        results += [grad, masters[kind] - rate * update, first, second]
    acts = out_store.reshape(1, seq_dev, length, width)
    input_grads = grad_store.reshape(1, seq_dev, length, width)
    return (acts, input_grads, grad_norm.reshape(1)) + tuple(results)


def solution(mesh):
    placed = (
        P("dp", None, None),
        P("dp", None, None),
        P("dp", None),
        P("dp"),
        P("section", "dp", None),
        P("section", "dp", None),
        P("section", "dp", None),
        P("section", "dp", None),
        P("section", "dp"),
        P("section", "dp", None),
        P("section", "dp", None),
        P("section", "dp", None),
        P("section", "dp", None),
        P("section", "dp"),
        P("section", "dp", None),
        P("section", "dp", None),
        P("section", "dp", None),
        P("section", "dp", None),
        P("section", "dp"),
    )
    return jax.shard_map(
        per_device,
        mesh=mesh,
        in_specs=placed,
        out_specs=(
            P("section", "dp", None, None),
            P("section", "dp", None, None),
            P(),
            P("section", "dp", None),
            P("section", "dp", None),
            P("section", "dp", None),
            P("section", "dp", None),
            P("section", "dp", None),
            P("section", "dp", None),
            P("section", "dp", None),
            P("section", "dp", None),
            P("section", "dp", None),
            P("section", "dp", None),
            P("section", "dp", None),
            P("section", "dp", None),
            P("section", "dp", None),
            P("section", "dp", None),
            P("section", "dp", None),
            P("section", "dp", None),
            P("section", "dp"),
            P("section", "dp"),
            P("section", "dp"),
            P("section", "dp"),
        ),
        check_vma=False,
    )
```

profile of v0, /device:TPU:0, one launch (start us, length us, event | category | flops | bytes accessed | tf_op | source)
XLA Modules:
  0.0 2244.9 jit_solution(11386528831503213497)
XLA Ops:
  14.5 32.4 %all_gather.15 = bf16[1,9216]{1,0:T(2,128)(2,1)S(1)} all-gather(bf16[1,1152]{1,0:T(2,128)(2,1)S(1)} %convert_element_type.971), channel_id=1, replica_groups=mesh['dp'=8,'section'=4] {'dp'}, dimensions={1}, use_global_device_ids=true | all-gather | bytes 20736 | tf_op jit(solution)/shard_map/all_gather | solution.py:246
  47.0 7.7 all-gather.7.cloned.1.call-done
  54.7 66.7 %all-gather.5.cloned.1.call-done = bf16[1,768,2304]{2,1,0:T(8,128)(2,1)} async-done(((bf16[1,96,2304]{2,1,0:T(8,128)(2,1)}), bf16[1,768,2304]{2,1,0:T(8,128)(2,1)}) %all-gather.5.cloned.1.call-update) | async-done | bytes 3538960 | tf_op jit(solution)/shard_map/all_gather | solution.py:242
  121.4 81.2 %all-gather.9.cloned.1.call-done = bf16[1,768,3072]{2,1,0:T(8,128)(2,1)} async-done(((bf16[1,96,3072]{2,1,0:T(8,128)(2,1)}), bf16[1,768,3072]{2,1,0:T(8,128)(2,1)}) %all-gather.9.cloned.1.call-update) | async-done | bytes 4718608 | tf_op jit(solution)/shard_map/all_gather | solution.py:244
  202.6 80.7 %all-gather.11.cloned.1.call-done = bf16[1,3072,768]{2,1,0:T(8,128)(2,1)} async-done(((bf16[1,384,768]{2,1,0:T(8,128)(2,1)}), bf16[1,3072,768]{2,1,0:T(8,128)(2,1)}) %all-gather.11.cloned.1.call-update) | async-done | bytes 4718608 | tf_op jit(solution)/shard_map/all_gather | solution.py:245
  283.4 29.4 %conditional.14 = (bf16[248,768]{1,0:T(8,128)(2,1)S(1)}, f32[248,768]{1,0:T(8,128)S(1)}, bf16[248,768]{1,0:T(8,128)(2,1)}, bf16[248,768]{1,0:T(8,128)(2,1)}, bf1...) conditional(s32[]{:T(128)} %convert_element_type.970, ...), branch_computations={%region_0.1_spmd, %region_1.8_spmd} | conditional | flops 3764988928 | bytes 87057992 | solution.py:280
  298.9 10.7 fusion.2
  352.4 42.5 %conditional.15 = (bf16[248,768]{1,0:T(8,128)(2,1)}, f32[248,768]{1,0:T(8,128)}, bf16[248,768]{1,0:T(8,128)(2,1)}, bf16[248,768]{1,0:T(8,128)(2,1)}, bf16[248,76...) conditional(s32[]{:T(128)} %convert_element_type.976, ...), branch_computations={%region_8.9_spmd, %region_9.16_spmd} | conditional | flops 3764988928 | bytes 69387624 | solution.py:280
  380.4 10.6 fusion.23
  409.6 11.2 collective-permute-start.1
  443.1 42.4 %conditional.16 = (bf16[248,768]{1,0:T(8,128)(2,1)}, f32[248,768]{1,0:T(8,128)}, bf16[248,768]{1,0:T(8,128)(2,1)}, bf16[248,768]{1,0:T(8,128)(2,1)}, bf16[248,76...) conditional(s32[]{:T(128)} %convert_element_type.977, ...), branch_computations={%region_16.17_spmd, %region_17.24_spmd} | conditional | flops 3764988928 | bytes 69387624 | solution.py:280
  471.1 10.6 fusion.44
  528.7 42.5 %conditional.17 = (bf16[248,768]{1,0:T(8,128)(2,1)}, f32[248,768]{1,0:T(8,128)}, bf16[248,768]{1,0:T(8,128)(2,1)}, bf16[248,768]{1,0:T(8,128)(2,1)}, bf16[248,76...) conditional(s32[]{:T(128)} %convert_element_type.978, ...), branch_computations={%region_24.25_spmd, %region_25.32_spmd} | conditional | flops 3764988928 | bytes 69387624 | solution.py:280
  556.7 10.7 fusion.65
  614.1 9.8 conditional.18
  637.3 14.5 collective-permute-start.4
  671.0 10.1 conditional.19
  694.6 8.6 collective-permute-start.5
  722.5 10.2 conditional.20
  744.4 15.5 conditional.21
  755.1 4.7 broadcast.4604
  761.2 18.7 collective-permute-done.6
  781.1 23.5 %conditional.22 = (bf16[248,768]{1,0:T(8,128)(2,1)}, f32[9216]{0:T(1024)}, f32[768,2304]{1,0:T(8,128)}, f32[768,768]{1,0:T(8,128)}, f32[768,3072]{1,0:T(8,128)}, /*index=5*/f32[3072,768]{1,0:T(8,128)}) conditional(s32[]{:T(128)} %convert_element_type.985, () %tuple.192, (f32[4,248,3072]{2,1,0:T(8,128)}, s32[]{:T(128)}, f32[248,768]{1,0:T(8,128)S(1)}, ...), branch_computations={%region_75.76_spmd, %region_76.0_spmd} | conditional | flops 7578904576 | bytes 153220720 | solution.py:304
  791.8 4.8 broadcast.4648
  805.9 12.8 collective-permute-done.7
  819.9 22.0 conditional.23
  830.5 4.8 broadcast.4692
  843.1 265.7 %collective-permute-done.8 = bf16[248,768]{1,0:T(8,128)(2,1)} collective-permute-done((bf16[248,768]{1,0:T(8,128)(2,1)}, bf16[248,768]{1,0:T(8,128)(2,1)}, u32[]{:S(2)}, u32[]{:S(2)}) %collective-permute-start.8) | collective-permute-done | bytes 380960 | tf_op jit(solution)/shard_map/ppermute | solution.py:24
  1110.0 107.2 %conditional.24 = (bf16[248,768]{1,0:T(8,128)(2,1)}, f32[9216]{0:T(1024)}, f32[768,2304]{1,0:T(8,128)}, f32[768,768]{1,0:T(8,128)}, f32[768,3072]{1,0:T(8,128)}, /*index=5*/f32[3072,768]{1,0:T(8,128)}) conditional(s32[]{:T(128)} %convert_element_type.989, () %tuple.196, (f32[4,248,3072]{2,1,0:T(8,128)}, s32[]{:T(128)}, ...), branch_computations={%region_113.114_spmd, %region_114.0_spmd} | conditional | flops 7578904576 | bytes 153220720 | solution.py:304
  1126.0 10.7 convert_reduce_fusion.15
  1136.8 6.1 multiply_reduce_fusion.29
  1199.5 6.5 fusion.283
  1206.1 5.1 fusion.297
  1211.2 6.1 fusion.293
  1218.5 8.0 collective-permute-done.9
  1227.7 107.7 %conditional.25 = (bf16[248,768]{1,0:T(8,128)(2,1)}, f32[9216]{0:T(1024)}, f32[768,2304]{1,0:T(8,128)}, f32[768,768]{1,0:T(8,128)}, f32[768,3072]{1,0:T(8,128)}, /*index=5*/f32[3072,768]{1,0:T(8,128)}) conditional(s32[]{:T(128)} %convert_element_type.991, () %tuple.198, (f32[4,248,3072]{2,1,0:T(8,128)}, s32[]{:T(128)}, ...), branch_computations={%region_132.133_spmd, %region_133.0_spmd} | conditional | flops 7578904576 | bytes 153220720 | solution.py:304
  1243.9 10.7 convert_reduce_fusion.19
  1254.6 6.1 multiply_reduce_fusion.36
  1317.3 6.5 fusion.339
  1323.8 5.1 fusion.353
  1328.9 6.1 fusion.349
  1336.7 8.0 collective-permute-done.10
  1345.8 107.1 %conditional.26 = (bf16[248,768]{1,0:T(8,128)(2,1)}, f32[9216]{0:T(1024)}, f32[768,2304]{1,0:T(8,128)}, f32[768,768]{1,0:T(8,128)}, f32[768,3072]{1,0:T(8,128)}, /*index=5*/f32[3072,768]{1,0:T(8,128)}) conditional(s32[]{:T(128)} %convert_element_type.993, () %tuple.200, (f32[4,248,3072]{2,1,0:T(8,128)}, s32[]{:T(128)}, ...), branch_computations={%region_151.152_spmd, %region_152.0_spmd} | conditional | flops 7578904576 | bytes 153220720 | solution.py:304
  1361.8 10.7 convert_reduce_fusion.23
  1372.5 6.1 multiply_reduce_fusion.43
  1435.1 6.5 fusion.395
  1441.6 5.1 fusion.409
  1446.7 6.0 fusion.405
  1454.2 8.0 collective-permute-done.11
  1463.3 82.2 %conditional.27 = (bf16[248,768]{1,0:T(8,128)(2,1)}, f32[9216]{0:T(1024)S(1)}, f32[768,2304]{1,0:T(8,128)}, f32[768,768]{1,0:T(8,128)S(1)}, f32[768,3072]{1,0:T(8,128)}, /*index=5*/f32[3072,768]{1,0:T(8,128)}) conditional(s32[]{:T(128)} %convert_element_type.995, () %tuple.202, (f32[4,248,3072]{2,1,0:T(8,128)}, s32[]{:T(128)}, ...), branch_computations={%region_170.171_spmd, %region_171.0_spmd} | conditional | flops 7578904576 | bytes 153420880 | solution.py:304
  1473.1 10.7 convert_reduce_fusion.27
  1483.9 6.1 multiply_reduce_fusion.50
  1527.7 6.5 fusion.451
  1534.1 5.1 fusion.465
  1539.2 6.2 fusion.461
  1549.4 8.0 add_bitcast_fusion.10
  1557.4 20.2 add_bitcast_fusion.9
  1577.7 27.3 %add_bitcast_fusion.8 = f32[1,768,3072]{2,1,0:T(8,128)} fusion(f32[768,3072]{1,0:T(8,128)} %get-tuple-element.2380, f32[768,3072]{1,0:T(8,128)} %get-tuple-element.2379, f32[768,3072]{1,0:T(8,128)} %get-tuple-element.2378, f32[768,3072]{1,0:T(8,128)} %get-tuple-element.2377, f32[768,3072]{1,0:T(8,128)} %get-tuple-element.2376, ...), kind=kLoop, calls=%fused_computation.1074 | loop fusion | flops 14155776 | bytes 75497472 | tf_op jit(solution)/shard_map/broadcast_in_dim | solution.py:315
  1605.1 25.8 %add_bitcast_fusion.7 = f32[1,3072,768]{2,1,0:T(8,128)} fusion(f32[3072,768]{1,0:T(8,128)} %get-tuple-element.2387, f32[3072,768]{1,0:T(8,128)} %get-tuple-element.2386, f32[3072,768]{1,0:T(8,128)} %get-tuple-element.2385, f32[3072,768]{1,0:T(8,128)} %get-tuple-element.2384, f32[3072,768]{1,0:T(8,128)} %get-tuple-element.2383, ...), kind=kLoop, calls=%fused_computation.1073 | loop fusion | flops 14155776 | bytes 75497472 | tf_op jit(solution)/shard_map/broadcast_in_dim | solution.py:316
  1644.1 70.1 %reduce-scatter.10.cloned.1.call-done = f32[1,96,768]{2,1,0:T(8,128)} async-done(((f32[1,768,768]{2,1,0:T(8,128)}), f32[1,96,768]{2,1,0:T(8,128)}) %reduce-scatter.10.cloned.1.call-update) | async-done | bytes 294928 | tf_op jit(solution)/shard_map/reduce_scatter | solution.py:314
  1715.9 130.1 %reduce-scatter.8.cloned.1.call-done = f32[1,96,2304]{2,1,0:T(8,128)} async-done(((f32[1,768,2304]{2,1,0:T(8,128)}), f32[1,96,2304]{2,1,0:T(8,128)}) %reduce-scatter.8.cloned.1.call-update) | async-done | bytes 884752 | tf_op jit(solution)/shard_map/reduce_scatter | solution.py:313
  1849.4 163.2 %reduce-scatter.12.cloned.1.call-done = f32[1,96,3072]{2,1,0:T(8,128)} async-done(((f32[1,768,3072]{2,1,0:T(8,128)}), f32[1,96,3072]{2,1,0:T(8,128)}) %reduce-scatter.12.cloned.1.call-update) | async-done | bytes 1179664 | tf_op jit(solution)/shard_map/reduce_scatter | solution.py:315
  2015.4 163.7 %reduce-scatter.14.cloned.1.call-done = f32[1,384,768]{2,1,0:T(8,128)} async-done(((f32[1,3072,768]{2,1,0:T(8,128)}), f32[1,384,768]{2,1,0:T(8,128)}) %reduce-scatter.14.cloned.1.call-update) | async-done | bytes 1179664 | tf_op jit(solution)/shard_map/reduce_scatter | solution.py:316
  2184.4 38.6 %psum.7 = f32[]{:T(128)} all-reduce(f32[]{:T(128)S(6)} %reduce_sum.1959), channel_id=1, replica_groups=mesh['dp'=8,'section'=4] {'dp','section'}, use_global_device_ids=true, to_apply=%region_199.200 | all-reduce | flops 1 | bytes 8 | tf_op jit(solution)/shard_map/psum | solution.py:321
  (1054 shorter events, 740.4 us)
Async XLA Ops:
  7.2 47.5 %all-gather.7.cloned.1.call-start = ((), (), s32[]{:S(2)}) async-start(), calls=%async_computation.6 | async-start | bytes 1327104 | tf_op jit(solution)/shard_map/all_gather | solution.py:243
  9.0 112.4 %all-gather.5.cloned.1.call-start = ((), (), s32[]{:S(2)}) async-start(), calls=%async_computation.5 | async-start | bytes 3981312 | tf_op jit(solution)/shard_map/all_gather | solution.py:242
  11.0 272.3 %copy-start.15 = (bf16[4,248,768]{2,1,0:T(8,128)(2,1)S(1)}, bf16[4,248,768]{2,1,0:T(8,128)(2,1)}, u32[]{:S(2)}) copy-start(bf16[4,248,768]{2,1,0:T(8,128)(2,1)} %param.47) | copy-start | bytes 4571140
  11.0 272.3 %copy-start.207 = (s32[4,248]{1,0:T(4,128)S(1)}, s32[4,248]{1,0:T(4,128)}, u32[]{:S(2)}) copy-start(s32[4,248]{1,0:T(4,128)} %param.49) | copy-start | bytes 11908
  11.0 272.3 %copy-start.267 = (s32[4]{0:T(128)S(1)}, s32[4]{0:T(128)}, u32[]{:S(2)}) copy-start(s32[4]{0:T(128)} %param.50) | copy-start | bytes 52
  11.1 191.5 %all-gather.9.cloned.1.call-start = ((), (), s32[]{:S(2)}) async-start(), calls=%async_computation.7 | async-start | bytes 5308416 | tf_op jit(solution)/shard_map/all_gather | solution.py:244
  13.4 269.9 %all-gather.11.cloned.1.call-start = ((), (), s32[]{:S(2)}) async-start(), calls=%async_computation.8 | async-start | bytes 5308416 | tf_op jit(solution)/shard_map/all_gather | solution.py:245
  14.4 1627.8 %reduce-scatter.16.cloned.1.call-start = ((), (), s32[]{:S(2)}) async-start(), calls=%async_computation.13 | async-start | bytes 5308416
  296.0 13.6 slice-start.2
  298.9 10.7 copy-start.135
  298.9 10.7 slice-start.3
  321.1 15.9 copy-start.9
  323.6 13.4 copy-start.12
  324.5 27.9 %collective-permute-start = (bf16[1,248,768]{2,1,0:T(8,128)(2,1)S(1)}, bf16[1,248,768]{2,1,0:T(8,128)(2,1)S(1)}, u32[]{:S(2)}, u32[]{:S(2)}) collective-permute-start(bf16[1,248,768]{2,1,0:T(8,128)(2,1)S(1)} %bitcast.1992), channel_id=1, source_target_pairs={{0,1},{1,2},{2,3},{4,5},{5,6},{6,7},{8,9},{9,10},{10,11},{12,13},{... | collective-permute-start | bytes 1142792 | tf_op jit(solution)/shard_map/ppermute | solution.py:24
  376.8 14.2 slice-start.4
  380.4 10.6 slice-start.5
  399.8 20.9 copy-start.114
  399.8 20.9 copy-start.115
  409.6 33.6 %collective-permute-start.1 = (bf16[1,248,768]{2,1,0:T(8,128)(2,1)}, bf16[1,248,768]{2,1,0:T(8,128)(2,1)S(1)}, u32[]{:S(2)}, u32[]{:S(2)}) collective-permute-start(bf16[1,248,768]{2,1,0:T(8,128)(2,1)} %bitcast.222), channel_id=1, source_target_pairs={{0,1},{1,2},{2,3},{4,5},{5,6},{6,7},{8,9},{9,10},{10,11},{12,13},{... | collective-permute-start | bytes 1142792 | tf_op jit(solution)/shard_map/ppermute | solution.py:24
  467.5 14.2 slice-start.6
  471.1 10.6 slice-start.7
  486.8 10.8 copy-start.160
  491.4 11.6 copy-start.124
  497.6 9.7 copy-start.123
  501.3 27.5 %collective-permute-start.2 = (bf16[1,248,768]{2,1,0:T(8,128)(2,1)}, bf16[1,248,768]{2,1,0:T(8,128)(2,1)S(1)}, u32[]{:S(2)}, u32[]{:S(2)}) collective-permute-start(bf16[1,248,768]{2,1,0:T(8,128)(2,1)} %bitcast.225), channel_id=1, source_target_pairs={{0,1},{1,2},{2,3},{4,5},{5,6},{6,7},{8,9},{9,10},{10,11},{12,13},{... | collective-permute-start | bytes 1142792 | tf_op jit(solution)/shard_map/ppermute | solution.py:24
  553.2 14.3 slice-start.8
  556.7 10.7 slice-start.9
  572.6 10.8 copy-start.147
  577.1 11.2 copy-start.117
  587.0 27.0 %collective-permute-start.3 = (bf16[1,248,768]{2,1,0:T(8,128)(2,1)}, bf16[1,248,768]{2,1,0:T(8,128)(2,1)S(1)}, u32[]{:S(2)}, u32[]{:S(2)}) collective-permute-start(bf16[1,248,768]{2,1,0:T(8,128)(2,1)} %bitcast.228), channel_id=1, source_target_pairs={{0,1},{1,2},{2,3},{4,5},{5,6},{6,7},{8,9},{9,10},{10,11},{12,13},{... | collective-permute-start | bytes 1142792 | tf_op jit(solution)/shard_map/ppermute | solution.py:24
  629.4 22.3 copy-start.119
  634.7 20.3 copy-start.120
  637.3 33.7 %collective-permute-start.4 = (bf16[1,248,768]{2,1,0:T(8,128)(2,1)}, bf16[1,248,768]{2,1,0:T(8,128)(2,1)S(1)}, u32[]{:S(2)}, u32[]{:S(2)}) collective-permute-start(bf16[1,248,768]{2,1,0:T(8,128)(2,1)} %bitcast.231), channel_id=1, source_target_pairs={{0,1},{1,2},{2,3},{4,5},{5,6},{6,7},{8,9},{9,10},{10,11},{12,13},{... | collective-permute-start | bytes 1142792 | tf_op jit(solution)/shard_map/ppermute | solution.py:24
  686.7 16.5 copy-start.121
  692.0 14.4 copy-start.122
  694.6 27.9 %collective-permute-start.5 = (bf16[1,248,768]{2,1,0:T(8,128)(2,1)}, bf16[1,248,768]{2,1,0:T(8,128)(2,1)S(1)}, u32[]{:S(2)}, u32[]{:S(2)}) collective-permute-start(bf16[1,248,768]{2,1,0:T(8,128)(2,1)} %bitcast.235), channel_id=1, source_target_pairs={{0,1},{1,2},{2,3},{4,5},{5,6},{6,7},{8,9},{9,10},{10,11},{12,13},{... | collective-permute-start | bytes 1142792 | tf_op jit(solution)/shard_map/ppermute | solution.py:24
  759.9 20.0 collective-permute-start.6
  804.6 14.1 collective-permute-start.7
  841.8 267.0 %collective-permute-start.8 = (bf16[248,768]{1,0:T(8,128)(2,1)}, bf16[248,768]{1,0:T(8,128)(2,1)}, u32[]{:S(2)}, u32[]{:S(2)}) collective-permute-start(bf16[248,768]{1,0:T(8,128)(2,1)} %get-tuple-element.2355), channel_id=1, source_target_pairs={{1,0},{2,1},{3,2},{5,4},{6,5},{7,6},{9,8},{10,9},{11,10},{13,12},{... | collective-permute-start | bytes 1142792 | tf_op jit(solution)/shard_map/ppermute | solution.py:24
  1126.0 10.7 copy-start.218
  1126.0 10.7 copy-start.236
  1126.0 10.7 copy-start.262
  1217.2 9.3 collective-permute-start.9
  1243.9 10.8 copy-start.219
  1243.9 10.8 copy-start.238
  1243.9 10.8 copy-start.263
  1335.4 9.3 collective-permute-start.10
  1361.8 10.7 copy-start.220
  1361.8 10.7 copy-start.240
  1361.8 10.7 copy-start.264
  1452.9 9.3 collective-permute-start.11
  1469.4 14.5 copy-start.241
  1473.1 10.7 copy-start.265
  1549.3 164.8 %reduce-scatter.10.cloned.1.call-start = ((), (), s32[]{:S(2)}) async-start(), calls=%async_computation.10 | async-start | bytes 2654208 | tf_op jit(solution)/shard_map/reduce_scatter | solution.py:314
  1557.4 288.6 %reduce-scatter.8.cloned.1.call-start = ((), (), s32[]{:S(2)}) async-start(), calls=%async_computation.9 | async-start | bytes 7962624 | tf_op jit(solution)/shard_map/reduce_scatter | solution.py:313
  1577.7 434.9 %reduce-scatter.12.cloned.1.call-start = ((), (), s32[]{:S(2)}) async-start(), calls=%async_computation.11 | async-start | bytes 10616832 | tf_op jit(solution)/shard_map/reduce_scatter | solution.py:315
  1605.0 574.0 %reduce-scatter.14.cloned.1.call-start = ((), (), s32[]{:S(2)}) async-start(), calls=%async_computation.12 | async-start | bytes 10616832 | tf_op jit(solution)/shard_map/reduce_scatter | solution.py:316
  1641.3 582.4 %copy-start.209 = (f32[1,1152]{1,0:T(1,128)S(1)}, f32[1,1152]{1,0:T(1,128)}, u32[]{:S(2)}) copy-start(f32[1,1152]{1,0:T(1,128)} %param.55) | copy-start | bytes 13828
  1641.3 582.4 %copy-start.251 = (f32[1,1152]{1,0:T(1,128)S(1)}, f32[1,1152]{1,0:T(1,128)}, u32[]{:S(2)}) copy-start(f32[1,1152]{1,0:T(1,128)} %param.60) | copy-start | bytes 13828
  1641.3 582.5 %copy-start.252 = (f32[1,1152]{1,0:T(1,128)S(1)}, f32[1,1152]{1,0:T(1,128)}, u32[]{:S(2)}) copy-start(f32[1,1152]{1,0:T(1,128)} %param.65) | copy-start | bytes 13828
  1641.3 583.1 %copy-start.183 = (f32[1,96,768]{2,1,0:T(8,128)S(1)}, f32[1,96,768]{2,1,0:T(8,128)}, u32[]{:S(2)}) copy-start(f32[1,96,768]{2,1,0:T(8,128)} %param.52) | copy-start | bytes 884740
  1641.3 583.1 %copy-start.192 = (f32[1,96,768]{2,1,0:T(8,128)S(1)}, f32[1,96,768]{2,1,0:T(8,128)}, u32[]{:S(2)}) copy-start(f32[1,96,768]{2,1,0:T(8,128)} %param.57) | copy-start | bytes 884740
  1714.2 510.2 %copy-start.184 = (f32[1,96,768]{2,1,0:T(8,128)S(1)}, f32[1,96,768]{2,1,0:T(8,128)}, u32[]{:S(2)}) copy-start(f32[1,96,768]{2,1,0:T(8,128)} %reduce-scatter.10.cloned.1.call-done) | copy-start | bytes 884740
  1848.0 378.5 %copy-start.81 = (f32[1,96,2304]{2,1,0:T(8,128)S(1)}, f32[1,96,2304]{2,1,0:T(8,128)}, u32[]{:S(2)}) copy-start(f32[1,96,2304]{2,1,0:T(8,128)} %reduce-scatter.8.cloned.1.call-done) | copy-start | bytes 2654212
  (160 other events, 621.2 us)
Sparse Core Ops, SparseCore 0:
  10.8 43.8 all-gather.6
  57.4 63.9 all-gather.4
  124.2 78.3 all-gather.8
  205.2 78.0 all-gather.10
  1549.5 92.6 reduce-scatter.15
  1645.5 68.6 reduce-scatter.9
  1717.9 128.0 reduce-scatter.7
  1850.0 162.5 reduce-scatter.11
  2016.6 162.4 reduce-scatter.13
where the time goes:
time: 2270 us; the launch traced here: 2240 us
  waiting for transfers between devices  1090 us (48%)
  local copies, waits for them, and re-layouts  374 us (16%)
  other arithmetic  353 us (16%)
  matrix products  276 us (12%)
  blocking collectives  71 us (3%)
  starting transfers between devices  46.9 us (2%)
    ppermute x12, waiting for transfers between devices, from_behind(): return lax.ppermute(value, axis, pairs)  321 us
    reduce_scatter x1, waiting for transfers between devices, per_device(): lax.psum_scatter(matrix_totals[3][None], 'dp', scatter_dimension=1, tiled...  164 us
    reduce_scatter x1, waiting for transfers between devices, per_device(): lax.psum_scatter(matrix_totals[2][None], 'dp', scatter_dimension=1, tiled...  163 us
    reduce_scatter x1, waiting for transfers between devices, per_device(): lax.psum_scatter(matrix_totals[0][None], 'dp', scatter_dimension=1, tiled...  130 us
    dynamic_slice x70, local copies, waits for them, and re-layouts, store_slot(): old = lax.dynamic_index_in_dim(store, position, 0, keepdims=False)  116 us
    dynamic_update_slice x87, other arithmetic, store_slot(): lax.dynamic_update_index_in_dim(store, jnp.where(valid, value, old), posi...  113 us
    another operation x76, local copies, waits for them, and re-layouts  108 us
    all_gather x1, waiting for transfers between devices, per_device(): lax.all_gather(up_master.astype(jnp.bfloat16), 'dp', axis=1, tiled=True)  81.2 us
  transfers between devices with their start and end apart: 21, of which 15 were waited for; matrix products, arithmetic and copies ran while one was open for 11% of the time, Pallas kernels for 0%

commit v1 on v0

v1 whole, which is shorter than its diff:
```python
import functools

import jax
import jax.numpy as jnp
from jax import lax
from jax.experimental import pallas as pl
from jax.experimental.pallas import tpu as pltpu
from jax.sharding import PartitionSpec as P

HEADS = 12
STEP = 3
F32 = jnp.float32
BF = jnp.bfloat16
MESH = pl.DeviceIdType.MESH
VMEM_CAP = 60 * 1024 * 1024

norm_eps = 1e-06
masked_score = -1e30
learn_rate = 0.05
small_rate = 0.3
decay_rate = 0.05
adam_eps = 1e-08

NT = (((1,), (1,)), ((), ()))


def mm(a, b):
    return jnp.dot(a, b, preferred_element_type=F32)


def mm_nt(a, b):
    return lax.dot_general(a, b, NT, preferred_element_type=F32)


def norm_parts(values):
    center = values - jnp.mean(values, axis=-1, keepdims=True)
    spread = jnp.mean(center * center, axis=-1, keepdims=True)
    inv = lax.rsqrt(spread + norm_eps)
    return center * inv, inv


def norm_back(y, normed, inv):
    pull = jnp.mean(y * normed, axis=-1, keepdims=True)
    return (y - jnp.mean(y, axis=-1, keepdims=True) - normed * pull) * inv


def column_sum(values):
    return jnp.sum(values, axis=0, keepdims=True)


def mask_bias(seg_row, seg_col, cls, length):
    size = seg_col.shape[0]
    key_at = lax.broadcasted_iota(jnp.int32, (size, size), 0)
    query_at = lax.broadcasted_iota(jnp.int32, (size, size), 1)
    allowed = (seg_row == seg_col) | (key_at == cls) | (query_at == cls)
    allowed = allowed & (key_at < length)
    return jnp.where(allowed, 0.0, masked_score).astype(F32)


def gelu_parts(z):
    density = jnp.exp(z * z * -0.5) * 0.3989422804014327
    below = 0.5 + 0.5 * lax.erf(z * 0.7071067811865476)
    return z * below, below + z * density


def layer_forward(x_ref, bias_ref, wqkv, wproj, wup, wdown, small, a_ref, qkv_ref, lse_ref, o_ref,
                  h_ref, a2_ref, gp_ref, u_ref, out_ref, ot_ref, before_up):
    rows, width = x_ref.shape
    hidden = wup.shape[1]
    normed, _ = norm_parts(x_ref[...].astype(F32))
    a_ref[...] = (normed * small[0:1, :] + small[1:2, :]).astype(BF)
    for part in range(3):
        cols = slice(part * width, (part + 1) * width)
        mixed = mm(a_ref[...], wqkv[:, cols])
        if part == 0:
            mixed = mixed + small[2:3, :]
        if part == 2:
            mixed = mixed + small[3:4, :]
        qkv_ref[:, cols] = mixed.astype(BF)
    lane = lax.broadcasted_iota(jnp.int32, (rows, 128), 1)
    for pair in range(HEADS // 2):
        q = qkv_ref[:, pair * 128 : pair * 128 + 128]
        k = qkv_ref[:, width + pair * 128 : width + pair * 128 + 128]
        vt = qkv_ref[:, 2 * width + pair * 128 : 2 * width + pair * 128 + 128].T
        for side in range(2):
            half = (lane < 64) if side == 0 else (lane >= 64)
            k_half = jnp.where(half, k, jnp.zeros_like(k))
            scores = mm_nt(k_half, q) * 0.125 + bias_ref[...]
            peak = jnp.max(scores, axis=0, keepdims=True)
            raised = jnp.exp(scores - peak)
            summed = jnp.sum(raised, axis=0, keepdims=True)
            mixed = mm(vt[side * 64 : side * 64 + 64, :], raised.astype(BF)) * (1.0 / summed)
            at = pair * 128 + side * 64
            ot_ref[at : at + 64, :] = mixed.astype(BF)
            head = 2 * pair + side
            lse_ref[head : head + 1, :] = peak + jnp.log(summed)
    o_ref[...] = ot_ref[...].T
    h = x_ref[...].astype(F32) + (mm(o_ref[...], wproj[...]) + small[4:5, :])
    h_ref[...] = h
    normed, _ = norm_parts(h)
    a2_ref[...] = (normed * small[5:6, :] + small[6:7, :]).astype(BF)
    before_up()
    for part in range(hidden // width):
        cols = slice(part * width, (part + 1) * width)
        z = mm(a2_ref[...], wup[:, cols]) + small[8 + part : 9 + part, :]
        u, slope = gelu_parts(z)
        u_ref[:, cols] = u.astype(BF)
        gp_ref[:, cols] = slope.astype(BF)
    out_ref[...] = (h_ref[...] + (mm(u_ref[...], wdown[...]) + small[7:8, :])).astype(BF)


def layer_backward(g_ref, x_ref, bias_ref, qkv_ref, lse_ref, h_ref, gp_ref, wqkv, wproj, wup, wdown,
                   small, dz_ref, f_ref, r_ref, gin_ref, sums_ref, do_ref, dh_ref, dqt_ref):
    rows, width = x_ref.shape
    hidden = wup.shape[1]
    carried = g_ref[...].astype(F32)
    sums_ref[7:8, :] += column_sum(carried)
    for part in range(hidden // width):
        cols = slice(part * width, (part + 1) * width)
        back = mm_nt(g_ref[...], wdown[cols, :])
        dz = (back * gp_ref[:, cols].astype(F32)).astype(BF)
        dz_ref[:, cols] = dz
        sums_ref[8 + part : 9 + part, :] += column_sum(dz.astype(F32))
    back = mm_nt(dz_ref[...], wup[...])
    normed, inv = norm_parts(h_ref[...])
    sums_ref[5:6, :] += column_sum(back * normed)
    sums_ref[6:7, :] += column_sum(back)
    dh = carried + norm_back(back * small[5:6, :], normed, inv)
    dh_ref[...] = dh
    f = dh.astype(BF)
    f_ref[...] = f
    sums_ref[4:5, :] += column_sum(f.astype(F32))
    do_ref[...] = mm_nt(f_ref[...], wproj[...]).astype(BF)
    lane = lax.broadcasted_iota(jnp.int32, (rows, 128), 1)
    for pair in range(HEADS // 2):
        q = qkv_ref[:, pair * 128 : pair * 128 + 128]
        k = qkv_ref[:, width + pair * 128 : width + pair * 128 + 128]
        v = qkv_ref[:, 2 * width + pair * 128 : 2 * width + pair * 128 + 128]
        do = do_ref[:, pair * 128 : pair * 128 + 128]
        kt = k.T
        dv_sides = []
        dk_sides = []
        for side in range(2):
            half = (lane < 64) if side == 0 else (lane >= 64)
            k_half = jnp.where(half, k, jnp.zeros_like(k))
            v_half = jnp.where(half, v, jnp.zeros_like(v))
            head = 2 * pair + side
            scores = mm_nt(k_half, q) * 0.125 + bias_ref[...]
            probs = jnp.exp(scores - lse_ref[head : head + 1, :])
            dv_sides.append(mm(probs.astype(BF), do))
            dp = mm_nt(v_half, do)
            inner = jnp.sum(probs * dp, axis=0, keepdims=True)
            ds = (probs * (dp - inner)).astype(BF)
            dk_sides.append(mm(ds, q))
            at = pair * 128 + side * 64
            dqt_ref[at : at + 64, :] = (mm(kt[side * 64 : side * 64 + 64, :], ds) * 0.125).astype(BF)
        at = width + pair * 128
        r_ref[:, at : at + 128] = (jnp.where(lane < 64, dk_sides[0], dk_sides[1]) * 0.125).astype(BF)
        at = 2 * width + pair * 128
        r_ref[:, at : at + 128] = jnp.where(lane < 64, dv_sides[0], dv_sides[1]).astype(BF)
    r_ref[:, 0:width] = dqt_ref[...].T
    sums_ref[2:3, :] += column_sum(r_ref[:, 0:width].astype(F32))
    sums_ref[3:4, :] += column_sum(r_ref[:, 2 * width :].astype(F32))
    back = mm_nt(r_ref[...], wqkv[...])
    normed, inv = norm_parts(x_ref[...].astype(F32))
    sums_ref[0:1, :] += column_sum(back * normed)
    sums_ref[1:2, :] += column_sum(back)
    gin_ref[...] = (dh_ref[...] + norm_back(back * small[0:1, :], normed, inv)).astype(BF)


class Line:
    def __init__(self, axis, count, stride):
        self.axis, self.count, self.stride = axis, count, stride

    def stage(self):
        return lax.axis_index(self.axis) // self.stride

    def beside(self, by):
        return {self.axis: lax.axis_index(self.axis) + by * self.stride}


def greet(line):
    stage = line.stage()
    barrier = pltpu.get_barrier_semaphore()

    @pl.when(stage > 0)
    def _():
        pl.semaphore_signal(barrier, inc=1, device_id=line.beside(-1), device_id_type=MESH)

    @pl.when(stage < line.count - 1)
    def _():
        pl.semaphore_signal(barrier, inc=1, device_id=line.beside(1), device_id_type=MESH)

    expected = jnp.where(stage > 0, 1, 0) + jnp.where(stage < line.count - 1, 1, 0)
    pl.semaphore_wait(barrier, expected)


def forward_kernel(line, length, x_in, segr, segc, cls, wqkv_h, wproj_h, wup_h, wdown_h, small,
                   x_o, a_o, qkv_o, lse_o, o_o, h_o, a2_o, gp_o, u_o, acts_o,
                   wqkv, wproj, wup, wdown, xs, outs, a, qkv, lse, o, h, a2, gp, u, bias, ot,
                   w_sem, in_sem, x_sem, save_sem, act_sem, send_sem, recv_sem):
    micro = xs.shape[0]
    stage = line.stage()
    loads = [
        pltpu.make_async_copy(src, dst, w_sem.at[i])
        for i, (src, dst) in enumerate(((wqkv_h, wqkv), (wproj_h, wproj), (wup_h, wup), (wdown_h, wdown)))
    ]
    for load in loads:
        load.start()

    def first_in(m):
        return pltpu.make_async_copy(x_in.at[m], xs.at[m], in_sem.at[m])

    @pl.when(stage == 0)
    def _():
        for m in range(micro):
            first_in(m).start()

    greet(line)

    saved = ((a, a_o), (qkv, qkv_o), (lse, lse_o), (o, o_o), (h, h_o), (a2, a2_o), (gp, gp_o), (u, u_o))

    def saves(m, slot):
        return [
            pltpu.make_async_copy(here.at[slot], there.at[m], save_sem.at[slot, i])
            for i, (here, there) in enumerate(saved)
        ]

    def hop(m):
        return pltpu.make_async_remote_copy(
            src_ref=outs.at[m], dst_ref=xs.at[m], send_sem=send_sem.at[m], recv_sem=recv_sem.at[m],
            device_id=line.beside(1), device_id_type=MESH)

    def step(m, carry):
        slot = lax.rem(m, 2)

        @pl.when(stage == 0)
        def _():
            first_in(m).wait()

        @pl.when(stage > 0)
        def _():
            hop(m).wait_recv()

        pltpu.make_async_copy(xs.at[m], x_o.at[m], x_sem.at[m]).start()

        @pl.when(m >= 2)
        def _():
            for save in saves(m - 2, slot):
                save.wait()

        @pl.when(m == 0)
        def _():
            loads[0].wait()
            loads[1].wait()

        bias[...] = mask_bias(segr[m], segc[m], cls[m], length)

        def before_up():
            @pl.when(m == 0)
            def _():
                loads[2].wait()
                loads[3].wait()

        layer_forward(xs.at[m], bias, wqkv, wproj, wup, wdown, small, a.at[slot], qkv.at[slot],
                      lse.at[slot], o.at[slot], h.at[slot], a2.at[slot], gp.at[slot], u.at[slot],
                      outs.at[m], ot, before_up)

        @pl.when(stage < line.count - 1)
        def _():
            hop(m).start()

        for save in saves(m, slot):
            save.start()
        pltpu.make_async_copy(outs.at[m], acts_o.at[m], act_sem.at[m]).start()
        return carry

    lax.fori_loop(0, micro, step, 0)

    for m in range(max(micro - 2, 0), micro):
        for save in saves(m, m % 2):
            save.wait()
    for m in range(micro):
        pltpu.make_async_copy(xs.at[m], x_o.at[m], x_sem.at[m]).wait()
        pltpu.make_async_copy(outs.at[m], acts_o.at[m], act_sem.at[m]).wait()

    @pl.when(stage < line.count - 1)
    def _():
        for m in range(micro):
            hop(m).wait_send()


def backward_kernel(line, length, g_in, x_h, qkv_h, lse_h, h_h, gp_h, segr, segc, cls,
                    wqkv_h, wproj_h, wup_h, wdown_h, small,
                    g_o, dz_o, f_o, r_o, gin_o, sums_o,
                    wqkv, wproj, wup, wdown, gs, gins, x, qkv, lse, h, gp, dz, f, r, bias, do, dh, dqt,
                    w_sem, in_sem, g_sem, load_sem, save_sem, act_sem, send_sem, recv_sem):
    micro = gs.shape[0]
    stage = line.stage()
    loads = [
        pltpu.make_async_copy(src, dst, w_sem.at[i])
        for i, (src, dst) in enumerate(((wdown_h, wdown), (wup_h, wup), (wproj_h, wproj), (wqkv_h, wqkv)))
    ]

    def last_in(m):
        return pltpu.make_async_copy(g_in.at[m], gs.at[m], in_sem.at[m])

    @pl.when(stage == line.count - 1)
    def _():
        for m in range(micro):
            last_in(m).start()

    kept = ((gp_h, gp), (h_h, h), (qkv_h, qkv), (lse_h, lse), (x_h, x))

    def fetches(m, slot):
        return [
            pltpu.make_async_copy(there.at[m], here.at[slot], load_sem.at[slot, i])
            for i, (there, here) in enumerate(kept)
        ]

    loads[0].start()
    for fetch in fetches(0, 0):
        fetch.start()
    for load in loads[1:]:
        load.start()
    sums_o[...] = jnp.zeros_like(sums_o)
    greet(line)

    saved = ((dz, dz_o), (f, f_o), (r, r_o))

    def saves(m, slot):
        return [
            pltpu.make_async_copy(here.at[slot], there.at[m], save_sem.at[slot, i])
            for i, (here, there) in enumerate(saved)
        ]

    def hop(m):
        return pltpu.make_async_remote_copy(
            src_ref=gins.at[m], dst_ref=gs.at[m], send_sem=send_sem.at[m], recv_sem=recv_sem.at[m],
            device_id=line.beside(-1), device_id_type=MESH)

    def step(m, carry):
        slot = lax.rem(m, 2)

        @pl.when(m + 1 < micro)
        def _():
            for fetch in fetches(m + 1, 1 - slot):
                fetch.start()

        @pl.when(m == 0)
        def _():
            for load in loads:
                load.wait()

        for fetch in fetches(m, slot):
            fetch.wait()
        bias[...] = mask_bias(segr[m], segc[m], cls[m], length)

        @pl.when(m >= 2)
        def _():
            for save in saves(m - 2, slot):
                save.wait()

        @pl.when(stage == line.count - 1)
        def _():
            last_in(m).wait()

        @pl.when(stage < line.count - 1)
        def _():
            hop(m).wait_recv()

        pltpu.make_async_copy(gs.at[m], g_o.at[m], g_sem.at[m]).start()
        layer_backward(gs.at[m], x.at[slot], bias, qkv.at[slot], lse.at[slot], h.at[slot], gp.at[slot],
                       wqkv, wproj, wup, wdown, small, dz.at[slot], f.at[slot], r.at[slot], gins.at[m],
                       sums_o, do, dh, dqt)

        @pl.when(stage > 0)
        def _():
            hop(m).start()

        for save in saves(m, slot):
            save.start()
        pltpu.make_async_copy(gins.at[m], gin_o.at[m], act_sem.at[m]).start()
        return carry

    lax.fori_loop(0, micro, step, 0)

    for m in range(max(micro - 2, 0), micro):
        for save in saves(m, m % 2):
            save.wait()
    for m in range(micro):
        pltpu.make_async_copy(gs.at[m], g_o.at[m], g_sem.at[m]).wait()
        pltpu.make_async_copy(gins.at[m], gin_o.at[m], act_sem.at[m]).wait()

    @pl.when(stage > 0)
    def _():
        for m in range(micro):
            hop(m).wait_send()


IN_VMEM = pl.BlockSpec(memory_space=pltpu.VMEM)
IN_SMEM = pl.BlockSpec(memory_space=pltpu.SMEM)
ANYWHERE = pl.BlockSpec(memory_space=pl.ANY)
DMA = pltpu.SemaphoreType.DMA


def run_forward(line, length, x_in, segr, segc, cls, weights, small):
    micro, rows, width = x_in.shape
    hidden = weights[2].shape[1]
    shape = jax.ShapeDtypeStruct
    saved = (
        ((rows, width), BF), ((rows, 3 * width), BF), ((16, rows), F32), ((rows, width), BF),
        ((rows, width), F32), ((rows, width), BF), ((rows, hidden), BF), ((rows, hidden), BF))
    many = shape((micro, rows, width), BF)
    return pl.pallas_call(
        functools.partial(forward_kernel, line, length),
        out_shape=[many] + [shape((micro,) + s, t) for s, t in saved] + [many],
        in_specs=[ANYWHERE, IN_VMEM, IN_VMEM, IN_SMEM] + [ANYWHERE] * 4 + [IN_VMEM],
        out_specs=[ANYWHERE] * 10,
        scratch_shapes=[pltpu.VMEM(w.shape, BF) for w in weights]
        + [pltpu.VMEM((micro, rows, width), BF)] * 2
        + [pltpu.VMEM((2,) + s, t) for s, t in saved]
        + [pltpu.VMEM((rows, rows), F32), pltpu.VMEM((width, rows), BF)]
        + [DMA((4,)), DMA((micro,)), DMA((micro,)), DMA((2, 8)), DMA((micro,)), DMA((micro,)), DMA((micro,))],
        compiler_params=pltpu.CompilerParams(
            collective_id=0, has_side_effects=True, vmem_limit_bytes=VMEM_CAP),
        name="forward_line",
    )(x_in, segr, segc, cls, *weights, small)


def run_backward(line, length, g_in, x, qkv, lse, h, gp, segr, segc, cls, weights, small):
    micro, rows, width = g_in.shape
    hidden = weights[2].shape[1]
    shape = jax.ShapeDtypeStruct
    many = shape((micro, rows, width), BF)
    wqkv, wproj, wup, wdown = weights
    return pl.pallas_call(
        functools.partial(backward_kernel, line, length),
        out_shape=[many, shape((micro, rows, hidden), BF), many, shape((micro, rows, 3 * width), BF), many,
                   shape((16, width), F32)],
        in_specs=[ANYWHERE] * 6 + [IN_VMEM, IN_VMEM, IN_SMEM] + [ANYWHERE] * 4 + [IN_VMEM],
        out_specs=[ANYWHERE] * 5 + [IN_VMEM],
        scratch_shapes=[pltpu.VMEM(w.shape, BF) for w in weights]
        + [pltpu.VMEM((micro, rows, width), BF)] * 2
        + [pltpu.VMEM((2, rows, width), BF), pltpu.VMEM((2, rows, 3 * width), BF), pltpu.VMEM((2, 16, rows), F32),
           pltpu.VMEM((2, rows, width), F32), pltpu.VMEM((2, rows, hidden), BF),
           pltpu.VMEM((2, rows, hidden), BF), pltpu.VMEM((2, rows, width), BF), pltpu.VMEM((2, rows, 3 * width), BF),
           pltpu.VMEM((rows, rows), F32), pltpu.VMEM((rows, width), BF), pltpu.VMEM((rows, width), F32),
           pltpu.VMEM((width, rows), BF)]
        + [DMA((4,)), DMA((micro,)), DMA((micro,)), DMA((2, 5)), DMA((2, 3)), DMA((micro,)), DMA((micro,)),
           DMA((micro,))],
        compiler_params=pltpu.CompilerParams(
            collective_id=1, has_side_effects=True, vmem_limit_bytes=VMEM_CAP),
        name="backward_line",
    )(g_in, x, qkv, lse, h, gp, segr, segc, cls, wqkv, wproj, wup, wdown, small)


def split_small(small, width, slices):
    share = width // slices
    stacked = small.reshape(slices, small.shape[0] // slices)
    eight = stacked[:, : 8 * share].reshape(slices, 8, share).transpose(1, 0, 2).reshape(8, width)
    up = stacked[:, 8 * share :].reshape(-1, width)
    return jnp.concatenate([eight, up, jnp.zeros((16 - 8 - up.shape[0], width), small.dtype)], axis=0)


def join_small(table, total, slices):
    width = table.shape[1]
    share = width // slices
    ups = total // width - 8
    eight = table[:8].reshape(8, slices, share).transpose(1, 0, 2).reshape(slices, 8 * share)
    up = table[8 : 8 + ups].reshape(slices, -1)
    return jnp.concatenate([eight, up], axis=1).reshape(-1)


def weight_grad(left, right):
    rows = left.shape[0] * left.shape[1]
    return lax.dot_general(left.reshape(rows, -1), right.reshape(rows, -1), (((0,), (0,)), ((), ())),
                           preferred_element_type=F32)


def per_device(inputs, out_grad, segment_ids, cls_index, *states):
    masters, firsts, seconds = states[0:5], states[5:10], states[10:15]
    slices = lax.axis_size("dp")
    line = Line("section", lax.axis_size("section"), 1)
    seq_dev, length, width = inputs.shape
    rows = -(-length // 128) * 128

    gathered = [lax.all_gather(m.astype(BF), "dp", axis=1, tiled=True)[0] for m in masters]
    weights = gathered[:4]
    total = gathered[4].shape[0]
    small = split_small(gathered[4].astype(F32), width, slices)

    extra = ((0, 0), (0, rows - length), (0, 0))
    x_in = jnp.pad(inputs, extra)
    g_in = jnp.pad(out_grad, extra)
    segs = jnp.pad(segment_ids, ((0, 0), (0, rows - length)), constant_values=-1)
    segr, segc = segs[:, None, :], segs[:, :, None]

    x, a, qkv, lse, o, h, a2, gp, u, acts = run_forward(line, length, x_in, segr, segc, cls_index, weights, small)
    g, dz, f, r, gin, sums = run_backward(line, length, g_in, x, qkv, lse, h, gp, segr, segc, cls_index, weights, small)
    totals = [weight_grad(a, r).astype(BF), weight_grad(o, f).astype(BF), weight_grad(a2, dz).astype(BF),
              weight_grad(u, g).astype(BF), join_small(sums, total, slices)]
    shards = [lax.psum_scatter(t[None], "dp", scatter_dimension=1, tiled=True).astype(F32) for t in totals]
    squares = jnp.sum(jnp.stack([jnp.sum(s * s) for s in shards]))
    grad_norm = jnp.sqrt(lax.psum(squares, ("dp", "section")))
    factor = 1.0 / jnp.maximum(grad_norm, 1.0)
    fix = 1.0 - 0.5**STEP
    results = []
    for kind in range(5):
        grad = shards[kind] * factor
        first = 0.5 * firsts[kind] + 0.5 * grad
        second = 0.5 * seconds[kind] + 0.5 * grad * grad
        update = first / fix / (jnp.sqrt(second / fix) + adam_eps)
        rate = small_rate
        if kind < 4:
            update = update + decay_rate * masters[kind]
            rate = learn_rate
        results += [grad, masters[kind] - rate * update, first, second]
    return (acts[:, :length][None], gin[:, :length][None], grad_norm.reshape(1)) + tuple(results)


def solution(mesh):
    matrix, vector = P("section", "dp", None), P("section", "dp")
    states = (matrix,) * 4 + (vector,)
    return jax.shard_map(
        per_device,
        mesh=mesh,
        in_specs=(P("dp", None, None), P("dp", None, None), P("dp", None), P("dp")) + states * 3,
        out_specs=(P("section", "dp", None, None), P("section", "dp", None, None), P())
        + (matrix,) * 16 + (vector,) * 4,
        check_vma=False,
    )
```

time: 2270 us -> 970 us (0.43); the launches traced: 2240 us -> 969 us
  waiting for transfers between devices: 1090 us -> 629 us
  local copies, waits for them, and re-layouts: 374 us -> 20.6 us
  other arithmetic: 353 us -> 26.3 us
  matrix products: 276 us -> 31.4 us
  Pallas kernels: 0 us -> 169 us
  starting transfers between devices: 46.9 us -> 0.59 us
    ppermute x12 -> x0, waiting for transfers between devices: 321 us -> none  [from_behind(): return lax.ppermute(value, axis, pairs)]
    dot_general x76 -> x4, matrix products: 276 us -> 31.4 us  [weight_grad(): lax.dot_general(left.reshape(rows, -1), right.reshape(rows, -1), (((0,),...]
    reduce_scatter x4, waiting for transfers between devices: 527 us -> 337 us  [per_device(): lax.psum_scatter(t[None], 'dp', scatter_dimension=1, tiled=True).astype(F32)]
    pallas_call x0 -> x2, Pallas kernels: none -> 169 us  [the longest x1 127 us: run_backward(): pl.pallas_call(functools.partial(backward_kernel, line, length), out_shap...]
    dynamic_slice x94 -> x0, local copies, waits for them, and re-layouts: 137 us -> none  [the longest x70 116 us: store_slot(): old = lax.dynamic_index_in_dim(store, position, 0, keepdims=False)]
    dynamic_update_slice x87 -> x0, other arithmetic: 113 us -> none  [store_slot(): lax.dynamic_update_index_in_dim(store, jnp.where(valid, value, old), posi...]
    another operation x76 -> x0, local copies, waits for them, and re-layouts: 108 us -> none
    broadcast_in_dim x4 -> x0, other arithmetic: 81.3 us -> none  [the longest x1 27.3 us: per_device(): matrix_totals[2][None]]
  transfers between devices with their start and end apart: 21 -> 9, of which waited for: 15 -> 9; matrix products, arithmetic and copies ran while one was open for 11% -> 5% of each run, Pallas kernels for 0% -> 0%
where the time goes in v1:
time: 970 us; the launch traced here: 969 us
  waiting for transfers between devices  629 us (65%)
  Pallas kernels  169 us (17%)
  blocking collectives  73 us (8%)
  matrix products  31.4 us (3%)
  other arithmetic  26.3 us (3%)
  local copies, waits for them, and re-layouts  20.6 us (2%)
  between operations  19.2 us (2%)
    reduce_scatter x4, waiting for transfers between devices, per_device(): lax.psum_scatter(t[None], 'dp', scatter_dimension=1, tiled=True).astype(F32)  337 us
    all_gather x4, waiting for transfers between devices, per_device(): lax.all_gather(m.astype(BF), 'dp', axis=1, tiled=True)[0]  230 us
    pallas_call x1, Pallas kernels, run_backward(): pl.pallas_call(functools.partial(backward_kernel, line, length), out_shap...  127 us
    unnamed x10, waiting for transfers between devices  61 us
    pallas_call x1, Pallas kernels, run_forward(): pl.pallas_call(functools.partial(forward_kernel, line, length), out_shape...  41.9 us
    psum x1, blocking collectives, per_device(): grad_norm = jnp.sqrt(lax.psum(squares, ('dp', 'section')))  40.4 us
    all_gather x1, blocking collectives, per_device(): lax.all_gather(m.astype(BF), 'dp', axis=1, tiled=True)[0]  32.6 us
    dot_general x4, matrix products, weight_grad(): lax.dot_general(left.reshape(rows, -1), right.reshape(rows, -1), (((0,),...  31.4 us
  transfers between devices with their start and end apart: 9, of which 9 were waited for; matrix products, arithmetic and copies ran while one was open for 5% of the time, Pallas kernels for 0%

profile of v1, /device:TPU:0, one launch (start us, length us, event | category | flops | bytes accessed | tf_op | source)
XLA Modules:
  0.0 969.1 jit_solution(15380543252072952158)
XLA Ops:
  7.2 0.0 all-gather.7.cloned.1.call-start
  7.2 1.7 convert_element_type.50
  9.0 0.0 all-gather.7.cloned.1.call-update
  9.0 0.0 all-gather.5.cloned.1.call-start
  9.0 2.0 convert_element_type.49
  11.1 0.0 all-gather.9.cloned.1.call-start
  11.1 0.9 convert_element_type.51
  12.1 0.0 all-gather.11.cloned.1.call-start
  12.1 0.4 copy-done
  12.5 0.9 convert_element_type.52
  13.4 0.0 all-gather.11.cloned.1.call-update
  13.4 0.0 reduce-scatter.16.cloned.1.call-start
  13.5 32.6 %all_gather.19 = bf16[1,9216]{1,0:T(2,128)(2,1)S(1)} all-gather(bf16[1,1152]{1,0:T(2,128)(2,1)S(1)} %convert_element_type.53), channel_id=1, replica_groups=mesh['dp'=8,'section'=4] {'dp'}, dimensions={1}, use_global_device_ids=true | all-gather | bytes 20736 | tf_op jit(solution)/shard_map/all_gather | solution.py:488
  46.1 0.1 convert_reduce_fusion
  46.3 0.6 broadcast_in_dim.27.segr
  46.9 0.1 reshape.84
  47.0 0.1 reshape.85
  47.0 1.0 copy.58.segc
  48.1 2.8 pad.11.x_in
  50.9 1.2 pad.13.g_in
  52.1 0.1 pad.18.clone
  52.2 0.7 maximum_maximum_fusion.small
  52.9 1.7 all-gather.7.cloned.1.call-done
  54.5 66.7 %all-gather.5.cloned.1.call-done = bf16[1,768,2304]{2,1,0:T(8,128)(2,1)} async-done(((bf16[1,96,2304]{2,1,0:T(8,128)(2,1)}), bf16[1,768,2304]{2,1,0:T(8,128)(2,1)}) %all-gather.5.cloned.1.call-update) | async-done | bytes 3538960 | tf_op jit(solution)/shard_map/all_gather | solution.py:488
  121.3 81.2 %all-gather.9.cloned.1.call-done = bf16[1,768,3072]{2,1,0:T(8,128)(2,1)} async-done(((bf16[1,96,3072]{2,1,0:T(8,128)(2,1)}), bf16[1,768,3072]{2,1,0:T(8,128)(2,1)}) %all-gather.9.cloned.1.call-update) | async-done | bytes 4718608 | tf_op jit(solution)/shard_map/all_gather | solution.py:488
  202.4 80.7 %all-gather.11.cloned.1.call-done = bf16[1,3072,768]{2,1,0:T(8,128)(2,1)} async-done(((bf16[1,384,768]{2,1,0:T(8,128)(2,1)}), bf16[1,3072,768]{2,1,0:T(8,128)(2,1)}) %all-gather.11.cloned.1.call-update) | async-done | bytes 4718608 | tf_op jit(solution)/shard_map/all_gather | solution.py:488
  283.1 41.9 %forward_line.1 = (bf16[4,256,768]{2,1,0:T(8,128)(2,1)}, bf16[4,256,768]{2,1,0:T(8,128)(2,1)}, bf16[4,256,2304]{2,1,0:T(8,128)(2,1)}, f32[4,16,256]{2,1,0:T(8,12...) custom-call(bf16[4,256,768]{2,1,0:T(8,128)(2,1)} %pad.11.x_in, ...), custom_call_target="tpu_custom_call" | custom-call | tf_op jit(solution)/shard_map/forward_line/pallas_call | solution.py:415
  325.0 127.3 %backward_line.1 = (bf16[4,256,768]{2,1,0:T(8,128)(2,1)}, bf16[4,256,3072]{2,1,0:T(8,128)(2,1)}, bf16[4,256,768]{2,1,0:T(8,128)(2,1)}, bf16[4,256,2304]{2,1,0:T(...) custom-call(bf16[4,256,768]{2,1,0:T(8,128)(2,1)} %pad.13.g_in, bf16[4,256,768]{2,1,0:T(8,128)(2,1)} %get-tuple-element.40.x_h, ...), custom_call_target="tpu_custom_call" | custom-call | tf_op jit(solution)/shard_map/backward_line/pallas_call | solution.py:437
  452.3 0.7 slice.23
  453.0 0.7 slice.22
  453.8 0.1 reshape.87
  453.9 0.1 reshape.88
  454.0 3.0 copy.72
  457.0 4.0 bitcast_bitcast_fusion
  461.0 0.0 reduce-scatter.16.cloned.1.call-update
  461.0 0.0 reduce-scatter.10.cloned.1.call-start
  461.1 4.3 fusion.3
  465.4 0.0 reduce-scatter.10.cloned.1.call-update
  465.4 0.3 reduce-scatter.8.cloned.1.call-start
  465.7 8.6 fusion
  474.3 0.0 reduce-scatter.8.cloned.1.call-update
  474.3 0.0 reduce-scatter.12.cloned.1.call-start
  474.3 9.2 fusion.1
  483.5 0.0 reduce-scatter.14.cloned.1.call-start
  483.6 9.3 fusion.2
  492.9 60.9 %reduce-scatter.16.cloned.1.call-done = f32[1152,1]{1,0:T(8,128)} async-done(((f32[9216,1]{1,0:T(8,128)}), f32[1152,1]{1,0:T(8,128)}) %reduce-scatter.16.cloned.1.call-update) | async-done | bytes 4624
  553.8 1.3 copy.70
  555.1 0.6 multiply_reduce_fusion
  555.7 65.7 %reduce-scatter.10.cloned.1.call-done = bf16[1,96,768]{2,1,0:T(8,128)(2,1)} async-done(((bf16[1,768,768]{2,1,0:T(8,128)(2,1)}), bf16[1,96,768]{2,1,0:T(8,128)(2,1)}) %reduce-scatter.10.cloned.1.call-update) | async-done | bytes 147472 | tf_op jit(solution)/shard_map/reduce_scatter | solution.py:503
  621.4 1.6 fusion.10
  623.0 80.3 %reduce-scatter.8.cloned.1.call-done = bf16[1,96,2304]{2,1,0:T(8,128)(2,1)} async-done(((bf16[1,768,2304]{2,1,0:T(8,128)(2,1)}), bf16[1,96,2304]{2,1,0:T(8,128)(2,1)}) %reduce-scatter.8.cloned.1.call-update) | async-done | bytes 442384 | tf_op jit(solution)/shard_map/reduce_scatter | solution.py:503
  703.3 1.8 fusion.8
  706.4 95.4 %reduce-scatter.12.cloned.1.call-done = bf16[1,96,3072]{2,1,0:T(8,128)(2,1)} async-done(((bf16[1,768,3072]{2,1,0:T(8,128)(2,1)}), bf16[1,96,3072]{2,1,0:T(8,128)(2,1)}) %reduce-scatter.12.cloned.1.call-update) | async-done | bytes 589840 | tf_op jit(solution)/shard_map/reduce_scatter | solution.py:503
  801.8 2.0 fusion.4
  804.4 96.1 %reduce-scatter.14.cloned.1.call-done = bf16[1,384,768]{2,1,0:T(8,128)(2,1)} async-done(((bf16[1,3072,768]{2,1,0:T(8,128)(2,1)}), bf16[1,384,768]{2,1,0:T(8,128)(2,1)}) %reduce-scatter.14.cloned.1.call-update) | async-done | bytes 589840 | tf_op jit(solution)/shard_map/reduce_scatter | solution.py:503
  900.5 2.0 fusion.5
  903.8 3.7 slice_bitcast_fusion
  907.5 40.4 %psum.7 = f32[]{:T(128)} all-reduce(f32[]{:T(128)S(6)} %reduce_sum.69), channel_id=1, replica_groups=mesh['dp'=8,'section'=4] {'dp','section'}, use_global_device_ids=true, to_apply=%region_10.11 | all-reduce | flops 1 | bytes 8 | tf_op jit(solution)/shard_map/psum | solution.py:505
  948.7 1.4 multiply_subtract_fusion.4
  950.2 2.2 multiply_subtract_fusion.3
  952.4 3.3 multiply_subtract_fusion.2
  955.8 2.5 multiply_subtract_fusion
  958.3 0.5 copy-done.10
  958.9 2.6 multiply_subtract_fusion.1
  (44 shorter events, 0.3 us)
Async XLA Ops:
  7.2 3.9 copy-start.1
  7.2 47.3 %all-gather.7.cloned.1.call-start = ((), (), s32[]{:S(2)}) async-start(), calls=%async_computation.6 | async-start | bytes 1327104 | tf_op jit(solution)/shard_map/all_gather | solution.py:488
  9.0 112.3 %all-gather.5.cloned.1.call-start = ((), (), s32[]{:S(2)}) async-start(), calls=%async_computation.5 | async-start | bytes 3981312 | tf_op jit(solution)/shard_map/all_gather | solution.py:488
  11.1 1.5 copy-start
  11.1 191.4 %all-gather.9.cloned.1.call-start = ((), (), s32[]{:S(2)}) async-start(), calls=%async_computation.7 | async-start | bytes 5308416 | tf_op jit(solution)/shard_map/all_gather | solution.py:488
  12.0 1.5 copy-start.13
  12.0 34.2 %copy-start.14 = (s32[4,248]{1,0:T(4,128)S(1)}, s32[4,248]{1,0:T(4,128)}, u32[]{:S(2)}) copy-start(s32[4,248]{1,0:T(4,128)} %param.21) | copy-start | bytes 11908
  12.1 271.1 %all-gather.11.cloned.1.call-start = ((), (), s32[]{:S(2)}) async-start(), calls=%async_computation.8 | async-start | bytes 5308416 | tf_op jit(solution)/shard_map/all_gather | solution.py:488
  13.4 540.4 %reduce-scatter.16.cloned.1.call-start = ((), (), s32[]{:S(2)}) async-start(), calls=%async_computation.13 | async-start | bytes 5308416
  48.1 2.8 copy-start.6
  461.0 160.4 %reduce-scatter.10.cloned.1.call-start = ((), (), s32[]{:S(2)}) async-start(), calls=%async_computation.10 | async-start | bytes 1327104 | tf_op jit(solution)/shard_map/reduce_scatter | solution.py:503
  465.4 237.9 %reduce-scatter.8.cloned.1.call-start = ((), (), s32[]{:S(2)}) async-start(), calls=%async_computation.9 | async-start | bytes 3981312 | tf_op jit(solution)/shard_map/reduce_scatter | solution.py:503
  474.3 327.5 %reduce-scatter.12.cloned.1.call-start = ((), (), s32[]{:S(2)}) async-start(), calls=%async_computation.11 | async-start | bytes 5308416 | tf_op jit(solution)/shard_map/reduce_scatter | solution.py:503
  483.5 417.0 %reduce-scatter.14.cloned.1.call-start = ((), (), s32[]{:S(2)}) async-start(), calls=%async_computation.12 | async-start | bytes 5308416 | tf_op jit(solution)/shard_map/reduce_scatter | solution.py:503
  903.8 46.4 %copy-start.11 = (f32[1,96,768]{2,1,0:T(8,128)S(1)}, f32[1,96,768]{2,1,0:T(8,128)}, u32[]{:S(2)}) copy-start(f32[1,96,768]{2,1,0:T(8,128)} %param.24) | copy-start | bytes 884740
  907.5 44.8 %copy-start.2 = (f32[1,96,2304]{2,1,0:T(8,128)S(1)}, f32[1,96,2304]{2,1,0:T(8,128)}, u32[]{:S(2)}) copy-start(f32[1,96,2304]{2,1,0:T(8,128)} %param.23) | copy-start | bytes 2654212
  948.7 3.6 copy-start.5
  948.7 3.6 copy-start.12
  952.4 3.4 copy-start.4
  952.4 3.4 copy-start.7
  952.4 3.4 copy-start.8
  955.8 2.6 copy-start.3
  955.8 2.6 copy-start.9
  955.8 3.1 copy-start.10
Sparse Core Ops, SparseCore 0:
  10.8 43.7 all-gather.6
  57.3 63.9 all-gather.4
  124.0 78.3 all-gather.8
  205.1 78.0 all-gather.10
  461.1 92.6 reduce-scatter.15
  557.6 63.7 reduce-scatter.9
  625.1 78.2 reduce-scatter.7
  706.9 94.8 reduce-scatter.11
  805.5 95.0 reduce-scatter.13

commit v2 on v1

--- a/solution.py
+++ b/solution.py
@@ -179,7 +179,50 @@
         return {self.axis: lax.axis_index(self.axis) + by * self.stride}
 
 
-def greet(line):
+class Spot:
+    def __init__(self, x, y, z, c):
+        self.x, self.y, self.z, self.c = x, y, z, c
+
+    @staticmethod
+    def here():
+        dp, section = lax.axis_index("dp"), lax.axis_index("section")
+        return Spot(dp % 2, section // 2, dp // 2, section % 2)
+
+    def dp(self):
+        return self.z * 2 + self.x
+
+    def section(self):
+        return self.y * 2 + self.c
+
+    def id(self):
+        return (self.dp(), self.section())
+
+    def flip(self, x=0, y=0, c=0):
+        return Spot(1 - self.x if x else self.x, 1 - self.y if y else self.y, self.z, 1 - self.c if c else self.c)
+
+    def turned(self):
+        return Spot(self.x, self.z // 2, self.section(), self.z % 2)
+
+    def drop(self):
+        return Spot(self.x, (self.y + self.z + self.c) % 2, self.section(), self.z // 2)
+
+    def source(self):
+        y, c = self.z // 2, self.z % 2
+        return Spot(self.x, y, 2 * self.c + (self.y + y + c) % 2, c)
+
+    def part(self):
+        return self.source().dp()
+
+
+def same(one, other):
+    return (one.dp() == other.dp()) & (one.section() == other.section())
+
+
+def hail(spot):
+    pl.semaphore_signal(pltpu.get_barrier_semaphore(), inc=1, device_id=spot.id(), device_id_type=MESH)
+
+
+def greet(line, turned):
     stage = line.stage()
     barrier = pltpu.get_barrier_semaphore()
 
@@ -192,10 +235,19 @@
         pl.semaphore_signal(barrier, inc=1, device_id=line.beside(1), device_id_type=MESH)
 
     expected = jnp.where(stage > 0, 1, 0) + jnp.where(stage < line.count - 1, 1, 0)
+    if turned:
+        me = Spot.here()
+        alone = same(me, me.turned())
+
+        @pl.when(jnp.logical_not(alone))
+        def _():
+            hail(me.turned())
+
+        expected = expected + jnp.where(alone, 0, 1)
     pl.semaphore_wait(barrier, expected)
 
 
-def forward_kernel(line, length, x_in, segr, segc, cls, wqkv_h, wproj_h, wup_h, wdown_h, small,
+def forward_kernel(line, length, turned, x_first, x_in, segr, segc, cls, wqkv_h, wproj_h, wup_h, wdown_h, small,
                    x_o, a_o, qkv_o, lse_o, o_o, h_o, a2_o, gp_o, u_o, acts_o,
                    wqkv, wproj, wup, wdown, xs, outs, a, qkv, lse, o, h, a2, gp, u, bias, ot,
                    w_sem, in_sem, x_sem, save_sem, act_sem, send_sem, recv_sem):
@@ -211,12 +263,38 @@
     def first_in(m):
         return pltpu.make_async_copy(x_in.at[m], xs.at[m], in_sem.at[m])
 
-    @pl.when(stage == 0)
-    def _():
-        for m in range(micro):
-            first_in(m).start()
-
-    greet(line)
+    greet(line, turned)
+    if turned:
+        me = Spot.here()
+        partner = me.turned()
+        alone = same(me, partner)
+
+        def turn_in(m):
+            return pltpu.make_async_remote_copy(
+                src_ref=x_in.at[m], dst_ref=xs.at[m], send_sem=in_sem.at[m], recv_sem=recv_sem.at[m],
+                device_id=partner.id(), device_id_type=MESH)
+
+        feeds = jnp.logical_and(me.section() == 0, jnp.logical_not(alone))
+        fed = jnp.logical_and(stage == 0, jnp.logical_not(alone))
+        feeds_self = jnp.logical_and(stage == 0, alone)
+
+        @pl.when(stage == 0)
+        def _():
+            pltpu.make_async_copy(x_first, xs.at[0], in_sem.at[0]).start()
+
+        for m in range(1, micro):
+            @pl.when(feeds)
+            def _():
+                turn_in(m).start()
+
+            @pl.when(feeds_self)
+            def _():
+                first_in(m).start()
+    else:
+        @pl.when(stage == 0)
+        def _():
+            for m in range(micro):
+                first_in(m).start()
 
     saved = ((a, a_o), (qkv, qkv_o), (lse, lse_o), (o, o_o), (h, h_o), (a2, a2_o), (gp, gp_o), (u, u_o))
 
@@ -234,11 +312,16 @@
     def step(m, carry):
         slot = lax.rem(m, 2)
 
-        @pl.when(stage == 0)
+        if turned:
+            here = jnp.logical_or(feeds_self, jnp.logical_and(stage == 0, m == 0))
+        else:
+            here = stage == 0
+
+        @pl.when(here)
         def _():
             first_in(m).wait()
 
-        @pl.when(stage > 0)
+        @pl.when(jnp.logical_not(here))
         def _():
             hop(m).wait_recv()
 
@@ -289,12 +372,18 @@
         for m in range(micro):
             hop(m).wait_send()
 
-
-def backward_kernel(line, length, g_in, x_h, qkv_h, lse_h, h_h, gp_h, segr, segc, cls,
+    if turned:
+        @pl.when(feeds)
+        def _():
+            for m in range(1, micro):
+                turn_in(m).wait_send()
+
+
+def backward_kernel(line, length, turned, acts_h, g_in, x_h, qkv_h, lse_h, h_h, gp_h, segr, segc, cls,
                     wqkv_h, wproj_h, wup_h, wdown_h, small,
-                    g_o, dz_o, f_o, r_o, gin_o, sums_o,
+                    acts_o, g_o, dz_o, f_o, r_o, gin_o, sums_o,
                     wqkv, wproj, wup, wdown, gs, gins, x, qkv, lse, h, gp, dz, f, r, bias, do, dh, dqt,
-                    w_sem, in_sem, g_sem, load_sem, save_sem, act_sem, send_sem, recv_sem):
+                    w_sem, in_sem, g_sem, load_sem, save_sem, act_sem, send_sem, recv_sem, home_sem):
     micro = gs.shape[0]
     stage = line.stage()
     loads = [
@@ -324,7 +413,26 @@
     for load in loads[1:]:
         load.start()
     sums_o[...] = jnp.zeros_like(sums_o)
-    greet(line)
+    greet(line, turned)
+    if turned:
+        me = Spot.here()
+        partner = me.turned()
+        alone = same(me, partner)
+
+        def home(m):
+            return pltpu.make_async_remote_copy(
+                src_ref=acts_h.at[m], dst_ref=acts_o.at[m], send_sem=home_sem.at[0, m], recv_sem=home_sem.at[1, m],
+                device_id=partner.id(), device_id_type=MESH)
+
+        def stay(m):
+            return pltpu.make_async_copy(acts_h.at[m], acts_o.at[m], home_sem.at[0, m])
+
+        for m in range(micro):
+            pl.when(alone)(lambda: stay(m).start())
+            pl.when(jnp.logical_not(alone))(lambda: home(m).start())
+    else:
+        for m in range(micro):
+            pltpu.make_async_copy(acts_h.at[m], acts_o.at[m], home_sem.at[0, m]).start()
 
     saved = ((dz, dz_o), (f, f_o), (r, r_o))
 
@@ -397,6 +505,13 @@
         for m in range(micro):
             hop(m).wait_send()
 
+    for m in range(micro):
+        if turned:
+            pl.when(alone)(lambda: stay(m).wait())
+            pl.when(jnp.logical_not(alone))(lambda: home(m).wait())
+        else:
+            pltpu.make_async_copy(acts_h.at[m], acts_o.at[m], home_sem.at[0, m]).wait()
+
 
 IN_VMEM = pl.BlockSpec(memory_space=pltpu.VMEM)
 IN_SMEM = pl.BlockSpec(memory_space=pltpu.SMEM)
@@ -404,7 +519,7 @@
 DMA = pltpu.SemaphoreType.DMA
 
 
-def run_forward(line, length, x_in, segr, segc, cls, weights, small):
+def run_forward(line, length, turned, x_first, x_in, segr, segc, cls, weights, small):
     micro, rows, width = x_in.shape
     hidden = weights[2].shape[1]
     shape = jax.ShapeDtypeStruct
@@ -413,9 +528,9 @@
         ((rows, width), F32), ((rows, width), BF), ((rows, hidden), BF), ((rows, hidden), BF))
     many = shape((micro, rows, width), BF)
     return pl.pallas_call(
-        functools.partial(forward_kernel, line, length),
+        functools.partial(forward_kernel, line, length, turned),
         out_shape=[many] + [shape((micro,) + s, t) for s, t in saved] + [many],
-        in_specs=[ANYWHERE, IN_VMEM, IN_VMEM, IN_SMEM] + [ANYWHERE] * 4 + [IN_VMEM],
+        in_specs=[ANYWHERE, ANYWHERE, IN_VMEM, IN_VMEM, IN_SMEM] + [ANYWHERE] * 4 + [IN_VMEM],
         out_specs=[ANYWHERE] * 10,
         scratch_shapes=[pltpu.VMEM(w.shape, BF) for w in weights]
         + [pltpu.VMEM((micro, rows, width), BF)] * 2
@@ -425,21 +540,21 @@
         compiler_params=pltpu.CompilerParams(
             collective_id=0, has_side_effects=True, vmem_limit_bytes=VMEM_CAP),
         name="forward_line",
-    )(x_in, segr, segc, cls, *weights, small)
-
-
-def run_backward(line, length, g_in, x, qkv, lse, h, gp, segr, segc, cls, weights, small):
+    )(x_first, x_in, segr, segc, cls, *weights, small)
+
+
+def run_backward(line, length, turned, acts, g_in, x, qkv, lse, h, gp, segr, segc, cls, weights, small):
     micro, rows, width = g_in.shape
     hidden = weights[2].shape[1]
     shape = jax.ShapeDtypeStruct
     many = shape((micro, rows, width), BF)
     wqkv, wproj, wup, wdown = weights
     return pl.pallas_call(
-        functools.partial(backward_kernel, line, length),
-        out_shape=[many, shape((micro, rows, hidden), BF), many, shape((micro, rows, 3 * width), BF), many,
+        functools.partial(backward_kernel, line, length, turned),
+        out_shape=[many, many, shape((micro, rows, hidden), BF), many, shape((micro, rows, 3 * width), BF), many,
                    shape((16, width), F32)],
-        in_specs=[ANYWHERE] * 6 + [IN_VMEM, IN_VMEM, IN_SMEM] + [ANYWHERE] * 4 + [IN_VMEM],
-        out_specs=[ANYWHERE] * 5 + [IN_VMEM],
+        in_specs=[ANYWHERE] * 7 + [IN_VMEM, IN_VMEM, IN_SMEM] + [ANYWHERE] * 4 + [IN_VMEM],
+        out_specs=[ANYWHERE] * 6 + [IN_VMEM],
         scratch_shapes=[pltpu.VMEM(w.shape, BF) for w in weights]
         + [pltpu.VMEM((micro, rows, width), BF)] * 2
         + [pltpu.VMEM((2, rows, width), BF), pltpu.VMEM((2, rows, 3 * width), BF), pltpu.VMEM((2, 16, rows), F32),
@@ -448,11 +563,328 @@
            pltpu.VMEM((rows, rows), F32), pltpu.VMEM((rows, width), BF), pltpu.VMEM((rows, width), F32),
            pltpu.VMEM((width, rows), BF)]
         + [DMA((4,)), DMA((micro,)), DMA((micro,)), DMA((2, 5)), DMA((2, 3)), DMA((micro,)), DMA((micro,)),
-           DMA((micro,))],
+           DMA((micro,)), DMA((2, micro))],
         compiler_params=pltpu.CompilerParams(
             collective_id=1, has_side_effects=True, vmem_limit_bytes=VMEM_CAP),
         name="backward_line",
-    )(g_in, x, qkv, lse, h, gp, segr, segc, cls, wqkv, wproj, wup, wdown, small)
+    )(acts, g_in, x, qkv, lse, h, gp, segr, segc, cls, wqkv, wproj, wup, wdown, small)
+
+
+GATHER_PIECES = ((0, 0, 96), (4, 0, 16), (1, 0, 96), (2, 0, 48), (2, 48, 48), (3, 0, 192), (3, 192, 192))
+SCATTER_PIECES = ((3, 0, 192), (3, 192, 192), (2, 0, 48), (2, 48, 48), (0, 0, 96), (1, 0, 96), (4, 0, 16))
+
+
+def gather_kernel(pieces, micro, *refs):
+    count = 5
+    shares, (x_in, g_in, seg_in) = refs[:count], refs[count : count + 3]
+    wholes, (x_o, g_o, seg_o) = refs[count + 3 : 2 * count + 3], refs[2 * count + 3 : 2 * count + 6]
+    send, recv, local, turn_send, turn_recv = refs[2 * count + 6 :]
+    me = Spot.here()
+    xn, yn, cn = me.flip(x=1), me.flip(y=1), me.flip(c=1)
+    target, source, partner = me.drop(), me.source(), me.turned()
+    stays, alone = same(me, target), same(me, partner)
+    moves, pairs = jnp.logical_not(stays), jnp.logical_not(alone)
+    for spot in (xn, yn, cn):
+        hail(spot)
+
+    @pl.when(moves)
+    def _():
+        hail(target)
+        hail(source)
+
+    @pl.when(pairs)
+    def _():
+        hail(partner)
+
+    pl.semaphore_wait(pltpu.get_barrier_semaphore(), 3 + jnp.where(stays, 0, 2) + jnp.where(alone, 0, 1))
+
+    def rows(k, part):
+        array, first, size = pieces[k]
+        share = shares[array].shape[0]
+        return wholes[array].at[pl.ds(pl.multiple_of(part * share + first, 16), size)]
+
+    def mine(k):
+        array, first, size = pieces[k]
+        return shares[array].at[pl.ds(first, size)]
+
+    def remote(src, dst, kind, k, spot):
+        return pltpu.make_async_remote_copy(
+            src_ref=src, dst_ref=dst, send_sem=send.at[kind, k], recv_sem=recv.at[kind, k],
+            device_id=spot.id(), device_id_type=MESH)
+
+    def brought(k, part):
+        return remote(mine(k), rows(k, part), 0, k, target)
+
+    def kept(k):
+        return pltpu.make_async_copy(mine(k), rows(k, me.dp()), local.at[k])
+
+    def passed(kind, k, part, spot):
+        return remote(rows(k, part), rows(k, part), kind, k, spot)
+
+    def parts(spot):
+        return [s.part() for s in (spot, spot.flip(x=1), spot.flip(y=1), spot.flip(x=1, y=1))]
+
+    own, own_x, own_y, own_d = parts(me)
+    beside = parts(cn)
+    turns = [(x_in, x_o), (seg_in, seg_o)] + [(g_in.at[m], g_o.at[m]) for m in range(micro)]
+    gives = [me.section() == 0, me.section() >= 0] + [me.section() == 3] * micro
+    takes = [me.z == 0, me.z >= 0] + [me.z == 3] * micro
+
+    def turn(i):
+        return pltpu.make_async_remote_copy(
+            src_ref=turns[i][0], dst_ref=turns[i][1], send_sem=turn_send.at[i], recv_sem=turn_recv.at[i],
+            device_id=partner.id(), device_id_type=MESH)
+
+    def turn_start(i):
+        pl.when(gives[i] & alone)(lambda: pltpu.make_async_copy(*turns[i], turn_send.at[i]).start())
+        pl.when(gives[i] & pairs)(lambda: turn(i).start())
+
+    def turn_end(i):
+        pl.when(gives[i] & alone)(lambda: pltpu.make_async_copy(*turns[i], turn_send.at[i]).wait())
+        pl.when(gives[i] & pairs)(lambda: turn(i).wait_send())
+        pl.when(takes[i] & pairs)(lambda: turn(i).wait_recv())
+
+    for k in range(len(pieces)):
+        pl.when(stays)(lambda: kept(k).start())
+        pl.when(moves)(lambda: brought(k, me.dp()).start())
+    turn_start(1)
+    turn_start(0)
+    for i in range(2, 2 + micro):
+        turn_start(i)
+    for k in range(len(pieces) + 2):
+        if k < len(pieces):
+            pl.when(stays)(lambda: kept(k).wait())
+            pl.when(moves)(lambda: brought(k, own).wait_recv())
+            passed(1, k, own, xn).start()
+            passed(2, k, own, yn).start()
+            passed(4, k, own, cn).start()
+        if 0 <= k - 1 < len(pieces):
+            passed(1, k - 1, own_x, xn).wait_recv()
+            passed(5, k - 1, own_x, cn).start()
+            pl.when(me.c == 0)(lambda: passed(3, k - 1, own_x, yn).start())
+            passed(2, k - 1, own_y, yn).wait_recv()
+            passed(6, k - 1, own_y, cn).start()
+            pl.when(me.c == 1)(lambda: passed(3, k - 1, own_y, xn).start())
+        if 0 <= k - 2 < len(pieces):
+            passed(3, k - 2, own_d, yn).wait_recv()
+            passed(7, k - 2, own_d, cn).start()
+    for k in range(len(pieces)):
+        for kind in range(4, 8):
+            passed(kind, k, beside[kind - 4], cn).wait_recv()
+        pl.when(moves)(lambda: brought(k, own).wait_send())
+        for kind in range(1, 8):
+            passed(kind, k, own, cn).wait_send()
+    for i in range(len(turns)):
+        turn_end(i)
+
+
+def run_gather(shares, x_first, g, segs):
+    pieces = GATHER_PIECES
+    micro = g.shape[0]
+    shape = jax.ShapeDtypeStruct
+    outs = [shape((s.shape[0] * 8,) + s.shape[1:], s.dtype) for s in shares]
+    outs += [shape(v.shape, v.dtype) for v in (x_first, g, segs)]
+    return pl.pallas_call(
+        functools.partial(gather_kernel, pieces, micro),
+        out_shape=outs,
+        in_specs=[ANYWHERE] * 8,
+        out_specs=[ANYWHERE] * 8,
+        scratch_shapes=[DMA((8, len(pieces))), DMA((8, len(pieces))), DMA((len(pieces),)), DMA((2 + micro,)),
+                        DMA((2 + micro,))],
+        compiler_params=pltpu.CompilerParams(collective_id=2, has_side_effects=True),
+        name="gather_layers",
+    )(*shares, x_first, g, segs)
+
+
+def scatter_kernel(pieces, micro, *refs):
+    count = 5
+    totals, gin_in = refs[:count], refs[count]
+    outs, gin_o, norm_o = refs[count + 1 : 2 * count + 1], refs[2 * count + 1], refs[2 * count + 2]
+    at = 2 * count + 3
+    held, beside, diag, from_x, from_y, done, home = (refs[at + i * count : at + (i + 1) * count] for i in range(7))
+    sums, tallies, load, send, recv, local, turn_sem, note_send, note_recv, out_sem = refs[at + 7 * count :]
+    me = Spot.here()
+    xn, yn, cn = me.flip(x=1), me.flip(y=1), me.flip(c=1)
+    target, partner = me.source(), me.turned()
+    giver = me.drop()
+    stays, alone = same(me, target), same(me, partner)
+    moves, pairs = jnp.logical_not(stays), jnp.logical_not(alone)
+    slab = [me.flip(x=i & 1, y=(i >> 1) & 1, c=i >> 2) for i in range(1, 8)]
+    column = [Spot(me.x, me.y, (me.z + i) % 4, me.c) for i in range(1, 4)]
+    for spot in slab + column:
+        hail(spot)
+
+    @pl.when(moves)
+    def _():
+        hail(target)
+        hail(giver)
+
+    @pl.when(pairs)
+    def _():
+        hail(partner)
+
+    pl.semaphore_wait(pltpu.get_barrier_semaphore(), 10 + jnp.where(stays, 0, 2) + jnp.where(alone, 0, 1))
+
+    def parts(spot):
+        return [s.part() for s in (spot, spot.flip(x=1), spot.flip(y=1), spot.flip(x=1, y=1))]
+
+    kept, given = parts(me), parts(cn)
+
+    def whole(k, part):
+        array, first, size = pieces[k]
+        share = done[array].shape[0]
+        return totals[array].at[pl.ds(pl.multiple_of(part * share + first, 16), size)]
+
+    def span(k):
+        return pl.ds(pieces[k][1], pieces[k][2])
+
+    def remote(src, dst, kind, k, spot):
+        return pltpu.make_async_remote_copy(
+            src_ref=src, dst_ref=dst, send_sem=send.at[kind, k], recv_sem=recv.at[kind, k],
+            device_id=spot.id(), device_id_type=MESH)
+
+    def loaded(k, j):
+        return pltpu.make_async_copy(whole(k, kept[j]), held[pieces[k][0]].at[j, span(k)], load.at[j, k])
+
+    def crossed(k, j):
+        return remote(whole(k, given[j]), beside[pieces[k][0]].at[j, span(k)], j, k, cn)
+
+    def to_diag(k, spot):
+        return remote(held[pieces[k][0]].at[3, span(k)], diag[pieces[k][0]].at[span(k)], 4, k, spot)
+
+    def to_x(k):
+        return remote(held[pieces[k][0]].at[1, span(k)], from_x[pieces[k][0]].at[span(k)], 5, k, xn)
+
+    def to_y(k):
+        return remote(held[pieces[k][0]].at[2, span(k)], from_y[pieces[k][0]].at[span(k)], 6, k, yn)
+
+    def to_home(k):
+        return remote(done[pieces[k][0]].at[span(k)], home[pieces[k][0]].at[span(k)], 7, k, target)
+
+    def stay_home(k):
+        return pltpu.make_async_copy(done[pieces[k][0]].at[span(k)], home[pieces[k][0]].at[span(k)], local.at[k])
+
+    def add(k, j, extra):
+        array = held[pieces[k][0]]
+        array[j, span(k)] = (array[j, span(k)].astype(F32) + extra.astype(F32)).astype(array.dtype)
+
+    def turn(m):
+        return pltpu.make_async_remote_copy(
+            src_ref=gin_in.at[m], dst_ref=gin_o.at[m], send_sem=turn_sem.at[0, m], recv_sem=turn_sem.at[1, m],
+            device_id=partner.id(), device_id_type=MESH)
+
+    def turn_stay(m):
+        return pltpu.make_async_copy(gin_in.at[m], gin_o.at[m], turn_sem.at[0, m])
+
+    for k in range(len(pieces)):
+        for j in (3, 2, 1, 0):
+            crossed(k, j).start()
+            loaded(k, j).start()
+    for m in range(micro):
+        pl.when(alone)(lambda: turn_stay(m).start())
+        pl.when(pairs)(lambda: turn(m).start())
+    for k in range(len(pieces) + 2):
+        if k < len(pieces):
+            array = pieces[k][0]
+            for j in (3, 2, 1, 0):
+                loaded(k, j).wait()
+                crossed(k, j).wait_recv()
+                add(k, j, beside[array][j, span(k)])
+                if j == 3:
+                    pl.when(me.c == 0)(lambda: to_diag(k, yn).start())
+                    pl.when(me.c == 1)(lambda: to_diag(k, xn).start())
+                if j == 2:
+                    pl.when(me.c == 0)(lambda: to_y(k).start())
+                if j == 1:
+                    pl.when(me.c == 1)(lambda: to_x(k).start())
+        if 0 <= k - 1 < len(pieces):
+            b = k - 1
+            to_diag(b, yn).wait_recv()
+
+            @pl.when(me.c == 0)
+            def _():
+                add(b, 1, diag[pieces[b][0]][span(b)])
+                to_x(b).start()
+
+            @pl.when(me.c == 1)
+            def _():
+                add(b, 2, diag[pieces[b][0]][span(b)])
+                to_y(b).start()
+        if 0 <= k - 2 < len(pieces):
+            b = k - 2
+            array = pieces[b][0]
+            to_x(b).wait_recv()
+            to_y(b).wait_recv()
+            total = (held[array][0, span(b)].astype(F32) + from_x[array][span(b)].astype(F32)
+                     + from_y[array][span(b)].astype(F32))
+            done[array][span(b)] = total.astype(done[array].dtype)
+            pl.when(stays)(lambda: stay_home(b).start())
+            pl.when(moves)(lambda: to_home(b).start())
+    tally = jnp.zeros((8, 128), F32)
+    for k in range(len(pieces)):
+        pl.when(stays)(lambda: stay_home(k).wait())
+        pl.when(moves)(lambda: to_home(k).wait_recv())
+        array = pieces[k][0]
+        value = home[array][span(k)].astype(F32)
+        value = value * value
+        tally = tally + jnp.sum(value.reshape(-1, 8, value.shape[1] // 128, 128), axis=(0, 2))
+    sums[0] = tally
+
+    def note(i, src, slot, spot):
+        return pltpu.make_async_remote_copy(
+            src_ref=src, dst_ref=tallies.at[slot], send_sem=note_send.at[i], recv_sem=note_recv.at[slot],
+            device_id=spot.id(), device_id_type=MESH)
+
+    for i, spot in enumerate(column):
+        note(i, sums.at[0], i, spot).start()
+    for array in range(count):
+        pltpu.make_async_copy(home[array], outs[array], out_sem.at[array]).start()
+    for i, spot in enumerate(column):
+        note(i, sums.at[0], i, spot).wait_recv()
+        tally = tally + tallies[i]
+    sums[1] = tally
+    for i, spot in enumerate(slab):
+        note(3 + i, sums.at[1], 3 + i, spot).start()
+    for i, spot in enumerate(slab):
+        note(3 + i, sums.at[1], 3 + i, spot).wait_recv()
+        tally = tally + tallies[3 + i]
+    norm_o[...] = tally
+    for i, spot in enumerate(column):
+        note(i, sums.at[0], i, spot).wait_send()
+    for i, spot in enumerate(slab):
+        note(3 + i, sums.at[1], 3 + i, spot).wait_send()
+    for k in range(len(pieces)):
+        for j in range(4):
+            crossed(k, j).wait_send()
+        to_diag(k, yn).wait_send()
+        to_x(k).wait_send()
+        to_y(k).wait_send()
+        pl.when(moves)(lambda: to_home(k).wait_send())
+    for m in range(micro):
+        pl.when(alone)(lambda: turn_stay(m).wait())
+        pl.when(pairs)(lambda: turn(m).wait())
+    for array in range(count):
+        pltpu.make_async_copy(home[array], outs[array], out_sem.at[array]).wait()
+
+
+def run_scatter(totals, gin):
+    pieces = SCATTER_PIECES
+    micro = gin.shape[0]
+    shape = jax.ShapeDtypeStruct
+    shares = [((t.shape[0] // 8, t.shape[1]), t.dtype) for t in totals]
+    four = [pltpu.VMEM((4,) + s, t) for s, t in shares]
+    one = [pltpu.VMEM(s, t) for s, t in shares]
+    return pl.pallas_call(
+        functools.partial(scatter_kernel, pieces, micro),
+        out_shape=[shape(s, t) for s, t in shares] + [shape(gin.shape, gin.dtype), shape((8, 128), F32)],
+        in_specs=[ANYWHERE] * 6,
+        out_specs=[ANYWHERE] * 6 + [IN_VMEM],
+        scratch_shapes=four + four + one * 5
+        + [pltpu.VMEM((2, 8, 128), F32), pltpu.VMEM((10, 8, 128), F32), DMA((4, len(pieces))), DMA((8, len(pieces))),
+           DMA((8, len(pieces))), DMA((len(pieces),)), DMA((2, micro)), DMA((10,)), DMA((10,)), DMA((5,))],
+        compiler_params=pltpu.CompilerParams(collective_id=3, has_side_effects=True, vmem_limit_bytes=VMEM_CAP),
+        name="scatter_layers",
+    )(*totals, gin)
 
 
 def split_small(small, width, slices):
@@ -481,28 +913,49 @@
 def per_device(inputs, out_grad, segment_ids, cls_index, *states):
     masters, firsts, seconds = states[0:5], states[5:10], states[10:15]
     slices = lax.axis_size("dp")
-    line = Line("section", lax.axis_size("section"), 1)
+    stages = lax.axis_size("section")
+    turned = slices == 8 and stages == 4
     seq_dev, length, width = inputs.shape
     rows = -(-length // 128) * 128
-
-    gathered = [lax.all_gather(m.astype(BF), "dp", axis=1, tiled=True)[0] for m in masters]
-    weights = gathered[:4]
-    total = gathered[4].shape[0]
-    small = split_small(gathered[4].astype(F32), width, slices)
+    total = masters[4].shape[1] * slices
 
     extra = ((0, 0), (0, rows - length), (0, 0))
     x_in = jnp.pad(inputs, extra)
     g_in = jnp.pad(out_grad, extra)
     segs = jnp.pad(segment_ids, ((0, 0), (0, rows - length)), constant_values=-1)
+    shares = [m.astype(BF)[0] for m in masters]
+    if turned:
+        line = Line("dp", 4, 2)
+        lanes = masters[4].shape[1] // 128
+        shares[4] = jnp.pad(shares[4].astype(F32).reshape(lanes, 128), ((0, 16 - lanes), (0, 0)))
+        words = jnp.concatenate([segs, jnp.broadcast_to(cls_index[:, None], (seq_dev, rows))], axis=0)
+        *gathered, x_first, g_in, words = run_gather(shares, x_in[0], g_in, words)
+        segs, classes = words[:seq_dev], words[seq_dev:, 0]
+        flat = gathered[4].reshape(slices, 16, 128)[:, :lanes].reshape(-1)
+    else:
+        line = Line("section", stages, 1)
+        gathered = [lax.all_gather(s, "dp", axis=0, tiled=True) for s in shares]
+        flat, classes, x_first = gathered[4].astype(F32), cls_index, x_in[0]
+    weights = gathered[:4]
+    small = split_small(flat, width, slices)
     segr, segc = segs[:, None, :], segs[:, :, None]
 
-    x, a, qkv, lse, o, h, a2, gp, u, acts = run_forward(line, length, x_in, segr, segc, cls_index, weights, small)
-    g, dz, f, r, gin, sums = run_backward(line, length, g_in, x, qkv, lse, h, gp, segr, segc, cls_index, weights, small)
+    x, a, qkv, lse, o, h, a2, gp, u, acts = run_forward(
+        line, length, turned, x_first, x_in, segr, segc, classes, weights, small)
+    acts, g, dz, f, r, gin, sums = run_backward(
+        line, length, turned, acts, g_in, x, qkv, lse, h, gp, segr, segc, classes, weights, small)
     totals = [weight_grad(a, r).astype(BF), weight_grad(o, f).astype(BF), weight_grad(a2, dz).astype(BF),
               weight_grad(u, g).astype(BF), join_small(sums, total, slices)]
-    shards = [lax.psum_scatter(t[None], "dp", scatter_dimension=1, tiled=True).astype(F32) for t in totals]
-    squares = jnp.sum(jnp.stack([jnp.sum(s * s) for s in shards]))
-    grad_norm = jnp.sqrt(lax.psum(squares, ("dp", "section")))
+    if turned:
+        table = jnp.pad(totals[4].reshape(slices, lanes, 128), ((0, 0), (0, 16 - lanes), (0, 0)))
+        *shards, gin, tally = run_scatter(totals[:4] + [table.reshape(slices * 16, 128)], gin)
+        shards[4] = shards[4][:lanes].reshape(-1)
+        shards = [s.astype(F32)[None] for s in shards]
+        grad_norm = jnp.sqrt(jnp.sum(tally))
+    else:
+        shards = [lax.psum_scatter(t[None], "dp", scatter_dimension=1, tiled=True).astype(F32) for t in totals]
+        squares = jnp.sum(jnp.stack([jnp.sum(s * s) for s in shards]))
+        grad_norm = jnp.sqrt(lax.psum(squares, ("dp", "section")))
     factor = 1.0 / jnp.maximum(grad_norm, 1.0)
     fix = 1.0 - 0.5**STEP
     results = []

time: 970 us -> 597 us (0.62)
  waiting for transfers between devices: 629 us -> 0 us
  Pallas kernels: 169 us -> 517 us
  blocking collectives: 73 us -> 0 us
  between operations: 19.2 us -> 3.19 us
    pallas_call x2 -> x4, Pallas kernels: 169 us -> 517 us  [the longest x1 199 us: run_backward(): pl.pallas_call(functools.partial(backward_kernel, line, length, turned),...]
    reduce_scatter x4 -> x0, waiting for transfers between devices: 337 us -> none  [per_device(): lax.psum_scatter(t[None], 'dp', scatter_dimension=1, tiled=True).astype(F32)]
    all_gather x4 -> x0, waiting for transfers between devices: 230 us -> none  [per_device(): lax.all_gather(m.astype(BF), 'dp', axis=1, tiled=True)[0]]
    unnamed x10 -> x0, waiting for transfers between devices: 61 us -> none
    psum x1 -> x0, blocking collectives: 40.4 us -> none  [per_device(): grad_norm = jnp.sqrt(lax.psum(squares, ('dp', 'section')))]
    all_gather x1 -> x0, blocking collectives: 32.6 us -> none  [per_device(): lax.all_gather(m.astype(BF), 'dp', axis=1, tiled=True)[0]]
  transfers between devices with their start and end apart: 9 -> 0, of which waited for: 9 -> 0; matrix products, arithmetic and copies ran while one was open for 5% -> 0% of each run, Pallas kernels for 0% -> 0%
where the time goes in v2:
time: 597 us; the launch traced here: 590 us
  Pallas kernels  517 us (87%)
  matrix products  30 us (5%)
  other arithmetic  21.8 us (4%)
  local copies, waits for them, and re-layouts  17.7 us (3%)
    pallas_call x1, Pallas kernels, run_backward(): pl.pallas_call(functools.partial(backward_kernel, line, length, turned),...  199 us
    pallas_call x1, Pallas kernels, run_scatter(): pl.pallas_call(functools.partial(scatter_kernel, pieces, micro), out_shap...  158 us
    pallas_call x1, Pallas kernels, run_gather(): pl.pallas_call(functools.partial(gather_kernel, pieces, micro), out_shape...  112 us
    pallas_call x1, Pallas kernels, run_forward(): pl.pallas_call(functools.partial(forward_kernel, line, length, turned), o...  48.2 us
    dot_general x4, matrix products, weight_grad(): lax.dot_general(left.reshape(rows, -1), right.reshape(rows, -1), (((0,),...  30 us

profile of v2, /device:TPU:0, one launch (start us, length us, event | category | flops | bytes accessed | tf_op | source)
XLA Modules:
  0.0 589.5 jit_solution(11979777439354533041)
XLA Ops:
  0.7 0.7 pad.33.clone
  1.4 0.1 pad.31.clone
  1.5 0.7 convert_reduce_fusion
  2.2 0.6 pad_convert_fusion.refs_4_
  2.8 1.4 select_add_fusion.refs_7_
  4.1 1.7 convert_bitcast_fusion.3.refs_1_
  5.9 1.9 slice_bitcast_fusion.2.refs_5_
  7.7 0.0 copy-done.3
  7.7 0.8 convert_bitcast_fusion.2.refs_0_
  8.5 0.0 copy-done.1
  8.5 0.9 convert_bitcast_fusion.1.refs_2_
  9.4 0.6 copy-done.2
  10.0 0.9 convert_bitcast_fusion.refs_3_
  10.9 0.7 copy-done.7
  11.6 1.3 pad.24.refs_6_
  12.9 0.7 copy-done
  13.6 1.2 pad.23.x_in
  14.8 112.3 %gather_layers.1 = (bf16[768,2304]{1,0:T(8,128)(2,1)}, bf16[768,768]{1,0:T(8,128)(2,1)}, bf16[768,3072]{1,0:T(8,128)(2,1)}, bf16[3072,768]{1,0:T(8,128)(2,1)}, f...) custom-call(bf16[96,2304]{1,0:T(8,128)(2,1)} %convert_bitcast_fusion.2.refs_0_, ...), custom_call_target="tpu_custom_call" | custom-call | tf_op jit(solution)/shard_map/gather_layers/pallas_call | solution.py:687
  127.2 0.9 copy.71
  128.0 1.3 slice_reduce_fusion.cls
  129.3 0.7 slice_bitcast_fusion.3
  130.0 0.6 broadcast_in_dim.26.segr
  130.7 0.1 reshape.129
  130.7 0.1 reshape.130
  130.8 0.7 maximum_maximum_fusion.small
  131.5 1.0 copy.51.segc
  132.5 48.2 %forward_line.1 = (bf16[4,256,768]{2,1,0:T(8,128)(2,1)}, bf16[4,256,768]{2,1,0:T(8,128)(2,1)}, bf16[4,256,2304]{2,1,0:T(8,128)(2,1)}, f32[4,16,256]{2,1,0:T(8,12...) custom-call(bf16[256,768]{1,0:T(8,128)(2,1)} %get-tuple-element.55.x, ...), custom_call_target="tpu_custom_call" | custom-call | tf_op jit(solution)/shard_map/forward_line/pallas_call | solution.py:530
  180.8 198.5 %backward_line.1 = (bf16[4,256,768]{2,1,0:T(8,128)(2,1)}, bf16[4,256,768]{2,1,0:T(8,128)(2,1)}, bf16[4,256,3072]{2,1,0:T(8,128)(2,1)}, bf16[4,256,768]{2,1,0:T(8...) custom-call(bf16[4,256,768]{2,1,0:T(8,128)(2,1)} %get-tuple-element.62.acts_h, ...), custom_call_target="tpu_custom_call" | custom-call | tf_op jit(solution)/shard_map/backward_line/pallas_call | solution.py:552
  379.3 0.0 copy-start.24
  379.3 9.4 %bitcast_convert_fusion.refs_3_ = bf16[3072,768]{1,0:T(8,128)(2,1)} fusion(bf16[4,256,3072]{2,1,0:T(8,128)(2,1)} %get-tuple-element.76, bf16[4,256,768]{2,1,0:T(8,128)(2,1)} %get-tuple-element.77), kind=kOutput, calls=%fused_computation | convolution fusion | flops 4834197504 | bytes 12582912 | tf_op jit(solution)/shard_map/dot_general | solution.py:909
  388.8 2.5 bitcast_convert_fusion.3.refs_1_
  391.3 0.0 copy-done.18
  391.3 0.1 reshape.132
  391.4 0.1 reshape.133
  391.5 0.6 pad.26.clone
  392.1 8.6 %bitcast_convert_fusion.2.refs_0_ = bf16[768,2304]{1,0:T(8,128)(2,1)} fusion(bf16[4,256,768]{2,1,0:T(8,128)(2,1)} %get-tuple-element.70, bf16[4,256,2304]{2,1,0:T(8,128)(2,1)} %get-tuple-element.71), kind=kOutput, calls=%fused_computation.2 | convolution fusion | flops 3625648128 | bytes 9830400 | tf_op jit(solution)/shard_map/dot_general | solution.py:909
  400.7 9.6 %bitcast_convert_fusion.1.refs_2_ = bf16[768,3072]{1,0:T(8,128)(2,1)} fusion(bf16[4,256,768]{2,1,0:T(8,128)(2,1)S(1)} %copy-done.23, bf16[4,256,3072]{2,1,0:T(8,128)(2,1)} %get-tuple-element.75), kind=kOutput, calls=%fused_computation.1 | convolution fusion | flops 4834197504 | bytes 12582912 | tf_op jit(solution)/shard_map/dot_general | solution.py:909
  410.2 157.8 %scatter_layers.1 = (bf16[96,2304]{1,0:T(8,128)(2,1)}, bf16[96,768]{1,0:T(8,128)(2,1)}, bf16[96,3072]{1,0:T(8,128)(2,1)}, bf16[384,768]{1,0:T(8,128)(2,1)}, f32[...) custom-call(bf16[768,2304]{1,0:T(8,128)(2,1)} %bitcast_convert_fusion.2.refs_0_, ...), custom_call_target="tpu_custom_call" | custom-call | tf_op jit(solution)/shard_map/scatter_layers/pallas_call | solution.py:877
  568.1 1.3 reduce_sum.9
  570.1 0.0 copy-start.19
  570.1 0.0 copy-start.21
  570.1 0.0 copy-start.22
  570.2 0.0 copy-start.8
  570.2 0.0 copy-start.16
  570.2 0.0 copy-start.17
  570.2 3.8 slice_bitcast_fusion
  574.0 0.0 copy-done.19
  574.0 0.0 copy-done.21
  574.0 0.0 copy-done.22
  574.0 0.6 multiply_subtract_fusion.4
  574.6 0.0 copy-done.15
  574.6 0.7 fusion.15
  575.4 1.1 multiply_subtract_fusion.3
  576.5 1.0 fusion.11
  577.5 1.1 fusion.6
  578.5 0.2 copy-done.5
  578.7 1.1 fusion.7
  579.8 0.4 copy-done.13
  580.2 0.4 copy-done.14
  580.6 2.1 multiply_subtract_fusion.2
  582.6 0.2 copy-done.10
  582.9 2.6 multiply_subtract_fusion.1
  585.4 0.0 copy-done.11
  585.4 2.5 multiply_subtract_fusion
  (42 shorter events, 0.1 us)
Async XLA Ops:
  4.1 3.6 copy-start.3
  5.9 2.7 copy-start.1
  8.5 1.5 copy-start.2
  10.0 1.6 copy-start.7
  11.6 2.0 copy-start
  379.3 9.5 %copy-start.24 = (bf16[4,256,768]{2,1,0:T(8,128)(2,1)S(1)}, bf16[4,256,768]{2,1,0:T(8,128)(2,1)}, u32[]{:S(2)}) copy-start(bf16[4,256,768]{2,1,0:T(8,128)(2,1)} %get-tuple-element.72) | copy-start | bytes 4718596
  379.3 9.5 %copy-start.25 = (bf16[4,256,768]{2,1,0:T(8,128)(2,1)S(1)}, bf16[4,256,768]{2,1,0:T(8,128)(2,1)}, u32[]{:S(2)}) copy-start(bf16[4,256,768]{2,1,0:T(8,128)(2,1)} %get-tuple-element.73) | copy-start | bytes 4718596
  388.8 2.5 copy-start.18
  392.1 8.6 %copy-start.23 = (bf16[4,256,768]{2,1,0:T(8,128)(2,1)S(1)}, bf16[4,256,768]{2,1,0:T(8,128)(2,1)}, u32[]{:S(2)}) copy-start(bf16[4,256,768]{2,1,0:T(8,128)(2,1)} %get-tuple-element.74) | copy-start | bytes 4718596
  570.1 3.9 copy-start.20
  570.1 3.9 copy-start.19
  570.1 3.8 copy-start.21
  570.1 3.8 copy-start.22
  570.2 4.5 copy-start.15
  570.2 5.2 copy-start.8
  570.2 5.2 copy-start.16
  570.2 5.2 copy-start.17
  574.6 1.8 copy-start.6
  575.4 2.1 copy-start.4
  577.5 1.3 copy-start.5
  578.7 1.5 copy-start.13
  578.7 1.9 copy-start.14
  580.6 2.1 copy-start.9
  580.6 2.3 copy-start.10
  582.9 2.6 copy-start.11
  582.9 2.6 copy-start.12

commit v3 on v2

--- a/solution.py
+++ b/solution.py
@@ -22,6 +22,7 @@
 adam_eps = 1e-08
 
 NT = (((1,), (1,)), ((), ()))
+TN = (((0,), (0,)), ((), ()))
 
 
 def mm(a, b):
@@ -200,15 +201,21 @@
     def flip(self, x=0, y=0, c=0):
         return Spot(1 - self.x if x else self.x, 1 - self.y if y else self.y, self.z, 1 - self.c if c else self.c)
 
-    def turned(self):
-        return Spot(self.x, self.z // 2, self.section(), self.z % 2)
+    def ahead(self):
+        return Spot(self.x, self.z % 2, self.section(), self.z // 2)
+
+    def back(self):
+        return Spot(self.x, self.z // 2, 2 * self.c + self.y, self.z % 2)
+
+    def crosses(self):
+        return (self.z + self.c) % 2 == 1
 
     def drop(self):
-        return Spot(self.x, (self.y + self.z + self.c) % 2, self.section(), self.z // 2)
+        return Spot(self.x, self.y, 2 * ((self.y + self.z + self.c) % 2) + self.c, self.z // 2)
 
     def source(self):
-        y, c = self.z // 2, self.z % 2
-        return Spot(self.x, y, 2 * self.c + (self.y + y + c) % 2, c)
+        c = self.z % 2
+        return Spot(self.x, self.y, 2 * self.c + (self.y + self.z // 2 + c) % 2, c)
 
     def part(self):
         return self.source().dp()
@@ -237,20 +244,21 @@
     expected = jnp.where(stage > 0, 1, 0) + jnp.where(stage < line.count - 1, 1, 0)
     if turned:
         me = Spot.here()
-        alone = same(me, me.turned())
+        alone = same(me, me.back())
 
         @pl.when(jnp.logical_not(alone))
         def _():
-            hail(me.turned())
-
-        expected = expected + jnp.where(alone, 0, 1)
+            hail(me.back())
+            hail(me.ahead())
+
+        expected = expected + jnp.where(alone, 0, 2)
     pl.semaphore_wait(barrier, expected)
 
 
 def forward_kernel(line, length, turned, x_first, x_in, segr, segc, cls, wqkv_h, wproj_h, wup_h, wdown_h, small,
-                   x_o, a_o, qkv_o, lse_o, o_o, h_o, a2_o, gp_o, u_o, acts_o,
+                   x_o, a_o, qkv_o, lse_o, o_o, h_o, a2_o, gp_o, u_o, acts_o, home_o,
                    wqkv, wproj, wup, wdown, xs, outs, a, qkv, lse, o, h, a2, gp, u, bias, ot,
-                   w_sem, in_sem, x_sem, save_sem, act_sem, send_sem, recv_sem):
+                   w_sem, in_sem, x_sem, save_sem, act_sem, send_sem, recv_sem, home_sem):
     micro = xs.shape[0]
     stage = line.stage()
     loads = [
@@ -266,17 +274,28 @@
     greet(line, turned)
     if turned:
         me = Spot.here()
-        partner = me.turned()
-        alone = same(me, partner)
+        ahead, back = me.ahead(), me.back()
+        alone = same(me, back)
 
         def turn_in(m):
             return pltpu.make_async_remote_copy(
                 src_ref=x_in.at[m], dst_ref=xs.at[m], send_sem=in_sem.at[m], recv_sem=recv_sem.at[m],
-                device_id=partner.id(), device_id_type=MESH)
+                device_id=ahead.id(), device_id_type=MESH)
 
         feeds = jnp.logical_and(me.section() == 0, jnp.logical_not(alone))
         fed = jnp.logical_and(stage == 0, jnp.logical_not(alone))
         feeds_self = jnp.logical_and(stage == 0, alone)
+        homing = jnp.logical_and(stage >= 2, jnp.logical_not(alone))
+        homed = jnp.logical_and(me.section() >= 2, jnp.logical_not(alone))
+        settled = jnp.logical_and(stage >= 2, alone)
+
+        def home(m):
+            return pltpu.make_async_remote_copy(
+                src_ref=outs.at[m], dst_ref=home_o.at[m], send_sem=home_sem.at[0, m], recv_sem=home_sem.at[1, m],
+                device_id=back.id(), device_id_type=MESH)
+
+        def settle(m):
+            return pltpu.make_async_copy(outs.at[m], home_o.at[m], home_sem.at[0, m])
 
         @pl.when(stage == 0)
         def _():
@@ -356,6 +375,9 @@
         for save in saves(m, slot):
             save.start()
         pltpu.make_async_copy(outs.at[m], acts_o.at[m], act_sem.at[m]).start()
+        if turned:
+            pl.when(homing & (m < micro - 1))(lambda: home(m).start())
+            pl.when(settled & (m < micro - 1))(lambda: settle(m).start())
         return carry
 
     lax.fori_loop(0, micro, step, 0)
@@ -378,12 +400,17 @@
             for m in range(1, micro):
                 turn_in(m).wait_send()
 
+        for m in range(micro - 1):
+            pl.when(homing)(lambda: home(m).wait_send())
+            pl.when(homed)(lambda: home(m).wait_recv())
+            pl.when(settled)(lambda: settle(m).wait())
+
 
 def backward_kernel(line, length, turned, acts_h, g_in, x_h, qkv_h, lse_h, h_h, gp_h, segr, segc, cls,
                     wqkv_h, wproj_h, wup_h, wdown_h, small,
-                    acts_o, g_o, dz_o, f_o, r_o, gin_o, sums_o,
+                    acts_o, home_o, g_o, dz_o, f_o, r_o, gin_o, sums_o,
                     wqkv, wproj, wup, wdown, gs, gins, x, qkv, lse, h, gp, dz, f, r, bias, do, dh, dqt,
-                    w_sem, in_sem, g_sem, load_sem, save_sem, act_sem, send_sem, recv_sem, home_sem):
+                    w_sem, in_sem, g_sem, load_sem, save_sem, act_sem, send_sem, recv_sem, home_sem, back_sem):
     micro = gs.shape[0]
     stage = line.stage()
     loads = [
@@ -416,20 +443,32 @@
     greet(line, turned)
     if turned:
         me = Spot.here()
-        partner = me.turned()
-        alone = same(me, partner)
+        back = me.back()
+        alone = same(me, back)
 
         def home(m):
             return pltpu.make_async_remote_copy(
                 src_ref=acts_h.at[m], dst_ref=acts_o.at[m], send_sem=home_sem.at[0, m], recv_sem=home_sem.at[1, m],
-                device_id=partner.id(), device_id_type=MESH)
+                device_id=back.id(), device_id_type=MESH)
 
         def stay(m):
             return pltpu.make_async_copy(acts_h.at[m], acts_o.at[m], home_sem.at[0, m])
 
+        pairs = jnp.logical_not(alone)
+        low, low_home = stage < 2, me.section() < 2
+
+        def home_back(m):
+            return pltpu.make_async_remote_copy(
+                src_ref=gins.at[m], dst_ref=home_o.at[m], send_sem=back_sem.at[0, m], recv_sem=back_sem.at[1, m],
+                device_id=back.id(), device_id_type=MESH)
+
+        def settle_back(m):
+            return pltpu.make_async_copy(gins.at[m], home_o.at[m], back_sem.at[0, m])
+
         for m in range(micro):
-            pl.when(alone)(lambda: stay(m).start())
-            pl.when(jnp.logical_not(alone))(lambda: home(m).start())
+            now = low | (m == micro - 1)
+            pl.when(alone & now)(lambda: stay(m).start())
+            pl.when(pairs & now)(lambda: home(m).start())
     else:
         for m in range(micro):
             pltpu.make_async_copy(acts_h.at[m], acts_o.at[m], home_sem.at[0, m]).start()
@@ -489,6 +528,9 @@
         for save in saves(m, slot):
             save.start()
         pltpu.make_async_copy(gins.at[m], gin_o.at[m], act_sem.at[m]).start()
+        if turned:
+            pl.when(pairs & low & (m < micro - 1))(lambda: home_back(m).start())
+            pl.when(alone & low & (m < micro - 1))(lambda: settle_back(m).start())
         return carry
 
     lax.fori_loop(0, micro, step, 0)
@@ -507,8 +549,14 @@
 
     for m in range(micro):
         if turned:
-            pl.when(alone)(lambda: stay(m).wait())
-            pl.when(jnp.logical_not(alone))(lambda: home(m).wait())
+            now, then = low | (m == micro - 1), low_home | (m == micro - 1)
+            pl.when(alone & now)(lambda: stay(m).wait())
+            pl.when(pairs & now)(lambda: home(m).wait_send())
+            pl.when(pairs & then)(lambda: home(m).wait_recv())
+            if m < micro - 1:
+                pl.when(pairs & low)(lambda: home_back(m).wait_send())
+                pl.when(pairs & low_home)(lambda: home_back(m).wait_recv())
+                pl.when(alone & low)(lambda: settle_back(m).wait())
         else:
             pltpu.make_async_copy(acts_h.at[m], acts_o.at[m], home_sem.at[0, m]).wait()
 
@@ -529,14 +577,15 @@
     many = shape((micro, rows, width), BF)
     return pl.pallas_call(
         functools.partial(forward_kernel, line, length, turned),
-        out_shape=[many] + [shape((micro,) + s, t) for s, t in saved] + [many],
+        out_shape=[many] + [shape((micro,) + s, t) for s, t in saved] + [many, many],
         in_specs=[ANYWHERE, ANYWHERE, IN_VMEM, IN_VMEM, IN_SMEM] + [ANYWHERE] * 4 + [IN_VMEM],
-        out_specs=[ANYWHERE] * 10,
+        out_specs=[ANYWHERE] * 11,
         scratch_shapes=[pltpu.VMEM(w.shape, BF) for w in weights]
         + [pltpu.VMEM((micro, rows, width), BF)] * 2
         + [pltpu.VMEM((2,) + s, t) for s, t in saved]
         + [pltpu.VMEM((rows, rows), F32), pltpu.VMEM((width, rows), BF)]
-        + [DMA((4,)), DMA((micro,)), DMA((micro,)), DMA((2, 8)), DMA((micro,)), DMA((micro,)), DMA((micro,))],
+        + [DMA((4,)), DMA((micro,)), DMA((micro,)), DMA((2, 8)), DMA((micro,)), DMA((micro,)), DMA((micro,)),
+           DMA((2, micro))],
         compiler_params=pltpu.CompilerParams(
             collective_id=0, has_side_effects=True, vmem_limit_bytes=VMEM_CAP),
         name="forward_line",
@@ -551,10 +600,10 @@
     wqkv, wproj, wup, wdown = weights
     return pl.pallas_call(
         functools.partial(backward_kernel, line, length, turned),
-        out_shape=[many, many, shape((micro, rows, hidden), BF), many, shape((micro, rows, 3 * width), BF), many,
+        out_shape=[many, many, many, shape((micro, rows, hidden), BF), many, shape((micro, rows, 3 * width), BF), many,
                    shape((16, width), F32)],
         in_specs=[ANYWHERE] * 7 + [IN_VMEM, IN_VMEM, IN_SMEM] + [ANYWHERE] * 4 + [IN_VMEM],
-        out_specs=[ANYWHERE] * 6 + [IN_VMEM],
+        out_specs=[ANYWHERE] * 7 + [IN_VMEM],
         scratch_shapes=[pltpu.VMEM(w.shape, BF) for w in weights]
         + [pltpu.VMEM((micro, rows, width), BF)] * 2
         + [pltpu.VMEM((2, rows, width), BF), pltpu.VMEM((2, rows, 3 * width), BF), pltpu.VMEM((2, 16, rows), F32),
@@ -563,27 +612,29 @@
            pltpu.VMEM((rows, rows), F32), pltpu.VMEM((rows, width), BF), pltpu.VMEM((rows, width), F32),
            pltpu.VMEM((width, rows), BF)]
         + [DMA((4,)), DMA((micro,)), DMA((micro,)), DMA((2, 5)), DMA((2, 3)), DMA((micro,)), DMA((micro,)),
-           DMA((micro,)), DMA((2, micro))],
+           DMA((micro,)), DMA((2, micro)), DMA((2, micro))],
         compiler_params=pltpu.CompilerParams(
             collective_id=1, has_side_effects=True, vmem_limit_bytes=VMEM_CAP),
         name="backward_line",
     )(acts, g_in, x, qkv, lse, h, gp, segr, segc, cls, wqkv, wproj, wup, wdown, small)
 
 
-GATHER_PIECES = ((0, 0, 96), (4, 0, 16), (1, 0, 96), (2, 0, 48), (2, 48, 48), (3, 0, 192), (3, 192, 192))
-SCATTER_PIECES = ((3, 0, 192), (3, 192, 192), (2, 0, 48), (2, 48, 48), (0, 0, 96), (1, 0, 96), (4, 0, 16))
+GATHER_PIECES = ((0, 0, 48, "c"), (0, 48, 48, "x"), (4, 0, 16, "x"), (1, 0, 96, "c"), (2, 0, 48, "x"), (2, 48, 48, "c"),
+                 (3, 0, 192, "x"), (3, 192, 192, "c"))
 
 
 def gather_kernel(pieces, micro, *refs):
     count = 5
     shares, (x_in, g_in, seg_in) = refs[:count], refs[count : count + 3]
     wholes, (x_o, g_o, seg_o) = refs[count + 3 : 2 * count + 3], refs[2 * count + 3 : 2 * count + 6]
-    send, recv, local, turn_send, turn_recv = refs[2 * count + 6 :]
+    swap, (send, recv, local, turn_send, turn_recv) = refs[2 * count + 6 : 3 * count + 6], refs[3 * count + 6 :]
     me = Spot.here()
     xn, yn, cn = me.flip(x=1), me.flip(y=1), me.flip(c=1)
-    target, source, partner = me.drop(), me.source(), me.turned()
-    stays, alone = same(me, target), same(me, partner)
+    target, source, ahead, back = me.drop(), me.source(), me.ahead(), me.back()
+    stays, alone = same(me, target), same(me, back)
     moves, pairs = jnp.logical_not(stays), jnp.logical_not(alone)
+    crosses = me.crosses()
+    direct = jnp.logical_and(moves, jnp.logical_not(crosses))
     for spot in (xn, yn, cn):
         hail(spot)
 
@@ -594,26 +645,37 @@
 
     @pl.when(pairs)
     def _():
-        hail(partner)
-
-    pl.semaphore_wait(pltpu.get_barrier_semaphore(), 3 + jnp.where(stays, 0, 2) + jnp.where(alone, 0, 1))
+        hail(ahead)
+        hail(back)
+
+    pl.semaphore_wait(pltpu.get_barrier_semaphore(), 3 + jnp.where(stays, 0, 2) + jnp.where(alone, 0, 2))
 
     def rows(k, part):
-        array, first, size = pieces[k]
+        array, first, size, _ = pieces[k]
         share = shares[array].shape[0]
         return wholes[array].at[pl.ds(pl.multiple_of(part * share + first, 16), size)]
 
     def mine(k):
-        array, first, size = pieces[k]
+        array, first, size, _ = pieces[k]
         return shares[array].at[pl.ds(first, size)]
+
+    def swapped(k):
+        array, first, size, _ = pieces[k]
+        return swap[array].at[pl.ds(first, size)]
 
     def remote(src, dst, kind, k, spot):
         return pltpu.make_async_remote_copy(
             src_ref=src, dst_ref=dst, send_sem=send.at[kind, k], recv_sem=recv.at[kind, k],
             device_id=spot.id(), device_id_type=MESH)
 
+    def crossed(k):
+        return remote(mine(k), swapped(k), 8, k, yn)
+
     def brought(k, part):
         return remote(mine(k), rows(k, part), 0, k, target)
+
+    def brought_on(k, part):
+        return remote(swapped(k), rows(k, part), 0, k, target)
 
     def kept(k):
         return pltpu.make_async_copy(mine(k), rows(k, me.dp()), local.at[k])
@@ -633,7 +695,7 @@
     def turn(i):
         return pltpu.make_async_remote_copy(
             src_ref=turns[i][0], dst_ref=turns[i][1], send_sem=turn_send.at[i], recv_sem=turn_recv.at[i],
-            device_id=partner.id(), device_id_type=MESH)
+            device_id=ahead.id(), device_id_type=MESH)
 
     def turn_start(i):
         pl.when(gives[i] & alone)(lambda: pltpu.make_async_copy(*turns[i], turn_send.at[i]).start())
@@ -646,32 +708,45 @@
 
     for k in range(len(pieces)):
         pl.when(stays)(lambda: kept(k).start())
-        pl.when(moves)(lambda: brought(k, me.dp()).start())
+        pl.when(direct)(lambda: brought(k, me.dp()).start())
+        pl.when(crosses)(lambda: crossed(k).start())
     turn_start(1)
     turn_start(0)
-    for i in range(2, 2 + micro):
-        turn_start(i)
-    for k in range(len(pieces) + 2):
+    for k in range(len(pieces) + 3):
         if k < len(pieces):
-            pl.when(stays)(lambda: kept(k).wait())
-            pl.when(moves)(lambda: brought(k, own).wait_recv())
-            passed(1, k, own, xn).start()
-            passed(2, k, own, yn).start()
-            passed(4, k, own, cn).start()
-        if 0 <= k - 1 < len(pieces):
-            passed(1, k - 1, own_x, xn).wait_recv()
-            passed(5, k - 1, own_x, cn).start()
-            pl.when(me.c == 0)(lambda: passed(3, k - 1, own_x, yn).start())
-            passed(2, k - 1, own_y, yn).wait_recv()
-            passed(6, k - 1, own_y, cn).start()
-            pl.when(me.c == 1)(lambda: passed(3, k - 1, own_y, xn).start())
-        if 0 <= k - 2 < len(pieces):
-            passed(3, k - 2, own_d, yn).wait_recv()
-            passed(7, k - 2, own_d, cn).start()
+            @pl.when(crosses)
+            def _():
+                crossed(k).wait_recv()
+                brought_on(k, me.dp()).start()
+
+        if k == len(pieces) - 1:
+            for i in range(2, 2 + micro):
+                turn_start(i)
+        b = k - 1
+        if 0 <= b < len(pieces):
+            pl.when(stays)(lambda: kept(b).wait())
+            pl.when(moves)(lambda: brought(b, own).wait_recv())
+            passed(1, b, own, xn).start()
+            passed(2, b, own, yn).start()
+            passed(4, b, own, cn).start()
+        b = k - 2
+        if 0 <= b < len(pieces):
+            turn_x = (me.c == 0) if pieces[b][3] == "c" else (me.c < 0)
+            passed(1, b, own_x, xn).wait_recv()
+            pl.when(turn_x)(lambda: passed(3, b, own_x, yn).start())
+            passed(5, b, own_x, cn).start()
+            passed(2, b, own_y, yn).wait_recv()
+            pl.when(jnp.logical_not(turn_x))(lambda: passed(3, b, own_y, xn).start())
+            passed(6, b, own_y, cn).start()
+        b = k - 3
+        if 0 <= b < len(pieces):
+            passed(3, b, own_d, yn).wait_recv()
+            passed(7, b, own_d, cn).start()
     for k in range(len(pieces)):
         for kind in range(4, 8):
             passed(kind, k, beside[kind - 4], cn).wait_recv()
         pl.when(moves)(lambda: brought(k, own).wait_send())
+        pl.when(crosses)(lambda: crossed(k).wait_send())
         for kind in range(1, 8):
             passed(kind, k, own, cn).wait_send()
     for i in range(len(turns)):
@@ -689,28 +764,62 @@
         out_shape=outs,
         in_specs=[ANYWHERE] * 8,
         out_specs=[ANYWHERE] * 8,
-        scratch_shapes=[DMA((8, len(pieces))), DMA((8, len(pieces))), DMA((len(pieces),)), DMA((2 + micro,)),
-                        DMA((2 + micro,))],
-        compiler_params=pltpu.CompilerParams(collective_id=2, has_side_effects=True),
+        scratch_shapes=[pltpu.VMEM(s.shape, s.dtype) for s in shares]
+        + [DMA((9, len(pieces))), DMA((9, len(pieces))), DMA((len(pieces),)), DMA((2 + micro,)), DMA((2 + micro,))],
+        compiler_params=pltpu.CompilerParams(collective_id=2, has_side_effects=True, vmem_limit_bytes=VMEM_CAP),
         name="gather_layers",
     )(*shares, x_first, g, segs)
 
 
+SCATTER_PIECES = ((3, 0, 128, 0, 768, "x"), (3, 128, 128, 0, 768, "x"), (3, 256, 128, 0, 768, "x"),
+                  (2, 0, 96, 0, 1024, "x"), (2, 0, 96, 1024, 1024, "x"), (2, 0, 96, 2048, 1024, "x"),
+                  (0, 0, 96, 0, 768, "x"), (0, 0, 96, 768, 768, "x"), (0, 0, 96, 1536, 768, "x"),
+                  (1, 0, 96, 0, 768, "x"), (4, 0, 16, 0, 128, "x"))
+
+
 def scatter_kernel(pieces, micro, *refs):
     count = 5
-    totals, gin_in = refs[:count], refs[count]
-    outs, gin_o, norm_o = refs[count + 1 : 2 * count + 1], refs[2 * count + 1], refs[2 * count + 2]
-    at = 2 * count + 3
-    held, beside, diag, from_x, from_y, done, home = (refs[at + i * count : at + (i + 1) * count] for i in range(7))
-    sums, tallies, load, send, recv, local, turn_sem, note_send, note_recv, out_sem = refs[at + 7 * count :]
+    a_h, r_h, o_h, f_h, a2_h, dz_h, u_h, g_h, small_h, gin_in = refs[:10]
+    outs, gin_o, norm_o = refs[10:15], refs[15], refs[16]
+    at = 17
+    totals, beside, diag, from_x, from_y, done, swap, home = (refs[at + i * count : at + (i + 1) * count] for i in range(8))
+    (stream, fixed, flipped, sums, tallies, stream_sem, fixed_sem, send, recv, local, turn_sem, note_send, note_recv,
+     out_sem) = refs[at + 8 * count :]
     me = Spot.here()
     xn, yn, cn = me.flip(x=1), me.flip(y=1), me.flip(c=1)
-    target, partner = me.source(), me.turned()
-    giver = me.drop()
-    stays, alone = same(me, target), same(me, partner)
+    target, giver, back, ahead = me.source(), me.drop(), me.back(), me.ahead()
+    stays, alone = same(me, target), same(me, back)
     moves, pairs = jnp.logical_not(stays), jnp.logical_not(alone)
+    crosses, target_crosses = me.crosses(), target.crosses()
     slab = [me.flip(x=i & 1, y=(i >> 1) & 1, c=i >> 2) for i in range(1, 8)]
     column = [Spot(me.x, me.y, (me.z + i) % 4, me.c) for i in range(1, 4)]
+    left_right = {0: (a_h, r_h), 1: (o_h, f_h), 2: (a2_h, dz_h), 3: (u_h, g_h)}
+    resting = (g_h, a2_h, a_h, o_h)
+    rest_at = {3: 0, 2: 1, 0: 2, 1: 3}
+
+    def streamed(k):
+        array, first, size, column_at, columns, _ = pieces[k]
+        slot = k % 2
+        if array == 3:
+            share = totals[3].shape[0] // 8
+            return [pltpu.make_async_copy(u_h.at[:, pl.ds(p * share + first, size)],
+                                          stream.at[slot, :, pl.ds(p * size, size)], stream_sem.at[slot, p])
+                    for p in range(8)]
+        if array == 4:
+            return [pltpu.make_async_copy(small_h, totals[4], stream_sem.at[slot, 0])]
+        return [pltpu.make_async_copy(left_right[array][1].at[:, pl.ds(column_at, columns)],
+                                      stream.at[slot, :, pl.ds(0, columns)], stream_sem.at[slot, 0])]
+
+    def rested(i):
+        return pltpu.make_async_copy(resting[i], fixed.at[i], fixed_sem.at[i])
+
+    for copy in streamed(0):
+        copy.start()
+    rested(0).start()
+    for copy in streamed(1):
+        copy.start()
+    for i in range(1, 4):
+        rested(i).start()
     for spot in slab + column:
         hail(spot)
 
@@ -721,113 +830,156 @@
 
     @pl.when(pairs)
     def _():
-        hail(partner)
-
-    pl.semaphore_wait(pltpu.get_barrier_semaphore(), 10 + jnp.where(stays, 0, 2) + jnp.where(alone, 0, 1))
+        hail(back)
+        hail(ahead)
+
+    def work(k):
+        array, first, size, column_at, columns, _ = pieces[k]
+        slot = k % 2
+        for copy in streamed(k):
+            copy.wait()
+        if array == 4:
+            return
+        if array == 3:
+            if first == 0:
+                rested(rest_at[3]).wait()
+            share = totals[3].shape[0] // 8
+            for p in range(0, 8, 2):
+                both = lax.dot_general(stream[slot, :, p * size : (p + 2) * size], fixed[rest_at[3]], TN,
+                                       preferred_element_type=F32).astype(BF)
+                for i in range(2):
+                    totals[3][(p + i) * share + first : (p + i) * share + first + size, :] = both[i * size : (i + 1) * size]
+        else:
+            if column_at == 0:
+                rested(rest_at[array]).wait()
+                flipped[...] = fixed[rest_at[array]].T
+            for c in range(0, columns, 256):
+                totals[array][:, column_at + c : column_at + c + 256] = mm(flipped[...], stream[slot, :, c : c + 256]).astype(BF)
+        if k + 2 < len(pieces):
+            for copy in streamed(k + 2):
+                copy.start()
 
     def parts(spot):
         return [s.part() for s in (spot, spot.flip(x=1), spot.flip(y=1), spot.flip(x=1, y=1))]
 
     kept, given = parts(me), parts(cn)
 
+    def box(k):
+        _, first, size, column_at, columns, _ = pieces[k]
+        return pl.ds(first, size), pl.ds(column_at, columns)
+
     def whole(k, part):
-        array, first, size = pieces[k]
+        array, first, size, column_at, columns, _ = pieces[k]
         share = done[array].shape[0]
-        return totals[array].at[pl.ds(pl.multiple_of(part * share + first, 16), size)]
-
-    def span(k):
-        return pl.ds(pieces[k][1], pieces[k][2])
+        return totals[array].at[pl.ds(pl.multiple_of(part * share + first, 16), size), pl.ds(column_at, columns)]
 
     def remote(src, dst, kind, k, spot):
         return pltpu.make_async_remote_copy(
             src_ref=src, dst_ref=dst, send_sem=send.at[kind, k], recv_sem=recv.at[kind, k],
             device_id=spot.id(), device_id_type=MESH)
 
-    def loaded(k, j):
-        return pltpu.make_async_copy(whole(k, kept[j]), held[pieces[k][0]].at[j, span(k)], load.at[j, k])
+    def of(refs_, k):
+        return refs_[pieces[k][0]].at[box(k)]
 
     def crossed(k, j):
-        return remote(whole(k, given[j]), beside[pieces[k][0]].at[j, span(k)], j, k, cn)
+        return remote(whole(k, given[j]), beside[pieces[k][0]].at[(j,) + box(k)], j, k, cn)
 
     def to_diag(k, spot):
-        return remote(held[pieces[k][0]].at[3, span(k)], diag[pieces[k][0]].at[span(k)], 4, k, spot)
+        return remote(whole(k, kept[3]), of(diag, k), 4, k, spot)
 
     def to_x(k):
-        return remote(held[pieces[k][0]].at[1, span(k)], from_x[pieces[k][0]].at[span(k)], 5, k, xn)
+        return remote(whole(k, kept[1]), of(from_x, k), 5, k, xn)
 
     def to_y(k):
-        return remote(held[pieces[k][0]].at[2, span(k)], from_y[pieces[k][0]].at[span(k)], 6, k, yn)
+        return remote(whole(k, kept[2]), of(from_y, k), 6, k, yn)
 
     def to_home(k):
-        return remote(done[pieces[k][0]].at[span(k)], home[pieces[k][0]].at[span(k)], 7, k, target)
+        return remote(of(done, k), of(home, k), 7, k, target)
+
+    def to_swap(k):
+        return remote(of(done, k), of(swap, k), 7, k, target)
 
     def stay_home(k):
-        return pltpu.make_async_copy(done[pieces[k][0]].at[span(k)], home[pieces[k][0]].at[span(k)], local.at[k])
+        return pltpu.make_async_copy(of(done, k), of(home, k), local.at[k])
+
+    def over(k):
+        return remote(of(swap, k), of(home, k), 8, k, yn)
 
     def add(k, j, extra):
-        array = held[pieces[k][0]]
-        array[j, span(k)] = (array[j, span(k)].astype(F32) + extra.astype(F32)).astype(array.dtype)
+        here = whole(k, kept[j])
+        here[...] = (here[...].astype(F32) + extra.astype(F32)).astype(here.dtype)
 
     def turn(m):
         return pltpu.make_async_remote_copy(
             src_ref=gin_in.at[m], dst_ref=gin_o.at[m], send_sem=turn_sem.at[0, m], recv_sem=turn_sem.at[1, m],
-            device_id=partner.id(), device_id_type=MESH)
+            device_id=back.id(), device_id_type=MESH)
 
     def turn_stay(m):
         return pltpu.make_async_copy(gin_in.at[m], gin_o.at[m], turn_sem.at[0, m])
 
-    for k in range(len(pieces)):
-        for j in (3, 2, 1, 0):
-            crossed(k, j).start()
-            loaded(k, j).start()
+    work(0)
+    pl.semaphore_wait(pltpu.get_barrier_semaphore(), 10 + jnp.where(stays, 0, 2) + jnp.where(alone, 0, 2))
     for m in range(micro):
-        pl.when(alone)(lambda: turn_stay(m).start())
-        pl.when(pairs)(lambda: turn(m).start())
-    for k in range(len(pieces) + 2):
+        now = (me.z >= 2) | (m == micro - 1)
+        pl.when(alone & now)(lambda: turn_stay(m).start())
+        pl.when(pairs & now)(lambda: turn(m).start())
+    for k in range(len(pieces) + 4):
         if k < len(pieces):
-            array = pieces[k][0]
+            if k > 0:
+                work(k)
             for j in (3, 2, 1, 0):
-                loaded(k, j).wait()
-                crossed(k, j).wait_recv()
-                add(k, j, beside[array][j, span(k)])
+                crossed(k, j).start()
+        b = k - 1
+        if 0 <= b < len(pieces):
+            turn_x = (me.c == 0) if pieces[b][5] == "c" else (me.c < 0)
+            for j in (3, 2, 1, 0):
+                crossed(b, j).wait_recv()
+                add(b, j, beside[pieces[b][0]][(j,) + box(b)])
                 if j == 3:
-                    pl.when(me.c == 0)(lambda: to_diag(k, yn).start())
-                    pl.when(me.c == 1)(lambda: to_diag(k, xn).start())
+                    pl.when(turn_x)(lambda: to_diag(b, yn).start())
+                    pl.when(jnp.logical_not(turn_x))(lambda: to_diag(b, xn).start())
                 if j == 2:
-                    pl.when(me.c == 0)(lambda: to_y(k).start())
+                    pl.when(turn_x)(lambda: to_y(b).start())
                 if j == 1:
-                    pl.when(me.c == 1)(lambda: to_x(k).start())
-        if 0 <= k - 1 < len(pieces):
-            b = k - 1
+                    pl.when(jnp.logical_not(turn_x))(lambda: to_x(b).start())
+        b = k - 2
+        if 0 <= b < len(pieces):
             to_diag(b, yn).wait_recv()
-
-            @pl.when(me.c == 0)
+            turn_x = (me.c == 0) if pieces[b][5] == "c" else (me.c < 0)
+
+            @pl.when(turn_x)
             def _():
-                add(b, 1, diag[pieces[b][0]][span(b)])
+                add(b, 1, of(diag, b)[...])
                 to_x(b).start()
 
-            @pl.when(me.c == 1)
+            @pl.when(jnp.logical_not(turn_x))
             def _():
-                add(b, 2, diag[pieces[b][0]][span(b)])
+                add(b, 2, of(diag, b)[...])
                 to_y(b).start()
-        if 0 <= k - 2 < len(pieces):
-            b = k - 2
-            array = pieces[b][0]
+        b = k - 3
+        if 0 <= b < len(pieces):
             to_x(b).wait_recv()
             to_y(b).wait_recv()
-            total = (held[array][0, span(b)].astype(F32) + from_x[array][span(b)].astype(F32)
-                     + from_y[array][span(b)].astype(F32))
-            done[array][span(b)] = total.astype(done[array].dtype)
+            total = (whole(b, kept[0])[...].astype(F32) + of(from_x, b)[...].astype(F32) + of(from_y, b)[...].astype(F32))
+            done[pieces[b][0]][box(b)] = total.astype(done[pieces[b][0]].dtype)
             pl.when(stays)(lambda: stay_home(b).start())
-            pl.when(moves)(lambda: to_home(b).start())
+            pl.when(moves & jnp.logical_not(target_crosses))(lambda: to_home(b).start())
+            pl.when(target_crosses)(lambda: to_swap(b).start())
+        b = k - 4
+        if 0 <= b < len(pieces):
+            @pl.when(crosses)
+            def _():
+                to_swap(b).wait_recv()
+                over(b).start()
     tally = jnp.zeros((8, 128), F32)
     for k in range(len(pieces)):
         pl.when(stays)(lambda: stay_home(k).wait())
-        pl.when(moves)(lambda: to_home(k).wait_recv())
-        array = pieces[k][0]
-        value = home[array][span(k)].astype(F32)
+        pl.when(moves & jnp.logical_not(crosses))(lambda: to_home(k).wait_recv())
+        pl.when(crosses)(lambda: over(k).wait_recv())
+        value = of(home, k)[...].astype(F32)
         value = value * value
-        tally = tally + jnp.sum(value.reshape(-1, 8, value.shape[1] // 128, 128), axis=(0, 2))
+        for c in range(0, value.shape[1], 128):
+            tally = tally + jnp.sum(value[:, c : c + 128].reshape(-1, 8, 128), axis=0)
     sums[0] = tally
 
     def note(i, src, slot, spot):
@@ -860,31 +1012,39 @@
         to_x(k).wait_send()
         to_y(k).wait_send()
         pl.when(moves)(lambda: to_home(k).wait_send())
+        pl.when(crosses)(lambda: over(k).wait_send())
     for m in range(micro):
-        pl.when(alone)(lambda: turn_stay(m).wait())
-        pl.when(pairs)(lambda: turn(m).wait())
+        now, then = (me.z >= 2) | (m == micro - 1), (me.section() >= 2) | (m == micro - 1)
+        pl.when(alone & now)(lambda: turn_stay(m).wait())
+        pl.when(pairs & now)(lambda: turn(m).wait_send())
+        pl.when(pairs & then)(lambda: turn(m).wait_recv())
     for array in range(count):
         pltpu.make_async_copy(home[array], outs[array], out_sem.at[array]).wait()
 
 
-def run_scatter(totals, gin):
+def run_scatter(operands, small, gin):
     pieces = SCATTER_PIECES
     micro = gin.shape[0]
     shape = jax.ShapeDtypeStruct
-    shares = [((t.shape[0] // 8, t.shape[1]), t.dtype) for t in totals]
-    four = [pltpu.VMEM((4,) + s, t) for s, t in shares]
+    a, r, o, f, a2, dz, u, g = operands = [v.reshape(-1, v.shape[-1]) for v in operands]
+    rows = a.shape[0]
+    sizes = [((left.shape[1], right.shape[1]), BF) for left, right in ((a, r), (o, f), (a2, dz), (u, g))]
+    sizes.append((small.shape, F32))
+    shares = [((s[0] // 8, s[1]), t) for s, t in sizes]
     one = [pltpu.VMEM(s, t) for s, t in shares]
     return pl.pallas_call(
         functools.partial(scatter_kernel, pieces, micro),
         out_shape=[shape(s, t) for s, t in shares] + [shape(gin.shape, gin.dtype), shape((8, 128), F32)],
-        in_specs=[ANYWHERE] * 6,
+        in_specs=[ANYWHERE] * 10,
         out_specs=[ANYWHERE] * 6 + [IN_VMEM],
-        scratch_shapes=four + four + one * 5
-        + [pltpu.VMEM((2, 8, 128), F32), pltpu.VMEM((10, 8, 128), F32), DMA((4, len(pieces))), DMA((8, len(pieces))),
-           DMA((8, len(pieces))), DMA((len(pieces),)), DMA((2, micro)), DMA((10,)), DMA((10,)), DMA((5,))],
+        scratch_shapes=[pltpu.VMEM(s, t) for s, t in sizes] + [pltpu.VMEM((4,) + s, t) for s, t in shares] + one * 6
+        + [pltpu.VMEM((2, rows, 1024), BF), pltpu.VMEM((4, rows, a.shape[1]), BF), pltpu.VMEM((a.shape[1], rows), BF),
+           pltpu.VMEM((2, 8, 128), F32), pltpu.VMEM((10, 8, 128), F32), DMA((2, 8)), DMA((4,)),
+           DMA((9, len(pieces))), DMA((9, len(pieces))), DMA((len(pieces),)), DMA((2, micro)), DMA((10,)), DMA((10,)),
+           DMA((5,))],
         compiler_params=pltpu.CompilerParams(collective_id=3, has_side_effects=True, vmem_limit_bytes=VMEM_CAP),
         name="scatter_layers",
-    )(*totals, gin)
+    )(*operands, small, gin)
 
 
 def split_small(small, width, slices):
@@ -940,19 +1100,24 @@
     small = split_small(flat, width, slices)
     segr, segc = segs[:, None, :], segs[:, :, None]
 
-    x, a, qkv, lse, o, h, a2, gp, u, acts = run_forward(
+    x, a, qkv, lse, o, h, a2, gp, u, acts, acts_early = run_forward(
         line, length, turned, x_first, x_in, segr, segc, classes, weights, small)
-    acts, g, dz, f, r, gin, sums = run_backward(
+    acts, gin_early, g, dz, f, r, gin, sums = run_backward(
         line, length, turned, acts, g_in, x, qkv, lse, h, gp, segr, segc, classes, weights, small)
-    totals = [weight_grad(a, r).astype(BF), weight_grad(o, f).astype(BF), weight_grad(a2, dz).astype(BF),
-              weight_grad(u, g).astype(BF), join_small(sums, total, slices)]
+    small_total = join_small(sums, total, slices)
     if turned:
-        table = jnp.pad(totals[4].reshape(slices, lanes, 128), ((0, 0), (0, 16 - lanes), (0, 0)))
-        *shards, gin, tally = run_scatter(totals[:4] + [table.reshape(slices * 16, 128)], gin)
+        table = jnp.pad(small_total.reshape(slices, lanes, 128), ((0, 0), (0, 16 - lanes), (0, 0)))
+        *shards, gin, tally = run_scatter([a, r, o, f, a2, dz, u, g], table.reshape(slices * 16, 128), gin)
         shards[4] = shards[4][:lanes].reshape(-1)
         shards = [s.astype(F32)[None] for s in shards]
         grad_norm = jnp.sqrt(jnp.sum(tally))
+        upper = lax.axis_index("section") >= 2
+        early = lax.broadcasted_iota(jnp.int32, (seq_dev, 1, 1), 0) < seq_dev - 1
+        acts = jnp.where(early & upper, acts_early, acts)
+        gin = jnp.where(early & jnp.logical_not(upper), gin_early, gin)
     else:
+        totals = [weight_grad(a, r).astype(BF), weight_grad(o, f).astype(BF), weight_grad(a2, dz).astype(BF),
+                  weight_grad(u, g).astype(BF), small_total]
         shards = [lax.psum_scatter(t[None], "dp", scatter_dimension=1, tiled=True).astype(F32) for t in totals]
         squares = jnp.sum(jnp.stack([jnp.sum(s * s) for s in shards]))
         grad_norm = jnp.sqrt(lax.psum(squares, ("dp", "section")))

time: 597 us -> 496 us (0.83)
  Pallas kernels: 517 us -> 446 us
  matrix products: 30 us -> 0 us
    pallas_call x1, Pallas kernels: 158 us -> 121 us  [run_scatter(): pl.pallas_call(functools.partial(scatter_kernel, pieces, micro), out_shap...]
    dot_general x4 -> x0, matrix products: 30 us -> none  [weight_grad(): lax.dot_general(left.reshape(rows, -1), right.reshape(rows, -1), (((0,),...]
    pallas_call x1, Pallas kernels: 199 us -> 177 us  [run_backward(): pl.pallas_call(functools.partial(backward_kernel, line, length, turned),...]
    pallas_call x1, Pallas kernels: 112 us -> 100 us  [run_gather(): pl.pallas_call(functools.partial(gather_kernel, pieces, micro), out_shape...]
where the time goes in v3:
time: 496 us; the launch traced here: 489 us
  Pallas kernels  446 us (90%)
  other arithmetic  25.5 us (5%)
  local copies, waits for them, and re-layouts  14 us (3%)
    pallas_call x1, Pallas kernels, run_backward(): pl.pallas_call(functools.partial(backward_kernel, line, length, turned),...  177 us
    pallas_call x1, Pallas kernels, run_scatter(): pl.pallas_call(functools.partial(scatter_kernel, pieces, micro), out_shap...  121 us
    pallas_call x1, Pallas kernels, run_gather(): pl.pallas_call(functools.partial(gather_kernel, pieces, micro), out_shape...  100 us
    pallas_call x1, Pallas kernels, run_forward(): pl.pallas_call(functools.partial(forward_kernel, line, length, turned), o...  47.8 us
    sub x5, other arithmetic, per_device(): results += [grad, masters[kind] - rate * update, first, second]  10.5 us

profile of v3, /device:TPU:0, one launch (start us, length us, event | category | flops | bytes accessed | tf_op | source)
XLA Modules:
  0.0 488.7 jit_solution(14721335125087532344)
XLA Ops:
  0.7 0.0 copy-start.1
  0.7 2.8 pad.24.refs_6_
  3.5 0.0 copy-done.1
  3.5 0.9 convert_bitcast_fusion.refs_3_
  4.4 0.6 copy-done.2
  5.0 0.9 convert_bitcast_fusion.1.refs_2_
  5.9 0.0 copy-done.4
  5.9 0.8 convert_bitcast_fusion.2.refs_0_
  6.7 0.0 copy-done
  6.7 0.0 copy-start.23
  6.7 0.8 slice_bitcast_fusion.refs_5_
  7.5 0.2 copy-done.11
  7.7 0.7 convert_bitcast_fusion.3.refs_1_
  8.4 0.0 copy-done.20
  8.4 0.6 pad_convert_fusion.refs_4_
  9.0 0.0 copy-done.24
  9.0 0.1 pad.33.clone
  9.1 0.0 copy-done.23
  9.1 0.7 select_add_fusion.refs_7_
  9.8 100.2 %gather_layers.1 = (bf16[768,2304]{1,0:T(8,128)(2,1)}, bf16[768,768]{1,0:T(8,128)(2,1)}, bf16[768,3072]{1,0:T(8,128)(2,1)}, bf16[3072,768]{1,0:T(8,128)(2,1)}, f...) custom-call(bf16[96,2304]{1,0:T(8,128)(2,1)} %convert_bitcast_fusion.2.refs_0_, ...), custom_call_target="tpu_custom_call" | custom-call | tf_op jit(solution)/shard_map/gather_layers/pallas_call | solution.py:762
  110.0 0.9 copy.59
  110.9 0.1 reshape.155
  111.0 0.1 reshape.156
  111.1 0.1 pad.31.clone
  111.2 0.7 maximum_maximum_fusion.small
  111.9 0.7 slice_bitcast_fusion.1
  112.5 1.0 copy.47.segc
  113.6 0.6 broadcast_in_dim.40.segr
  114.2 1.3 slice_reduce_fusion.cls
  115.5 1.3 pad.23.x_in
  116.8 47.8 %forward_line.1 = (bf16[4,256,768]{2,1,0:T(8,128)(2,1)}, bf16[4,256,768]{2,1,0:T(8,128)(2,1)}, bf16[4,256,2304]{2,1,0:T(8,128)(2,1)}, f32[4,16,256]{2,1,0:T(8,12...) custom-call(bf16[256,768]{1,0:T(8,128)(2,1)} %get-tuple-element.57.x, ...), custom_call_target="tpu_custom_call" | custom-call | tf_op jit(solution)/shard_map/forward_line/pallas_call | solution.py:578
  164.5 176.8 %backward_line.1 = (bf16[4,256,768]{2,1,0:T(8,128)(2,1)}, bf16[4,256,768]{2,1,0:T(8,128)(2,1)}, bf16[4,256,768]{2,1,0:T(8,128)(2,1)}, bf16[4,256,3072]{2,1,0:T(8...) custom-call(bf16[4,256,768]{2,1,0:T(8,128)(2,1)} %get-tuple-element., ...), custom_call_target="tpu_custom_call" | custom-call | tf_op jit(solution)/shard_map/backward_line/pallas_call | solution.py:601
  341.3 0.7 slice.40
  342.1 0.1 reshape.166
  342.2 0.1 reshape.167
  342.3 0.7 slice.41
  343.0 0.6 pad.26.clone
  343.7 121.2 %scatter_layers.1 = (bf16[96,2304]{1,0:T(8,128)(2,1)}, bf16[96,768]{1,0:T(8,128)(2,1)}, bf16[96,3072]{1,0:T(8,128)(2,1)}, bf16[384,768]{1,0:T(8,128)(2,1)}, f32[...) custom-call(bf16[1024,768]{1,0:T(8,128)(2,1)} %bitcast.97, bf16[1024,2304]{1,0:T(8,128)(2,1)} %bitcast.96, ...), custom_call_target="tpu_custom_call" | custom-call | tf_op jit(solution)/shard_map/scatter_layers/pallas_call | solution.py:1035
  464.9 1.3 reduce_sum.9
  466.9 0.7 multiply_bitcast_fusion.4
  467.6 0.0 copy-done.21
  467.6 0.0 copy-done.22
  467.6 0.6 multiply_subtract_fusion.4
  468.2 0.0 copy-done.12
  468.3 4.1 multiply_subtract_fusion
  472.4 0.0 copy-done.7
  472.4 1.1 fusion.8
  473.5 0.0 copy-done.13
  473.5 0.0 copy-done.14
  473.5 0.6 copy-done.3
  474.1 0.1 copy-done.6
  474.2 2.6 multiply_subtract_fusion.1
  476.8 1.1 fusion.9
  477.9 0.0 copy-done.17
  477.9 0.0 copy-done.18
  477.9 0.2 copy-done.19
  478.2 1.1 multiply_subtract_fusion.3
  479.3 0.7 fusion.17
  480.0 0.0 copy-done.16
  480.0 0.1 copy-done.15
  480.1 2.1 multiply_subtract_fusion.2
  482.2 1.0 fusion.13
  483.2 0.0 copy-done.10
  483.2 3.9 fusion
  (38 shorter events, 0.2 us)
Async XLA Ops:
  0.7 2.8 copy-start.1
  3.5 1.5 copy-start.2
  3.5 2.4 copy-start.4
  5.0 1.7 copy-start
  6.7 1.0 copy-start.11
  6.7 1.7 copy-start.20
  6.7 2.3 copy-start.24
  6.7 2.4 copy-start.23
  343.7 123.9 %copy-start.21 = (f32[1,1152]{1,0:T(1,128)S(1)}, f32[1,1152]{1,0:T(1,128)}, u32[]{:S(2)}) copy-start(f32[1,1152]{1,0:T(1,128)} %param.32) | copy-start | bytes 13828
  343.7 123.9 %copy-start.22 = (f32[1,1152]{1,0:T(1,128)S(1)}, f32[1,1152]{1,0:T(1,128)}, u32[]{:S(2)}) copy-start(f32[1,1152]{1,0:T(1,128)} %param.37) | copy-start | bytes 13828
  343.7 124.6 %copy-start.12 = (f32[1,384,768]{2,1,0:T(8,128)S(1)}, f32[1,384,768]{2,1,0:T(8,128)}, u32[]{:S(2)}) copy-start(f32[1,384,768]{2,1,0:T(8,128)} %param.31) | copy-start | bytes 3538948
  468.2 4.1 copy-start.7
  468.3 5.2 %copy-start.13 = (f32[1,96,3072]{2,1,0:T(8,128)S(1)}, f32[1,96,3072]{2,1,0:T(8,128)}, u32[]{:S(2)}) copy-start(f32[1,96,3072]{2,1,0:T(8,128)} %param.30) | copy-start | bytes 3538948
  468.3 5.2 %copy-start.14 = (f32[1,96,3072]{2,1,0:T(8,128)S(1)}, f32[1,96,3072]{2,1,0:T(8,128)}, u32[]{:S(2)}) copy-start(f32[1,96,3072]{2,1,0:T(8,128)} %param.35) | copy-start | bytes 3538948
  472.4 1.7 copy-start.3
  472.4 1.8 copy-start.6
  476.8 1.1 copy-start.17
  476.8 1.1 copy-start.18
  476.8 1.4 copy-start.19
  476.8 3.2 copy-start.16
  478.2 1.8 copy-start.5
  478.2 1.8 copy-start.8
  478.2 1.9 copy-start.15
  480.1 3.1 copy-start.9
  480.1 3.1 copy-start.10

commit v4 on v3

--- a/solution.py
+++ b/solution.py
@@ -49,13 +49,43 @@
     return jnp.sum(values, axis=0, keepdims=True)
 
 
-def mask_bias(seg_row, seg_col, cls, length):
+def mask_bias(seg_row, seg_col, cls_row, length):
     size = seg_col.shape[0]
     key_at = lax.broadcasted_iota(jnp.int32, (size, size), 0)
     query_at = lax.broadcasted_iota(jnp.int32, (size, size), 1)
-    allowed = (seg_row == seg_col) | (key_at == cls) | (query_at == cls)
+    allowed = (seg_row == seg_col) | (key_at == cls_row) | (query_at == cls_row)
     allowed = allowed & (key_at < length)
     return jnp.where(allowed, 0.0, masked_score).astype(F32)
+
+
+def micro_bias(words, m, micro, length):
+    seg_row, cls_row = words[pl.ds(m, 1), :], words[pl.ds(micro + m, 1), :]
+    size = seg_row.shape[1]
+    on_diagonal = lax.broadcasted_iota(jnp.int32, (size, size), 0) == lax.broadcasted_iota(jnp.int32, (size, size), 1)
+    seg_col = jnp.sum(jnp.where(on_diagonal, seg_row.astype(F32), 0.0), axis=1, keepdims=True)
+    return mask_bias(seg_row.astype(F32), seg_col, cls_row, length)
+
+
+def spread_small(table, small):
+    width = small.shape[1]
+    share, ups = width // 8, width // 256
+    small[...] = jnp.zeros_like(small)
+    for i in range(8):
+        small[0:8, i * share : (i + 1) * share] = table[16 * i : 16 * i + 8, 0:share]
+        for j in range(ups):
+            at = i % 2 * (width // 2) + j * 128
+            small[8 + i // 2 : 9 + i // 2, at : at + 128] = table[16 * i + 8 + j : 16 * i + 9 + j, :]
+
+
+def share_small(sums, table):
+    width = sums.shape[1]
+    share, ups = width // 8, width // 256
+    table[...] = jnp.zeros_like(table)
+    for i in range(8):
+        table[16 * i : 16 * i + 8, 0:share] = sums[0:8, i * share : (i + 1) * share]
+        for j in range(ups):
+            at = i % 2 * (width // 2) + j * 128
+            table[16 * i + 8 + j : 16 * i + 9 + j, :] = sums[8 + i // 2 : 9 + i // 2, at : at + 128]
 
 
 def gelu_parts(z):
@@ -79,35 +109,50 @@
             mixed = mixed + small[3:4, :]
         qkv_ref[:, cols] = mixed.astype(BF)
     lane = lax.broadcasted_iota(jnp.int32, (rows, 128), 1)
-    for pair in range(HEADS // 2):
-        q = qkv_ref[:, pair * 128 : pair * 128 + 128]
-        k = qkv_ref[:, width + pair * 128 : width + pair * 128 + 128]
-        vt = qkv_ref[:, 2 * width + pair * 128 : 2 * width + pair * 128 + 128].T
-        for side in range(2):
-            half = (lane < 64) if side == 0 else (lane >= 64)
-            k_half = jnp.where(half, k, jnp.zeros_like(k))
-            scores = mm_nt(k_half, q) * 0.125 + bias_ref[...]
-            peak = jnp.max(scores, axis=0, keepdims=True)
-            raised = jnp.exp(scores - peak)
-            summed = jnp.sum(raised, axis=0, keepdims=True)
-            mixed = mm(vt[side * 64 : side * 64 + 64, :], raised.astype(BF)) * (1.0 / summed)
-            at = pair * 128 + side * 64
-            ot_ref[at : at + 64, :] = mixed.astype(BF)
-            head = 2 * pair + side
+    scores, raised, inverse = {}, {}, {}
+    for step in range(HEADS + 2):
+        if step < HEADS:
+            at = step // 2 * 128
+            half = (lane < 64) if step % 2 == 0 else (lane >= 64)
+            k = qkv_ref[:, width + at : width + at + 128]
+            k = jnp.where(half, k, jnp.zeros_like(k)) * jnp.asarray(0.125, BF)
+            scores[step] = mm_nt(k, qkv_ref[:, at : at + 128])
+        head = step - 1
+        if 0 <= head < HEADS:
+            shifted = scores.pop(head) + bias_ref[...]
+            peak = jnp.max(shifted, axis=0, keepdims=True)
+            grown = jnp.exp(shifted - peak)
+            summed = jnp.sum(grown, axis=0, keepdims=True)
+            raised[head] = grown.astype(BF)
+            inverse[head] = 1.0 / summed
             lse_ref[head : head + 1, :] = peak + jnp.log(summed)
+        head = step - 2
+        if 0 <= head < HEADS:
+            if head % 2 == 0:
+                vt = qkv_ref[:, 2 * width + head * 64 : 2 * width + head * 64 + 128].T
+            mixed = mm(vt[head % 2 * 64 : head % 2 * 64 + 64, :], raised.pop(head)) * inverse.pop(head)
+            ot_ref[head * 64 : head * 64 + 64, :] = mixed.astype(BF)
     o_ref[...] = ot_ref[...].T
     h = x_ref[...].astype(F32) + (mm(o_ref[...], wproj[...]) + small[4:5, :])
     h_ref[...] = h
     normed, _ = norm_parts(h)
     a2_ref[...] = (normed * small[5:6, :] + small[6:7, :]).astype(BF)
     before_up()
-    for part in range(hidden // width):
-        cols = slice(part * width, (part + 1) * width)
-        z = mm(a2_ref[...], wup[:, cols]) + small[8 + part : 9 + part, :]
-        u, slope = gelu_parts(z)
-        u_ref[:, cols] = u.astype(BF)
-        gp_ref[:, cols] = slope.astype(BF)
-    out_ref[...] = (h_ref[...] + (mm(u_ref[...], wdown[...]) + small[7:8, :])).astype(BF)
+    chunk = width
+    z = {}
+    for step in range(hidden // chunk + 1):
+        cols = slice(step * chunk, (step + 1) * chunk)
+        if step < hidden // chunk:
+            row, start = 8 + step * chunk // width, step * chunk % width
+            z[step] = mm(a2_ref[...], wup[:, cols]) + small[row : row + 1, start : start + chunk]
+        part = step - 1
+        if 0 <= part < hidden // chunk:
+            cols = slice(part * chunk, (part + 1) * chunk)
+            u, slope = gelu_parts(z.pop(part))
+            u_ref[:, cols] = u.astype(BF)
+            gp_ref[:, cols] = slope.astype(BF)
+    total = mm(u_ref[...], wdown[...])
+    out_ref[...] = (h_ref[...] + (total + small[7:8, :])).astype(BF)
 
 
 def layer_backward(g_ref, x_ref, bias_ref, qkv_ref, lse_ref, h_ref, gp_ref, wqkv, wproj, wup, wdown,
@@ -116,12 +161,16 @@
     hidden = wup.shape[1]
     carried = g_ref[...].astype(F32)
     sums_ref[7:8, :] += column_sum(carried)
-    for part in range(hidden // width):
-        cols = slice(part * width, (part + 1) * width)
-        back = mm_nt(g_ref[...], wdown[cols, :])
-        dz = (back * gp_ref[:, cols].astype(F32)).astype(BF)
-        dz_ref[:, cols] = dz
-        sums_ref[8 + part : 9 + part, :] += column_sum(dz.astype(F32))
+    back = {}
+    for step in range(hidden // width + 1):
+        if step < hidden // width:
+            back[step] = mm_nt(g_ref[...], wdown[step * width : (step + 1) * width, :])
+        part = step - 1
+        if part >= 0:
+            cols = slice(part * width, (part + 1) * width)
+            dz = (back.pop(part) * gp_ref[:, cols].astype(F32)).astype(BF)
+            dz_ref[:, cols] = dz
+            sums_ref[8 + part : 9 + part, :] += column_sum(dz.astype(F32))
     back = mm_nt(dz_ref[...], wup[...])
     normed, inv = norm_parts(h_ref[...])
     sums_ref[5:6, :] += column_sum(back * normed)
@@ -133,32 +182,36 @@
     sums_ref[4:5, :] += column_sum(f.astype(F32))
     do_ref[...] = mm_nt(f_ref[...], wproj[...]).astype(BF)
     lane = lax.broadcasted_iota(jnp.int32, (rows, 128), 1)
-    for pair in range(HEADS // 2):
-        q = qkv_ref[:, pair * 128 : pair * 128 + 128]
-        k = qkv_ref[:, width + pair * 128 : width + pair * 128 + 128]
-        v = qkv_ref[:, 2 * width + pair * 128 : 2 * width + pair * 128 + 128]
-        do = do_ref[:, pair * 128 : pair * 128 + 128]
-        kt = k.T
-        dv_sides = []
-        dk_sides = []
-        for side in range(2):
-            half = (lane < 64) if side == 0 else (lane >= 64)
-            k_half = jnp.where(half, k, jnp.zeros_like(k))
-            v_half = jnp.where(half, v, jnp.zeros_like(v))
-            head = 2 * pair + side
-            scores = mm_nt(k_half, q) * 0.125 + bias_ref[...]
-            probs = jnp.exp(scores - lse_ref[head : head + 1, :])
-            dv_sides.append(mm(probs.astype(BF), do))
-            dp = mm_nt(v_half, do)
-            inner = jnp.sum(probs * dp, axis=0, keepdims=True)
-            ds = (probs * (dp - inner)).astype(BF)
-            dk_sides.append(mm(ds, q))
-            at = pair * 128 + side * 64
-            dqt_ref[at : at + 64, :] = (mm(kt[side * 64 : side * 64 + 64, :], ds) * 0.125).astype(BF)
-        at = width + pair * 128
-        r_ref[:, at : at + 128] = (jnp.where(lane < 64, dk_sides[0], dk_sides[1]) * 0.125).astype(BF)
-        at = 2 * width + pair * 128
-        r_ref[:, at : at + 128] = jnp.where(lane < 64, dv_sides[0], dv_sides[1]).astype(BF)
+    scores, grads, probs, slopes, dks, dvs = {}, {}, {}, {}, {}, {}
+    eighth = jnp.asarray(0.125, BF)
+    for step in range(HEADS + 2):
+        if step < HEADS:
+            at = step // 2 * 128
+            half = (lane < 64) if step % 2 == 0 else (lane >= 64)
+            k = qkv_ref[:, width + at : width + at + 128]
+            v = qkv_ref[:, 2 * width + at : 2 * width + at + 128]
+            scores[step] = mm_nt(jnp.where(half, k, jnp.zeros_like(k)) * eighth, qkv_ref[:, at : at + 128])
+            grads[step] = mm_nt(jnp.where(half, v, jnp.zeros_like(v)), do_ref[:, at : at + 128])
+        head = step - 1
+        if 0 <= head < HEADS:
+            p = jnp.exp(scores.pop(head) + bias_ref[...] - lse_ref[head : head + 1, :])
+            dp = grads.pop(head)
+            inner = jnp.sum(p * dp, axis=0, keepdims=True)
+            slopes[head] = (p * (dp - inner)).astype(BF)
+            probs[head] = p.astype(BF)
+        head = step - 2
+        if 0 <= head < HEADS:
+            at = head // 2 * 128
+            side = head % 2
+            ds = slopes.pop(head)
+            dvs[side] = mm(probs.pop(head), do_ref[:, at : at + 128])
+            dks[side] = mm(ds, qkv_ref[:, at : at + 128] * eighth)
+            if side == 0:
+                kt = (qkv_ref[:, width + at : width + at + 128] * eighth).T
+            dqt_ref[head * 64 : head * 64 + 64, :] = mm(kt[side * 64 : side * 64 + 64, :], ds).astype(BF)
+            if side == 1:
+                r_ref[:, width + at : width + at + 128] = jnp.where(lane < 64, dks[0], dks[1]).astype(BF)
+                r_ref[:, 2 * width + at : 2 * width + at + 128] = jnp.where(lane < 64, dvs[0], dvs[1]).astype(BF)
     r_ref[:, 0:width] = dqt_ref[...].T
     sums_ref[2:3, :] += column_sum(r_ref[:, 0:width].astype(F32))
     sums_ref[3:4, :] += column_sum(r_ref[:, 2 * width :].astype(F32))
@@ -207,6 +260,15 @@
     def back(self):
         return Spot(self.x, self.z // 2, 2 * self.c + self.y, self.z % 2)
 
+    def feeds(self, stage, core):
+        return ((self.y == self.z % 2) & (self.c == core)) & (self.z >= 0)
+
+    def fed_at(self, stage):
+        return Spot(self.x, self.y, stage, self.z // 2)
+
+    def feeder(self, core):
+        return Spot(self.x, self.y, 2 * self.c + self.y, core)
+
     def crosses(self):
         return (self.z + self.c) % 2 == 1
 
@@ -229,7 +291,15 @@
     pl.semaphore_signal(pltpu.get_barrier_semaphore(), inc=1, device_id=spot.id(), device_id_type=MESH)
 
 
-def greet(line, turned):
+def hail_feeding(me, stage, core):
+    gives = me.feeds(stage, core) & jnp.logical_not(same(me, me.fed_at(stage)))
+    takes = (me.z == stage) & jnp.logical_not(same(me, me.feeder(core)))
+    pl.when(gives)(lambda: hail(me.fed_at(stage)))
+    pl.when(takes)(lambda: hail(me.feeder(core)))
+    return jnp.where(gives, 1, 0) + jnp.where(takes, 1, 0)
+
+
+def greet(line, turned, feeding=False):
     stage = line.stage()
     barrier = pltpu.get_barrier_semaphore()
 
@@ -252,12 +322,14 @@
             hail(me.ahead())
 
         expected = expected + jnp.where(alone, 0, 2)
+        if feeding:
+            expected = expected + hail_feeding(me, 0, 0)
     pl.semaphore_wait(barrier, expected)
 
 
-def forward_kernel(line, length, turned, x_first, x_in, segr, segc, cls, wqkv_h, wproj_h, wup_h, wdown_h, small,
+def forward_kernel(line, length, turned, x_first, x_in, words, wqkv_h, wproj_h, wup_h, wdown_h, small_in,
                    x_o, a_o, qkv_o, lse_o, o_o, h_o, a2_o, gp_o, u_o, acts_o, home_o,
-                   wqkv, wproj, wup, wdown, xs, outs, a, qkv, lse, o, h, a2, gp, u, bias, ot,
+                   wqkv, wproj, wup, wdown, xs, outs, a, qkv, lse, o, h, a2, gp, u, bias, ot, small,
                    w_sem, in_sem, x_sem, save_sem, act_sem, send_sem, recv_sem, home_sem):
     micro = xs.shape[0]
     stage = line.stage()
@@ -271,20 +343,24 @@
     def first_in(m):
         return pltpu.make_async_copy(x_in.at[m], xs.at[m], in_sem.at[m])
 
-    greet(line, turned)
+    if turned:
+        spread_small(small_in, small)
+    else:
+        small[...] = small_in[...]
+    greet(line, turned, feeding=True)
     if turned:
         me = Spot.here()
-        ahead, back = me.ahead(), me.back()
+        back = me.back()
         alone = same(me, back)
 
         def turn_in(m):
             return pltpu.make_async_remote_copy(
                 src_ref=x_in.at[m], dst_ref=xs.at[m], send_sem=in_sem.at[m], recv_sem=recv_sem.at[m],
-                device_id=ahead.id(), device_id_type=MESH)
-
-        feeds = jnp.logical_and(me.section() == 0, jnp.logical_not(alone))
-        fed = jnp.logical_and(stage == 0, jnp.logical_not(alone))
-        feeds_self = jnp.logical_and(stage == 0, alone)
+                device_id=taker.id(), device_id_type=MESH)
+
+        taker, feeder = me.fed_at(0), me.feeder(0)
+        feeds = me.feeds(0, 0) & jnp.logical_not(same(me, taker))
+        feeds_self = me.feeds(0, 0) & same(me, taker)
         homing = jnp.logical_and(stage >= 2, jnp.logical_not(alone))
         homed = jnp.logical_and(me.section() >= 2, jnp.logical_not(alone))
         settled = jnp.logical_and(stage >= 2, alone)
@@ -356,7 +432,7 @@
             loads[0].wait()
             loads[1].wait()
 
-        bias[...] = mask_bias(segr[m], segc[m], cls[m], length)
+        bias[...] = micro_bias(words, m, micro, length)
 
         def before_up():
             @pl.when(m == 0)
@@ -406,10 +482,10 @@
             pl.when(settled)(lambda: settle(m).wait())
 
 
-def backward_kernel(line, length, turned, acts_h, g_in, x_h, qkv_h, lse_h, h_h, gp_h, segr, segc, cls,
-                    wqkv_h, wproj_h, wup_h, wdown_h, small,
-                    acts_o, home_o, g_o, dz_o, f_o, r_o, gin_o, sums_o,
-                    wqkv, wproj, wup, wdown, gs, gins, x, qkv, lse, h, gp, dz, f, r, bias, do, dh, dqt,
+def backward_kernel(line, length, turned, acts_h, g_in, x_h, qkv_h, lse_h, h_h, gp_h, words,
+                    wqkv_h, wproj_h, wup_h, wdown_h, small_in,
+                    acts_o, home_o, g_o, dz_o, f_o, r_o, gin_o, sums_out,
+                    wqkv, wproj, wup, wdown, gs, gins, x, qkv, lse, h, gp, dz, f, r, bias, do, dh, dqt, small, sums_o,
                     w_sem, in_sem, g_sem, load_sem, save_sem, act_sem, send_sem, recv_sem, home_sem, back_sem):
     micro = gs.shape[0]
     stage = line.stage()
@@ -440,6 +516,10 @@
     for load in loads[1:]:
         load.start()
     sums_o[...] = jnp.zeros_like(sums_o)
+    if turned:
+        spread_small(small_in, small)
+    else:
+        small[...] = small_in[...]
     greet(line, turned)
     if turned:
         me = Spot.here()
@@ -501,7 +581,7 @@
 
         for fetch in fetches(m, slot):
             fetch.wait()
-        bias[...] = mask_bias(segr[m], segc[m], cls[m], length)
+        bias[...] = micro_bias(words, m, micro, length)
 
         @pl.when(m >= 2)
         def _():
@@ -534,6 +614,10 @@
         return carry
 
     lax.fori_loop(0, micro, step, 0)
+    if turned:
+        share_small(sums_o, sums_out)
+    else:
+        sums_out[...] = sums_o[...]
 
     for m in range(max(micro - 2, 0), micro):
         for save in saves(m, m % 2):
@@ -567,7 +651,7 @@
 DMA = pltpu.SemaphoreType.DMA
 
 
-def run_forward(line, length, turned, x_first, x_in, segr, segc, cls, weights, small):
+def run_forward(line, length, turned, x_first, x_in, words, weights, small):
     micro, rows, width = x_in.shape
     hidden = weights[2].shape[1]
     shape = jax.ShapeDtypeStruct
@@ -578,21 +662,21 @@
     return pl.pallas_call(
         functools.partial(forward_kernel, line, length, turned),
         out_shape=[many] + [shape((micro,) + s, t) for s, t in saved] + [many, many],
-        in_specs=[ANYWHERE, ANYWHERE, IN_VMEM, IN_VMEM, IN_SMEM] + [ANYWHERE] * 4 + [IN_VMEM],
+        in_specs=[ANYWHERE, ANYWHERE, IN_VMEM] + [ANYWHERE] * 4 + [IN_VMEM],
         out_specs=[ANYWHERE] * 11,
         scratch_shapes=[pltpu.VMEM(w.shape, BF) for w in weights]
         + [pltpu.VMEM((micro, rows, width), BF)] * 2
         + [pltpu.VMEM((2,) + s, t) for s, t in saved]
-        + [pltpu.VMEM((rows, rows), F32), pltpu.VMEM((width, rows), BF)]
+        + [pltpu.VMEM((rows, rows), F32), pltpu.VMEM((width, rows), BF), pltpu.VMEM((16, width), F32)]
         + [DMA((4,)), DMA((micro,)), DMA((micro,)), DMA((2, 8)), DMA((micro,)), DMA((micro,)), DMA((micro,)),
            DMA((2, micro))],
         compiler_params=pltpu.CompilerParams(
             collective_id=0, has_side_effects=True, vmem_limit_bytes=VMEM_CAP),
         name="forward_line",
-    )(x_first, x_in, segr, segc, cls, *weights, small)
-
-
-def run_backward(line, length, turned, acts, g_in, x, qkv, lse, h, gp, segr, segc, cls, weights, small):
+    )(x_first, x_in, words, *weights, small)
+
+
+def run_backward(line, length, turned, acts, g_in, x, qkv, lse, h, gp, words, weights, small):
     micro, rows, width = g_in.shape
     hidden = weights[2].shape[1]
     shape = jax.ShapeDtypeStruct
@@ -601,8 +685,8 @@
     return pl.pallas_call(
         functools.partial(backward_kernel, line, length, turned),
         out_shape=[many, many, many, shape((micro, rows, hidden), BF), many, shape((micro, rows, 3 * width), BF), many,
-                   shape((16, width), F32)],
-        in_specs=[ANYWHERE] * 7 + [IN_VMEM, IN_VMEM, IN_SMEM] + [ANYWHERE] * 4 + [IN_VMEM],
+                   shape(small.shape, F32)],
+        in_specs=[ANYWHERE] * 7 + [IN_VMEM] + [ANYWHERE] * 4 + [IN_VMEM],
         out_specs=[ANYWHERE] * 7 + [IN_VMEM],
         scratch_shapes=[pltpu.VMEM(w.shape, BF) for w in weights]
         + [pltpu.VMEM((micro, rows, width), BF)] * 2
@@ -610,13 +694,13 @@
            pltpu.VMEM((2, rows, width), F32), pltpu.VMEM((2, rows, hidden), BF),
            pltpu.VMEM((2, rows, hidden), BF), pltpu.VMEM((2, rows, width), BF), pltpu.VMEM((2, rows, 3 * width), BF),
            pltpu.VMEM((rows, rows), F32), pltpu.VMEM((rows, width), BF), pltpu.VMEM((rows, width), F32),
-           pltpu.VMEM((width, rows), BF)]
+           pltpu.VMEM((width, rows), BF), pltpu.VMEM((16, width), F32), pltpu.VMEM((16, width), F32)]
         + [DMA((4,)), DMA((micro,)), DMA((micro,)), DMA((2, 5)), DMA((2, 3)), DMA((micro,)), DMA((micro,)),
            DMA((micro,)), DMA((2, micro)), DMA((2, micro))],
         compiler_params=pltpu.CompilerParams(
             collective_id=1, has_side_effects=True, vmem_limit_bytes=VMEM_CAP),
         name="backward_line",
-    )(acts, g_in, x, qkv, lse, h, gp, segr, segc, cls, wqkv, wproj, wup, wdown, small)
+    )(acts, g_in, x, qkv, lse, h, gp, words, wqkv, wproj, wup, wdown, small)
 
 
 GATHER_PIECES = ((0, 0, 48, "c"), (0, 48, 48, "x"), (4, 0, 16, "x"), (1, 0, 96, "c"), (2, 0, 48, "x"), (2, 48, 48, "c"),
@@ -625,9 +709,16 @@
 
 def gather_kernel(pieces, micro, *refs):
     count = 5
-    shares, (x_in, g_in, seg_in) = refs[:count], refs[count : count + 3]
-    wholes, (x_o, g_o, seg_o) = refs[count + 3 : 2 * count + 3], refs[2 * count + 3 : 2 * count + 6]
-    swap, (send, recv, local, turn_send, turn_recv) = refs[2 * count + 6 : 3 * count + 6], refs[3 * count + 6 :]
+    masters, (x_in, g_in, seg_in) = refs[:count], refs[count : count + 3]
+    wholes, (x_o, x_all, g_o, seg_o) = refs[count + 3 : 2 * count + 3], refs[2 * count + 3 : 2 * count + 7]
+    refs = refs[2 * count + 7 :]
+    swap, wide, narrow, (x_raw, g_raw, x_pad, g_pad) = refs[:5], refs[5:9], refs[9:13], refs[13:17]
+    send, recv, local, turn_send, turn_recv, load_sem = refs[17:]
+    shares = narrow + (masters[4],)
+    loads = [pltpu.make_async_copy(masters[i], wide[i], load_sem.at[i]) for i in range(4)]
+    loads += [pltpu.make_async_copy(x_in, x_raw, load_sem.at[4]), pltpu.make_async_copy(g_in, g_raw, load_sem.at[5])]
+    for i in (0, 1, 2, 3, 4, 5):
+        loads[i].start()
     me = Spot.here()
     xn, yn, cn = me.flip(x=1), me.flip(y=1), me.flip(c=1)
     target, source, ahead, back = me.drop(), me.source(), me.ahead(), me.back()
@@ -648,7 +739,8 @@
         hail(ahead)
         hail(back)
 
-    pl.semaphore_wait(pltpu.get_barrier_semaphore(), 3 + jnp.where(stays, 0, 2) + jnp.where(alone, 0, 2))
+    fed = hail_feeding(me, 0, 0) + hail_feeding(me, 3, 1)
+    expected = 3 + jnp.where(stays, 0, 2) + jnp.where(alone, 0, 2) + fed
 
     def rows(k, part):
         array, first, size, _ = pieces[k]
@@ -688,30 +780,56 @@
 
     own, own_x, own_y, own_d = parts(me)
     beside = parts(cn)
-    turns = [(x_in, x_o), (seg_in, seg_o)] + [(g_in.at[m], g_o.at[m]) for m in range(micro)]
-    gives = [me.section() == 0, me.section() >= 0] + [me.section() == 3] * micro
+    turns = [(x_pad.at[0], x_o), (seg_in, seg_o)] + [(g_pad.at[m], g_o.at[m]) for m in range(micro)]
+    gives = [me.feeds(0, 0), me.z >= 0] + [me.feeds(3, 1)] * micro
     takes = [me.z == 0, me.z >= 0] + [me.z == 3] * micro
+    takers = [me.fed_at(0), ahead] + [me.fed_at(3)] * micro
+    givers = [me.feeder(0), back] + [me.feeder(1)] * micro
 
     def turn(i):
         return pltpu.make_async_remote_copy(
             src_ref=turns[i][0], dst_ref=turns[i][1], send_sem=turn_send.at[i], recv_sem=turn_recv.at[i],
-            device_id=ahead.id(), device_id_type=MESH)
+            device_id=takers[i].id(), device_id_type=MESH)
 
     def turn_start(i):
-        pl.when(gives[i] & alone)(lambda: pltpu.make_async_copy(*turns[i], turn_send.at[i]).start())
-        pl.when(gives[i] & pairs)(lambda: turn(i).start())
+        here = same(me, takers[i])
+        pl.when(gives[i] & here)(lambda: pltpu.make_async_copy(*turns[i], turn_send.at[i]).start())
+        pl.when(gives[i] & jnp.logical_not(here))(lambda: turn(i).start())
 
     def turn_end(i):
-        pl.when(gives[i] & alone)(lambda: pltpu.make_async_copy(*turns[i], turn_send.at[i]).wait())
-        pl.when(gives[i] & pairs)(lambda: turn(i).wait_send())
-        pl.when(takes[i] & pairs)(lambda: turn(i).wait_recv())
-
+        here = same(me, takers[i])
+        pl.when(gives[i] & here)(lambda: pltpu.make_async_copy(*turns[i], turn_send.at[i]).wait())
+        pl.when(gives[i] & jnp.logical_not(here))(lambda: turn(i).wait_send())
+        pl.when(takes[i] & jnp.logical_not(same(me, givers[i])))(lambda: turn(i).wait_recv())
+
+    def pad(raw, padded):
+        for m in range(micro):
+            short = raw[m]
+            rest = jnp.zeros((padded.shape[1] - short.shape[0], short.shape[1]), short.dtype)
+            padded[m] = jnp.concatenate([short, rest], axis=0)
+
+    ready = set()
     for k in range(len(pieces)):
+        array = pieces[k][0]
+        if array < 4 and array not in ready:
+            ready.add(array)
+            loads[array].wait()
+            size = wide[array].shape[0]
+            for first in range(0, size, 48):
+                narrow[array][first : first + 48, :] = wide[array][first : first + 48, :].astype(BF)
+        if k == 0:
+            pl.semaphore_wait(pltpu.get_barrier_semaphore(), expected)
         pl.when(stays)(lambda: kept(k).start())
         pl.when(direct)(lambda: brought(k, me.dp()).start())
         pl.when(crosses)(lambda: crossed(k).start())
     turn_start(1)
+    loads[4].wait()
+    pad(x_raw, x_pad)
     turn_start(0)
+    x_save = pltpu.make_async_copy(x_pad, x_all, load_sem.at[4])
+    x_save.start()
+    loads[5].wait()
+    pad(g_raw, g_pad)
     for k in range(len(pieces) + 3):
         if k < len(pieces):
             @pl.when(crosses)
@@ -751,24 +869,30 @@
             passed(kind, k, own, cn).wait_send()
     for i in range(len(turns)):
         turn_end(i)
-
-
-def run_gather(shares, x_first, g, segs):
+    x_save.wait()
+
+
+def run_gather(masters, inputs, g, words, rows):
     pieces = GATHER_PIECES
-    micro = g.shape[0]
+    micro, _, width = g.shape
     shape = jax.ShapeDtypeStruct
+    shares = [shape(m.shape, BF) for m in masters[:4]] + [shape(masters[4].shape, F32)]
+    many = shape((micro, rows, width), BF)
     outs = [shape((s.shape[0] * 8,) + s.shape[1:], s.dtype) for s in shares]
-    outs += [shape(v.shape, v.dtype) for v in (x_first, g, segs)]
+    outs += [shape((rows, width), BF), many, many, shape(words.shape, words.dtype)]
     return pl.pallas_call(
         functools.partial(gather_kernel, pieces, micro),
         out_shape=outs,
         in_specs=[ANYWHERE] * 8,
-        out_specs=[ANYWHERE] * 8,
-        scratch_shapes=[pltpu.VMEM(s.shape, s.dtype) for s in shares]
-        + [DMA((9, len(pieces))), DMA((9, len(pieces))), DMA((len(pieces),)), DMA((2 + micro,)), DMA((2 + micro,))],
+        out_specs=[ANYWHERE] * 9,
+        scratch_shapes=[pltpu.VMEM(s.shape, s.dtype) for s in shares] + [pltpu.VMEM(m.shape, F32) for m in masters[:4]]
+        + [pltpu.VMEM(s.shape, BF) for s in shares[:4]] + [pltpu.VMEM(g.shape, BF)] * 2
+        + [pltpu.VMEM((micro, rows, width), BF)] * 2
+        + [DMA((9, len(pieces))), DMA((9, len(pieces))), DMA((len(pieces),)), DMA((2 + micro,)), DMA((2 + micro,)),
+           DMA((6,))],
         compiler_params=pltpu.CompilerParams(collective_id=2, has_side_effects=True, vmem_limit_bytes=VMEM_CAP),
         name="gather_layers",
-    )(*shares, x_first, g, segs)
+    )(*masters, inputs, g, words)
 
 
 SCATTER_PIECES = ((3, 0, 128, 0, 768, "x"), (3, 128, 128, 0, 768, "x"), (3, 256, 128, 0, 768, "x"),
@@ -923,6 +1047,7 @@
         now = (me.z >= 2) | (m == micro - 1)
         pl.when(alone & now)(lambda: turn_stay(m).start())
         pl.when(pairs & now)(lambda: turn(m).start())
+    tally = jnp.zeros((8, 128), F32)
     for k in range(len(pieces) + 4):
         if k < len(pieces):
             if k > 0:
@@ -961,7 +1086,11 @@
             to_x(b).wait_recv()
             to_y(b).wait_recv()
             total = (whole(b, kept[0])[...].astype(F32) + of(from_x, b)[...].astype(F32) + of(from_y, b)[...].astype(F32))
-            done[pieces[b][0]][box(b)] = total.astype(done[pieces[b][0]].dtype)
+            total = total.astype(done[pieces[b][0]].dtype)
+            done[pieces[b][0]][box(b)] = total
+            square = total.astype(F32) * total.astype(F32)
+            for c in range(0, square.shape[1], 128):
+                tally = tally + jnp.sum(square[:, c : c + 128].reshape(-1, 8, 128), axis=0)
             pl.when(stays)(lambda: stay_home(b).start())
             pl.when(moves & jnp.logical_not(target_crosses))(lambda: to_home(b).start())
             pl.when(target_crosses)(lambda: to_swap(b).start())
@@ -971,15 +1100,6 @@
             def _():
                 to_swap(b).wait_recv()
                 over(b).start()
-    tally = jnp.zeros((8, 128), F32)
-    for k in range(len(pieces)):
-        pl.when(stays)(lambda: stay_home(k).wait())
-        pl.when(moves & jnp.logical_not(crosses))(lambda: to_home(k).wait_recv())
-        pl.when(crosses)(lambda: over(k).wait_recv())
-        value = of(home, k)[...].astype(F32)
-        value = value * value
-        for c in range(0, value.shape[1], 128):
-            tally = tally + jnp.sum(value[:, c : c + 128].reshape(-1, 8, 128), axis=0)
     sums[0] = tally
 
     def note(i, src, slot, spot):
@@ -989,8 +1109,6 @@
 
     for i, spot in enumerate(column):
         note(i, sums.at[0], i, spot).start()
-    for array in range(count):
-        pltpu.make_async_copy(home[array], outs[array], out_sem.at[array]).start()
     for i, spot in enumerate(column):
         note(i, sums.at[0], i, spot).wait_recv()
         tally = tally + tallies[i]
@@ -1000,7 +1118,18 @@
     for i, spot in enumerate(slab):
         note(3 + i, sums.at[1], 3 + i, spot).wait_recv()
         tally = tally + tallies[3 + i]
-    norm_o[...] = tally
+    whole_norm = jnp.sqrt(jnp.sum(jnp.sum(tally, axis=0, keepdims=True), axis=1, keepdims=True))
+    norm_o[...] = jnp.broadcast_to(whole_norm, norm_o.shape)
+    last = {}
+    for k in range(len(pieces)):
+        last[pieces[k][0]] = k
+    for k in range(len(pieces)):
+        pl.when(stays)(lambda: stay_home(k).wait())
+        pl.when(moves & jnp.logical_not(crosses))(lambda: to_home(k).wait_recv())
+        pl.when(crosses)(lambda: over(k).wait_recv())
+        array = pieces[k][0]
+        if last[array] == k:
+            pltpu.make_async_copy(home[array], outs[array], out_sem.at[array]).start()
     for i, spot in enumerate(column):
         note(i, sums.at[0], i, spot).wait_send()
     for i, spot in enumerate(slab):
@@ -1047,6 +1176,90 @@
     )(*operands, small, gin)
 
 
+def finish_kernel(order, micro, norm, *refs):
+    shards_h, state_h, (acts_early, acts_late, gin_early, gin_late) = refs[:4], refs[4:16], refs[16:20]
+    state_o, acts_o, gin_o = refs[20:36], refs[36], refs[37]
+    shards, state, (acts, gin, acts_cut, gin_cut) = refs[38:42], refs[42:58], refs[58:62]
+    load_sem, pick_sem, out_sem = refs[62:]
+    upper = lax.axis_index("section") >= 2
+
+    def loads(array):
+        copies = [pltpu.make_async_copy(shards_h[array], shards[array], load_sem.at[array, 0])]
+        for i in range(3):
+            copies.append(pltpu.make_async_copy(state_h[4 * i + array], state[4 * (i + 1) + array], load_sem.at[array, 1 + i]))
+        return copies
+
+    def pick(i, m, src, dst):
+        return pltpu.make_async_copy(src.at[m], dst.at[m], pick_sem.at[i, m])
+
+    def saves(array):
+        return [pltpu.make_async_copy(state[4 * i + array], state_o[4 * array + i], out_sem.at[array, i]) for i in range(4)]
+
+    for array in order:
+        for copy in loads(array):
+            copy.start()
+    for i, (early, late, dst, is_early) in enumerate(
+            ((acts_early, acts_late, acts, upper), (gin_early, gin_late, gin, jnp.logical_not(upper)))):
+        for m in range(micro):
+            if m == micro - 1:
+                pick(i, m, late, dst).start()
+            else:
+                pl.when(is_early)(lambda: pick(i, m, early, dst).start())
+                pl.when(jnp.logical_not(is_early))(lambda: pick(i, m, late, dst).start())
+    factor = 1.0 / jnp.maximum(norm[0:1, 0:1], 1.0)
+    fix = 1.0 / (1.0 - 0.5**STEP)
+    strip = 16
+    for array in order:
+        for copy in loads(array):
+            copy.wait()
+        grads, master, first, second = state[array], state[4 + array], state[8 + array], state[12 + array]
+
+        def update(i, carry):
+            rows = pl.ds(pl.multiple_of(i * strip, strip), strip)
+            grad = shards[array][rows, :].astype(F32) * factor
+            first_new = 0.5 * first[rows, :] + 0.5 * grad
+            second_new = 0.5 * second[rows, :] + 0.5 * grad * grad
+            old = master[rows, :]
+            change = (first_new * fix) / (jnp.sqrt(second_new * fix) + adam_eps) + decay_rate * old
+            grads[rows, :] = grad
+            first[rows, :] = first_new
+            second[rows, :] = second_new
+            master[rows, :] = old - learn_rate * change
+            return carry
+
+        lax.fori_loop(0, grads.shape[0] // strip, update, 0)
+        for copy in saves(array):
+            copy.start()
+    length = acts_cut.shape[1]
+    for i, (src, cut, out) in enumerate(((acts, acts_cut, acts_o), (gin, gin_cut, gin_o))):
+        for m in range(micro):
+            pick(i, m, gin_late, src).wait()
+            cut[m] = src[m, 0:length, :]
+        pltpu.make_async_copy(cut, out, out_sem.at[4, i]).start()
+    for array in order:
+        for copy in saves(array):
+            copy.wait()
+    for i, (cut, out) in enumerate(((acts_cut, acts_o), (gin_cut, gin_o))):
+        pltpu.make_async_copy(cut, out, out_sem.at[4, i]).wait()
+
+
+def run_finish(norm, shards, states, tall, length):
+    micro, rows, width = tall[0].shape
+    shape = jax.ShapeDtypeStruct
+    return pl.pallas_call(
+        functools.partial(finish_kernel, (1, 0, 2, 3), micro),
+        out_shape=[shape(s.shape, F32) for s in shards for _ in range(4)] + [shape((micro, length, width), BF)] * 2,
+        in_specs=[IN_VMEM] + [ANYWHERE] * 20,
+        out_specs=[ANYWHERE] * 18,
+        scratch_shapes=[pltpu.VMEM(s.shape, BF) for s in shards]
+        + [pltpu.VMEM(s.shape, F32) for _ in range(4) for s in shards]
+        + [pltpu.VMEM((micro, rows, width), BF)] * 2 + [pltpu.VMEM((micro, length, width), BF)] * 2
+        + [DMA((4, 4)), DMA((2, micro)), DMA((5, 4))],
+        compiler_params=pltpu.CompilerParams(vmem_limit_bytes=VMEM_CAP),
+        name="finish",
+    )(norm, *shards, *states, *tall)
+
+
 def split_small(small, width, slices):
     share = width // slices
     stacked = small.reshape(slices, small.shape[0] // slices)
@@ -1070,6 +1283,16 @@
                            preferred_element_type=F32)
 
 
+def adam(grad, master, first, second, rate, decay):
+    fix = 1.0 - 0.5**STEP
+    first = 0.5 * first + 0.5 * grad
+    second = 0.5 * second + 0.5 * grad * grad
+    update = first / fix / (jnp.sqrt(second / fix) + adam_eps)
+    if decay:
+        update = update + decay * master
+    return [grad, master - rate * update, first, second]
+
+
 def per_device(inputs, out_grad, segment_ids, cls_index, *states):
     masters, firsts, seconds = states[0:5], states[5:10], states[10:15]
     slices = lax.axis_size("dp")
@@ -1077,64 +1300,55 @@
     turned = slices == 8 and stages == 4
     seq_dev, length, width = inputs.shape
     rows = -(-length // 128) * 128
-    total = masters[4].shape[1] * slices
-
-    extra = ((0, 0), (0, rows - length), (0, 0))
-    x_in = jnp.pad(inputs, extra)
-    g_in = jnp.pad(out_grad, extra)
+    share = masters[4].shape[1]
+    total = share * slices
+
     segs = jnp.pad(segment_ids, ((0, 0), (0, rows - length)), constant_values=-1)
-    shares = [m.astype(BF)[0] for m in masters]
+    words = jnp.concatenate([segs, jnp.broadcast_to(cls_index[:, None], (seq_dev, rows))], axis=0)
     if turned:
         line = Line("dp", 4, 2)
-        lanes = masters[4].shape[1] // 128
-        shares[4] = jnp.pad(shares[4].astype(F32).reshape(lanes, 128), ((0, 16 - lanes), (0, 0)))
-        words = jnp.concatenate([segs, jnp.broadcast_to(cls_index[:, None], (seq_dev, rows))], axis=0)
-        *gathered, x_first, g_in, words = run_gather(shares, x_in[0], g_in, words)
-        segs, classes = words[:seq_dev], words[seq_dev:, 0]
-        flat = gathered[4].reshape(slices, 16, 128)[:, :lanes].reshape(-1)
+        eighth = width // slices
+        flat = masters[4][0].astype(BF).astype(F32)
+        small = jnp.concatenate([
+            jnp.pad(flat[: 8 * eighth].reshape(8, eighth), ((0, 0), (0, 128 - eighth))),
+            flat[8 * eighth :].reshape(-1, 128), jnp.zeros((8 - (share - 8 * eighth) // 128, 128), F32)], axis=0)
+        *weights, small, x_first, x_in, g_in, words = run_gather(
+            [m[0] for m in masters[:4]] + [small], inputs, out_grad, words, rows)
     else:
         line = Line("section", stages, 1)
-        gathered = [lax.all_gather(s, "dp", axis=0, tiled=True) for s in shares]
-        flat, classes, x_first = gathered[4].astype(F32), cls_index, x_in[0]
-    weights = gathered[:4]
-    small = split_small(flat, width, slices)
-    segr, segc = segs[:, None, :], segs[:, :, None]
+        extra = ((0, 0), (0, rows - length), (0, 0))
+        x_in, g_in = jnp.pad(inputs, extra), jnp.pad(out_grad, extra)
+        gathered = [lax.all_gather(m[0].astype(BF), "dp", axis=0, tiled=True) for m in masters]
+        weights, x_first = gathered[:4], x_in[0]
+        small = split_small(gathered[4].astype(F32), width, slices)
 
     x, a, qkv, lse, o, h, a2, gp, u, acts, acts_early = run_forward(
-        line, length, turned, x_first, x_in, segr, segc, classes, weights, small)
+        line, length, turned, x_first, x_in, words, weights, small)
     acts, gin_early, g, dz, f, r, gin, sums = run_backward(
-        line, length, turned, acts, g_in, x, qkv, lse, h, gp, segr, segc, classes, weights, small)
-    small_total = join_small(sums, total, slices)
+        line, length, turned, acts, g_in, x, qkv, lse, h, gp, words, weights, small)
+    results = []
     if turned:
-        table = jnp.pad(small_total.reshape(slices, lanes, 128), ((0, 0), (0, 16 - lanes), (0, 0)))
-        *shards, gin, tally = run_scatter([a, r, o, f, a2, dz, u, g], table.reshape(slices * 16, 128), gin)
-        shards[4] = shards[4][:lanes].reshape(-1)
-        shards = [s.astype(F32)[None] for s in shards]
-        grad_norm = jnp.sqrt(jnp.sum(tally))
-        upper = lax.axis_index("section") >= 2
-        early = lax.broadcasted_iota(jnp.int32, (seq_dev, 1, 1), 0) < seq_dev - 1
-        acts = jnp.where(early & upper, acts_early, acts)
-        gin = jnp.where(early & jnp.logical_not(upper), gin_early, gin)
+        matrix_states = [v[0] for group in (masters, firsts, seconds) for v in group[:4]]
+        *shards, table, gin, norm = run_scatter([a, r, o, f, a2, dz, u, g], sums, gin)
+        *matrices, acts, gin = run_finish(norm, shards, matrix_states, [acts_early, acts, gin_early, gin], length)
+        results = [v[None] for v in matrices]
+        grad_norm = norm[0, 0]
+        ups = (share - 8 * eighth) // 128
+        small_share = jnp.concatenate([table[:8, :eighth].reshape(-1), table[8 : 8 + ups].reshape(-1)])[None]
+        factor = 1.0 / jnp.maximum(grad_norm, 1.0)
+        results += adam(small_share * factor, masters[4], firsts[4], seconds[4], small_rate, 0.0)
     else:
+        acts, gin = acts[:, :length], gin[:, :length]
         totals = [weight_grad(a, r).astype(BF), weight_grad(o, f).astype(BF), weight_grad(a2, dz).astype(BF),
-                  weight_grad(u, g).astype(BF), small_total]
+                  weight_grad(u, g).astype(BF), join_small(sums, total, slices)]
         shards = [lax.psum_scatter(t[None], "dp", scatter_dimension=1, tiled=True).astype(F32) for t in totals]
         squares = jnp.sum(jnp.stack([jnp.sum(s * s) for s in shards]))
         grad_norm = jnp.sqrt(lax.psum(squares, ("dp", "section")))
-    factor = 1.0 / jnp.maximum(grad_norm, 1.0)
-    fix = 1.0 - 0.5**STEP
-    results = []
-    for kind in range(5):
-        grad = shards[kind] * factor
-        first = 0.5 * firsts[kind] + 0.5 * grad
-        second = 0.5 * seconds[kind] + 0.5 * grad * grad
-        update = first / fix / (jnp.sqrt(second / fix) + adam_eps)
-        rate = small_rate
-        if kind < 4:
-            update = update + decay_rate * masters[kind]
-            rate = learn_rate
-        results += [grad, masters[kind] - rate * update, first, second]
-    return (acts[:, :length][None], gin[:, :length][None], grad_norm.reshape(1)) + tuple(results)
+        factor = 1.0 / jnp.maximum(grad_norm, 1.0)
+        for kind in range(5):
+            rate, decay = (learn_rate, decay_rate) if kind < 4 else (small_rate, 0.0)
+            results += adam(shards[kind] * factor, masters[kind], firsts[kind], seconds[kind], rate, decay)
+    return (acts[None], gin[None], grad_norm.reshape(1)) + tuple(results)
 
 
 def solution(mesh):

time: 496 us -> 436 us (0.88); the launches traced: 489 us -> 435 us
  other arithmetic: 25.5 us -> 3.39 us
  Pallas kernels: 446 us -> 427 us
  local copies, waits for them, and re-layouts: 14 us -> 3.56 us
    pallas_call x1, Pallas kernels: 177 us -> 156 us  [run_backward(): pl.pallas_call(functools.partial(backward_kernel, line, length, turned),...]
    pallas_call x0 -> x1, Pallas kernels: none -> 12.8 us  [run_finish(): pl.pallas_call(functools.partial(finish_kernel, (1, 0, 2, 3), micro), out...]
    sub x5 -> x1, other arithmetic: 10.5 us -> 0.64 us  [adam(): return [grad, master - rate * update, first, second]]
    pallas_call x1, Pallas kernels: 121 us -> 114 us  [run_scatter(): pl.pallas_call(functools.partial(scatter_kernel, pieces, micro), out_shap...]
where the time goes in v4:
time: 436 us; the launch traced here: 435 us
  Pallas kernels  427 us (98%)
    pallas_call x1, Pallas kernels, run_backward(): pl.pallas_call(functools.partial(backward_kernel, line, length, turned),...  156 us
    pallas_call x1, Pallas kernels, run_scatter(): pl.pallas_call(functools.partial(scatter_kernel, pieces, micro), out_shap...  114 us
    pallas_call x1, Pallas kernels, run_gather(): pl.pallas_call(functools.partial(gather_kernel, pieces, micro), out_shape...  95.8 us
    pallas_call x1, Pallas kernels, run_forward(): pl.pallas_call(functools.partial(forward_kernel, line, length, turned), o...  48.3 us
    pallas_call x1, Pallas kernels, run_finish(): pl.pallas_call(functools.partial(finish_kernel, (1, 0, 2, 3), micro), out...  12.8 us

profile of v4, /device:TPU:0, one launch (start us, length us, event | category | flops | bytes accessed | tf_op | source)
XLA Modules:
  0.0 435.1 jit_solution(1368299613483758662)
XLA Ops:
  0.7 0.7 pad.17.clone
  1.4 0.1 pad.20.clone
  1.5 0.7 convert_element_type.14
  2.2 0.1 slice.28
  2.3 0.7 maximum_maximum_fusion.refs_4_
  3.0 1.4 select_add_fusion.refs_7_
  4.3 95.8 %gather_layers.1 = (bf16[768,2304]{1,0:T(8,128)(2,1)}, bf16[768,768]{1,0:T(8,128)(2,1)}, bf16[768,3072]{1,0:T(8,128)(2,1)}, bf16[3072,768]{1,0:T(8,128)(2,1)}, f...) custom-call(f32[96,2304]{1,0:T(8,128)} %bitcast.54, ...), custom_call_target="tpu_custom_call" | custom-call | tf_op jit(solution)/shard_map/gather_layers/pallas_call | solution.py:883
  100.2 48.3 %forward_line.1 = (bf16[4,256,768]{2,1,0:T(8,128)(2,1)}, bf16[4,256,768]{2,1,0:T(8,128)(2,1)}, bf16[4,256,2304]{2,1,0:T(8,128)(2,1)}, f32[4,16,256]{2,1,0:T(8,12...) custom-call(bf16[256,768]{1,0:T(8,128)(2,1)} %get-tuple-element.76.x, ...), custom_call_target="tpu_custom_call" | custom-call | tf_op jit(solution)/shard_map/forward_line/pallas_call | solution.py:662
  148.5 156.0 %backward_line.1 = (bf16[4,256,768]{2,1,0:T(8,128)(2,1)}, bf16[4,256,768]{2,1,0:T(8,128)(2,1)}, bf16[4,256,768]{2,1,0:T(8,128)(2,1)}, bf16[4,256,3072]{2,1,0:T(8...) custom-call(bf16[4,256,768]{2,1,0:T(8,128)(2,1)} %get-tuple-element., ...), custom_call_target="tpu_custom_call" | custom-call | tf_op jit(solution)/shard_map/backward_line/pallas_call | solution.py:685
  304.5 0.0 copy-start
  304.5 0.0 copy-start.1
  304.5 0.0 copy-start.2
  304.6 113.6 %scatter_layers.1 = (bf16[96,2304]{1,0:T(8,128)(2,1)}, bf16[96,768]{1,0:T(8,128)(2,1)}, bf16[96,3072]{1,0:T(8,128)(2,1)}, bf16[384,768]{1,0:T(8,128)(2,1)}, f32[...) custom-call(bf16[1024,768]{1,0:T(8,128)(2,1)} %bitcast.56, bf16[1024,2304]{1,0:T(8,128)(2,1)} %bitcast.53, ...), custom_call_target="tpu_custom_call" | custom-call | tf_op jit(solution)/shard_map/scatter_layers/pallas_call | solution.py:1164
  418.1 1.2 slice.32
  420.0 0.7 slice_bitcast_fusion
  420.7 0.7 slice.33
  421.4 0.1 concatenate.30
  421.4 0.0 copy-done
  421.4 0.0 copy-done.1
  421.4 0.0 copy-done.2
  421.5 0.6 multiply_subtract_fusion
  422.1 12.8 %finish.1 = (f32[96,2304]{1,0:T(8,128)}, f32[96,2304]{1,0:T(8,128)}, f32[96,2304]{1,0:T(8,128)}, f32[96,2304]{1,0:T(8,128)}, f32[96,768]{1,0:T(8,128)}, /*index=...) custom-call(f32[8,128]{1,0:T(8,128)} %get-tuple-element.101.norm, ...), custom_call_target="tpu_custom_call" | custom-call | tf_op jit(solution)/shard_map/finish/pallas_call | solution.py:1249
  (5 shorter events, 0.1 us)
Async XLA Ops:
  304.5 116.9 %copy-start = (f32[1,1152]{1,0:T(1,128)S(1)}, f32[1,1152]{1,0:T(1,128)}, u32[]{:S(2)}) copy-start(f32[1,1152]{1,0:T(1,128)} %param.27) | copy-start | bytes 13828
  304.5 116.9 %copy-start.1 = (f32[1,1152]{1,0:T(1,128)S(1)}, f32[1,1152]{1,0:T(1,128)}, u32[]{:S(2)}) copy-start(f32[1,1152]{1,0:T(1,128)} %param.32) | copy-start | bytes 13828
  304.5 116.9 %copy-start.2 = (f32[1,1152]{1,0:T(1,128)S(1)}, f32[1,1152]{1,0:T(1,128)}, u32[]{:S(2)}) copy-start(f32[1,1152]{1,0:T(1,128)} %param.37) | copy-start | bytes 13828

commit v5 on v4

--- a/solution.py
+++ b/solution.py
@@ -13,6 +13,8 @@
 BF = jnp.bfloat16
 MESH = pl.DeviceIdType.MESH
 VMEM_CAP = 60 * 1024 * 1024
+EARLY = 3
+FIRST = 2
 
 norm_eps = 1e-06
 masked_score = -1e30
@@ -95,7 +97,7 @@
 
 
 def layer_forward(x_ref, bias_ref, wqkv, wproj, wup, wdown, small, a_ref, qkv_ref, lse_ref, o_ref,
-                  h_ref, a2_ref, gp_ref, u_ref, out_ref, ot_ref, before_up):
+                  h_ref, a2_ref, gp_ref, u_ref, out_ref, ot_ref, before):
     rows, width = x_ref.shape
     hidden = wup.shape[1]
     normed, _ = norm_parts(x_ref[...].astype(F32))
@@ -133,11 +135,12 @@
             mixed = mm(vt[head % 2 * 64 : head % 2 * 64 + 64, :], raised.pop(head)) * inverse.pop(head)
             ot_ref[head * 64 : head * 64 + 64, :] = mixed.astype(BF)
     o_ref[...] = ot_ref[...].T
+    before(1)
     h = x_ref[...].astype(F32) + (mm(o_ref[...], wproj[...]) + small[4:5, :])
     h_ref[...] = h
     normed, _ = norm_parts(h)
     a2_ref[...] = (normed * small[5:6, :] + small[6:7, :]).astype(BF)
-    before_up()
+    before(2)
     chunk = width
     z = {}
     for step in range(hidden // chunk + 1):
@@ -151,12 +154,13 @@
             u, slope = gelu_parts(z.pop(part))
             u_ref[:, cols] = u.astype(BF)
             gp_ref[:, cols] = slope.astype(BF)
+    before(3)
     total = mm(u_ref[...], wdown[...])
     out_ref[...] = (h_ref[...] + (total + small[7:8, :])).astype(BF)
 
 
 def layer_backward(g_ref, x_ref, bias_ref, qkv_ref, lse_ref, h_ref, gp_ref, wqkv, wproj, wup, wdown,
-                   small, dz_ref, f_ref, r_ref, gin_ref, sums_ref, do_ref, dh_ref, dqt_ref):
+                   small, dz_ref, f_ref, r_ref, gin_ref, sums_ref, do_ref, dh_ref, dqt_ref, before):
     rows, width = x_ref.shape
     hidden = wup.shape[1]
     carried = g_ref[...].astype(F32)
@@ -171,6 +175,7 @@
             dz = (back.pop(part) * gp_ref[:, cols].astype(F32)).astype(BF)
             dz_ref[:, cols] = dz
             sums_ref[8 + part : 9 + part, :] += column_sum(dz.astype(F32))
+    before(1)
     back = mm_nt(dz_ref[...], wup[...])
     normed, inv = norm_parts(h_ref[...])
     sums_ref[5:6, :] += column_sum(back * normed)
@@ -180,6 +185,7 @@
     f = dh.astype(BF)
     f_ref[...] = f
     sums_ref[4:5, :] += column_sum(f.astype(F32))
+    before(2)
     do_ref[...] = mm_nt(f_ref[...], wproj[...]).astype(BF)
     lane = lax.broadcasted_iota(jnp.int32, (rows, 128), 1)
     scores, grads, probs, slopes, dks, dvs = {}, {}, {}, {}, {}, {}
@@ -215,6 +221,7 @@
     r_ref[:, 0:width] = dqt_ref[...].T
     sums_ref[2:3, :] += column_sum(r_ref[:, 0:width].astype(F32))
     sums_ref[3:4, :] += column_sum(r_ref[:, 2 * width :].astype(F32))
+    before(3)
     back = mm_nt(r_ref[...], wqkv[...])
     normed, inv = norm_parts(x_ref[...].astype(F32))
     sums_ref[0:1, :] += column_sum(back * normed)
@@ -269,6 +276,12 @@
     def feeder(self, core):
         return Spot(self.x, self.y, 2 * self.c + self.y, core)
 
+    def gives_down(self):
+        return self.back().z < self.z
+
+    def takes_down(self):
+        return self.z < self.section()
+
     def crosses(self):
         return (self.z + self.c) % 2 == 1
 
@@ -289,6 +302,26 @@
 
 def hail(spot):
     pl.semaphore_signal(pltpu.get_barrier_semaphore(), inc=1, device_id=spot.id(), device_id_type=MESH)
+
+
+def hail_stagger(me, leading, by):
+    waits = (me.z == leading) & (me.c == 1)
+    tells = (me.z == leading + by) & (me.c == 0)
+    pl.when(waits)(lambda: hail(Spot(me.x, me.y, me.z + by, 0)))
+    pl.when(tells)(lambda: hail(Spot(me.x, me.y, me.z - by, 1)))
+    return jnp.where(waits, 1, 0) + jnp.where(tells, 1, 0)
+
+
+def tell_stagger(me, leading, by, token, m):
+    @pl.when((me.z == leading + by) & (me.c == 0) & (m == 0))
+    def _():
+        pl.semaphore_signal(token, inc=1, device_id=Spot(me.x, me.y, me.z - by, 1).id(), device_id_type=MESH)
+
+
+def wait_stagger(me, leading, token, m):
+    @pl.when((me.z == leading) & (me.c == 1) & (m == 0))
+    def _():
+        pl.semaphore_wait(token, 1)
 
 
 def hail_feeding(me, stage, core):
@@ -323,22 +356,23 @@
 
         expected = expected + jnp.where(alone, 0, 2)
         if feeding:
-            expected = expected + hail_feeding(me, 0, 0)
+            expected = expected + hail_feeding(me, 0, 0) + hail_stagger(me, 0, 1)
+        else:
+            expected = expected + hail_stagger(me, line.count - 1, -1)
     pl.semaphore_wait(barrier, expected)
 
 
 def forward_kernel(line, length, turned, x_first, x_in, words, wqkv_h, wproj_h, wup_h, wdown_h, small_in,
                    x_o, a_o, qkv_o, lse_o, o_o, h_o, a2_o, gp_o, u_o, acts_o, home_o,
                    wqkv, wproj, wup, wdown, xs, outs, a, qkv, lse, o, h, a2, gp, u, bias, ot, small,
-                   w_sem, in_sem, x_sem, save_sem, act_sem, send_sem, recv_sem, home_sem):
+                   w_sem, in_sem, x_sem, save_sem, act_sem, send_sem, recv_sem, home_sem, token):
     micro = xs.shape[0]
     stage = line.stage()
     loads = [
         pltpu.make_async_copy(src, dst, w_sem.at[i])
         for i, (src, dst) in enumerate(((wqkv_h, wqkv), (wproj_h, wproj), (wup_h, wup), (wdown_h, wdown)))
     ]
-    for load in loads:
-        load.start()
+    loads[0].start()
 
     def first_in(m):
         return pltpu.make_async_copy(x_in.at[m], xs.at[m], in_sem.at[m])
@@ -351,7 +385,6 @@
     if turned:
         me = Spot.here()
         back = me.back()
-        alone = same(me, back)
 
         def turn_in(m):
             return pltpu.make_async_remote_copy(
@@ -361,23 +394,19 @@
         taker, feeder = me.fed_at(0), me.feeder(0)
         feeds = me.feeds(0, 0) & jnp.logical_not(same(me, taker))
         feeds_self = me.feeds(0, 0) & same(me, taker)
-        homing = jnp.logical_and(stage >= 2, jnp.logical_not(alone))
-        homed = jnp.logical_and(me.section() >= 2, jnp.logical_not(alone))
-        settled = jnp.logical_and(stage >= 2, alone)
+        homing, homed = me.gives_down(), me.takes_down()
 
         def home(m):
             return pltpu.make_async_remote_copy(
                 src_ref=outs.at[m], dst_ref=home_o.at[m], send_sem=home_sem.at[0, m], recv_sem=home_sem.at[1, m],
                 device_id=back.id(), device_id_type=MESH)
 
-        def settle(m):
-            return pltpu.make_async_copy(outs.at[m], home_o.at[m], home_sem.at[0, m])
-
         @pl.when(stage == 0)
         def _():
-            pltpu.make_async_copy(x_first, xs.at[0], in_sem.at[0]).start()
-
-        for m in range(1, micro):
+            for m in range(FIRST):
+                pltpu.make_async_copy(x_first.at[m], xs.at[m], in_sem.at[m]).start()
+
+        for m in range(FIRST, micro):
             @pl.when(feeds)
             def _():
                 turn_in(m).start()
@@ -391,6 +420,10 @@
             for m in range(micro):
                 first_in(m).start()
 
+    loads[0].wait()
+    for load in loads[1:]:
+        load.start()
+
     saved = ((a, a_o), (qkv, qkv_o), (lse, lse_o), (o, o_o), (h, h_o), (a2, a2_o), (gp, gp_o), (u, u_o))
 
     def saves(m, slot):
@@ -408,7 +441,7 @@
         slot = lax.rem(m, 2)
 
         if turned:
-            here = jnp.logical_or(feeds_self, jnp.logical_and(stage == 0, m == 0))
+            here = jnp.logical_or(feeds_self, jnp.logical_and(stage == 0, m < FIRST))
         else:
             here = stage == 0
 
@@ -420,6 +453,8 @@
         def _():
             hop(m).wait_recv()
 
+        if turned:
+            tell_stagger(me, 0, 1, token, m)
         pltpu.make_async_copy(xs.at[m], x_o.at[m], x_sem.at[m]).start()
 
         @pl.when(m >= 2)
@@ -427,22 +462,19 @@
             for save in saves(m - 2, slot):
                 save.wait()
 
-        @pl.when(m == 0)
-        def _():
-            loads[0].wait()
-            loads[1].wait()
-
         bias[...] = micro_bias(words, m, micro, length)
 
-        def before_up():
+        def before(i):
             @pl.when(m == 0)
             def _():
-                loads[2].wait()
-                loads[3].wait()
+                loads[i].wait()
 
         layer_forward(xs.at[m], bias, wqkv, wproj, wup, wdown, small, a.at[slot], qkv.at[slot],
                       lse.at[slot], o.at[slot], h.at[slot], a2.at[slot], gp.at[slot], u.at[slot],
-                      outs.at[m], ot, before_up)
+                      outs.at[m], ot, before)
+
+        if turned:
+            wait_stagger(me, 0, token, m)
 
         @pl.when(stage < line.count - 1)
         def _():
@@ -452,8 +484,7 @@
             save.start()
         pltpu.make_async_copy(outs.at[m], acts_o.at[m], act_sem.at[m]).start()
         if turned:
-            pl.when(homing & (m < micro - 1))(lambda: home(m).start())
-            pl.when(settled & (m < micro - 1))(lambda: settle(m).start())
+            pl.when(homing & (m < EARLY))(lambda: home(m).start())
         return carry
 
     lax.fori_loop(0, micro, step, 0)
@@ -473,20 +504,19 @@
     if turned:
         @pl.when(feeds)
         def _():
-            for m in range(1, micro):
+            for m in range(FIRST, micro):
                 turn_in(m).wait_send()
 
-        for m in range(micro - 1):
+        for m in range(EARLY):
             pl.when(homing)(lambda: home(m).wait_send())
             pl.when(homed)(lambda: home(m).wait_recv())
-            pl.when(settled)(lambda: settle(m).wait())
 
 
 def backward_kernel(line, length, turned, acts_h, g_in, x_h, qkv_h, lse_h, h_h, gp_h, words,
                     wqkv_h, wproj_h, wup_h, wdown_h, small_in,
                     acts_o, home_o, g_o, dz_o, f_o, r_o, gin_o, sums_out,
                     wqkv, wproj, wup, wdown, gs, gins, x, qkv, lse, h, gp, dz, f, r, bias, do, dh, dqt, small, sums_o,
-                    w_sem, in_sem, g_sem, load_sem, save_sem, act_sem, send_sem, recv_sem, home_sem, back_sem):
+                    w_sem, in_sem, g_sem, load_sem, save_sem, act_sem, send_sem, recv_sem, home_sem, back_sem, token):
     micro = gs.shape[0]
     stage = line.stage()
     loads = [
@@ -511,10 +541,7 @@
         ]
 
     loads[0].start()
-    for fetch in fetches(0, 0):
-        fetch.start()
-    for load in loads[1:]:
-        load.start()
+    fetches(0, 0)[0].start()
     sums_o[...] = jnp.zeros_like(sums_o)
     if turned:
         spread_small(small_in, small)
@@ -535,7 +562,7 @@
             return pltpu.make_async_copy(acts_h.at[m], acts_o.at[m], home_sem.at[0, m])
 
         pairs = jnp.logical_not(alone)
-        low, low_home = stage < 2, me.section() < 2
+        low, low_home = jnp.logical_not(me.gives_down()), jnp.logical_not(me.takes_down())
 
         def home_back(m):
             return pltpu.make_async_remote_copy(
@@ -546,13 +573,18 @@
             return pltpu.make_async_copy(gins.at[m], home_o.at[m], back_sem.at[0, m])
 
         for m in range(micro):
-            now = low | (m == micro - 1)
+            now = low | (m >= EARLY)
             pl.when(alone & now)(lambda: stay(m).start())
             pl.when(pairs & now)(lambda: home(m).start())
     else:
         for m in range(micro):
             pltpu.make_async_copy(acts_h.at[m], acts_o.at[m], home_sem.at[0, m]).start()
 
+    loads[0].wait()
+    for load, some in zip(loads[1:], ((1,), (2, 3), (4,))):
+        for i in some:
+            fetches(0, 0)[i].start()
+        load.start()
     saved = ((dz, dz_o), (f, f_o), (r, r_o))
 
     def saves(m, slot):
@@ -574,13 +606,15 @@
             for fetch in fetches(m + 1, 1 - slot):
                 fetch.start()
 
-        @pl.when(m == 0)
-        def _():
-            for load in loads:
-                load.wait()
-
-        for fetch in fetches(m, slot):
-            fetch.wait()
+        def before(i):
+            @pl.when(m == 0)
+            def _():
+                loads[i].wait()
+
+            for at in ((), (1,), (2, 3), (4,))[i]:
+                fetches(m, slot)[at].wait()
+
+        fetches(m, slot)[0].wait()
         bias[...] = micro_bias(words, m, micro, length)
 
         @pl.when(m >= 2)
@@ -596,10 +630,15 @@
         def _():
             hop(m).wait_recv()
 
+        if turned:
+            tell_stagger(me, line.count - 1, -1, token, m)
         pltpu.make_async_copy(gs.at[m], g_o.at[m], g_sem.at[m]).start()
         layer_backward(gs.at[m], x.at[slot], bias, qkv.at[slot], lse.at[slot], h.at[slot], gp.at[slot],
                        wqkv, wproj, wup, wdown, small, dz.at[slot], f.at[slot], r.at[slot], gins.at[m],
-                       sums_o, do, dh, dqt)
+                       sums_o, do, dh, dqt, before)
+
+        if turned:
+            wait_stagger(me, line.count - 1, token, m)
 
         @pl.when(stage > 0)
         def _():
@@ -633,7 +672,7 @@
 
     for m in range(micro):
         if turned:
-            now, then = low | (m == micro - 1), low_home | (m == micro - 1)
+            now, then = low | (m >= EARLY), low_home | (m >= EARLY)
             pl.when(alone & now)(lambda: stay(m).wait())
             pl.when(pairs & now)(lambda: home(m).wait_send())
             pl.when(pairs & then)(lambda: home(m).wait_recv())
@@ -669,7 +708,7 @@
         + [pltpu.VMEM((2,) + s, t) for s, t in saved]
         + [pltpu.VMEM((rows, rows), F32), pltpu.VMEM((width, rows), BF), pltpu.VMEM((16, width), F32)]
         + [DMA((4,)), DMA((micro,)), DMA((micro,)), DMA((2, 8)), DMA((micro,)), DMA((micro,)), DMA((micro,)),
-           DMA((2, micro))],
+           DMA((2, micro)), pltpu.SemaphoreType.REGULAR],
         compiler_params=pltpu.CompilerParams(
             collective_id=0, has_side_effects=True, vmem_limit_bytes=VMEM_CAP),
         name="forward_line",
@@ -696,7 +735,7 @@
            pltpu.VMEM((rows, rows), F32), pltpu.VMEM((rows, width), BF), pltpu.VMEM((rows, width), F32),
            pltpu.VMEM((width, rows), BF), pltpu.VMEM((16, width), F32), pltpu.VMEM((16, width), F32)]
         + [DMA((4,)), DMA((micro,)), DMA((micro,)), DMA((2, 5)), DMA((2, 3)), DMA((micro,)), DMA((micro,)),
-           DMA((micro,)), DMA((2, micro)), DMA((2, micro))],
+           DMA((micro,)), DMA((2, micro)), DMA((2, micro)), pltpu.SemaphoreType.REGULAR],
         compiler_params=pltpu.CompilerParams(
             collective_id=1, has_side_effects=True, vmem_limit_bytes=VMEM_CAP),
         name="backward_line",
@@ -709,12 +748,12 @@
 
 def gather_kernel(pieces, micro, *refs):
     count = 5
-    masters, (x_in, g_in, seg_in) = refs[:count], refs[count : count + 3]
-    wholes, (x_o, x_all, g_o, seg_o) = refs[count + 3 : 2 * count + 3], refs[2 * count + 3 : 2 * count + 7]
-    refs = refs[2 * count + 7 :]
-    swap, wide, narrow, (x_raw, g_raw, x_pad, g_pad) = refs[:5], refs[5:9], refs[9:13], refs[13:17]
-    send, recv, local, turn_send, turn_recv, load_sem = refs[17:]
-    shares = narrow + (masters[4],)
+    masters, (x_in, g_in, seg_in, cls_in) = refs[:count], refs[count : count + 4]
+    wholes, (x_o, x_all, g_o, seg_o) = refs[count + 4 : 2 * count + 4], refs[2 * count + 4 : 2 * count + 8]
+    refs = refs[2 * count + 8 :]
+    swap, wide, narrow, (x_raw, g_raw, x_pad, g_pad, words, table) = refs[:5], refs[5:9], refs[9:13], refs[13:19]
+    send, recv, local, turn_send, turn_recv, load_sem = refs[19:]
+    shares = narrow + (table,)
     loads = [pltpu.make_async_copy(masters[i], wide[i], load_sem.at[i]) for i in range(4)]
     loads += [pltpu.make_async_copy(x_in, x_raw, load_sem.at[4]), pltpu.make_async_copy(g_in, g_raw, load_sem.at[5])]
     for i in (0, 1, 2, 3, 4, 5):
@@ -780,11 +819,11 @@
 
     own, own_x, own_y, own_d = parts(me)
     beside = parts(cn)
-    turns = [(x_pad.at[0], x_o), (seg_in, seg_o)] + [(g_pad.at[m], g_o.at[m]) for m in range(micro)]
-    gives = [me.feeds(0, 0), me.z >= 0] + [me.feeds(3, 1)] * micro
-    takes = [me.z == 0, me.z >= 0] + [me.z == 3] * micro
-    takers = [me.fed_at(0), ahead] + [me.fed_at(3)] * micro
-    givers = [me.feeder(0), back] + [me.feeder(1)] * micro
+    turns = [(words, seg_o)] + [(x_pad.at[m], x_o.at[m]) for m in range(FIRST)] + [(g_pad.at[m], g_o.at[m]) for m in range(micro)]
+    gives = [me.z >= 0] + [me.feeds(0, 0)] * FIRST + [me.feeds(3, 1)] * micro
+    takes = [me.z >= 0] + [me.z == 0] * FIRST + [me.z == 3] * micro
+    takers = [ahead] + [me.fed_at(0)] * FIRST + [me.fed_at(3)] * micro
+    givers = [back] + [me.feeder(0)] * FIRST + [me.feeder(1)] * micro
 
     def turn(i):
         return pltpu.make_async_remote_copy(
@@ -801,6 +840,18 @@
         pl.when(gives[i] & here)(lambda: pltpu.make_async_copy(*turns[i], turn_send.at[i]).wait())
         pl.when(gives[i] & jnp.logical_not(here))(lambda: turn(i).wait_send())
         pl.when(takes[i] & jnp.logical_not(same(me, givers[i])))(lambda: turn(i).wait_recv())
+
+    flat = masters[4][...].astype(BF).astype(F32)
+    share = flat.shape[1] // 12
+    table[...] = jnp.zeros_like(table)
+    for i in range(8):
+        table[i : i + 1, 0:share] = flat[:, i * share : (i + 1) * share]
+    for i in range(share // 32):
+        table[8 + i : 9 + i, :] = flat[:, 8 * share + 128 * i : 8 * share + 128 * (i + 1)]
+    words[...] = jnp.full_like(words, -1)
+    words[0:micro, 0 : seg_in.shape[1]] = seg_in[...]
+    for m in range(micro):
+        words[micro + m : micro + m + 1, :] = jnp.full((1, words.shape[1]), cls_in[m], jnp.int32)
 
     def pad(raw, padded):
         for m in range(micro):
@@ -822,10 +873,11 @@
         pl.when(stays)(lambda: kept(k).start())
         pl.when(direct)(lambda: brought(k, me.dp()).start())
         pl.when(crosses)(lambda: crossed(k).start())
-    turn_start(1)
+    turn_start(0)
     loads[4].wait()
     pad(x_raw, x_pad)
-    turn_start(0)
+    for i in range(FIRST):
+        turn_start(1 + i)
     x_save = pltpu.make_async_copy(x_pad, x_all, load_sem.at[4])
     x_save.start()
     loads[5].wait()
@@ -838,7 +890,7 @@
                 brought_on(k, me.dp()).start()
 
         if k == len(pieces) - 1:
-            for i in range(2, 2 + micro):
+            for i in range(1 + FIRST, 1 + FIRST + micro):
                 turn_start(i)
         b = k - 1
         if 0 <= b < len(pieces):
@@ -872,33 +924,37 @@
     x_save.wait()
 
 
-def run_gather(masters, inputs, g, words, rows):
+def run_gather(masters, inputs, g, segs, classes, rows):
     pieces = GATHER_PIECES
     micro, _, width = g.shape
     shape = jax.ShapeDtypeStruct
-    shares = [shape(m.shape, BF) for m in masters[:4]] + [shape(masters[4].shape, F32)]
+    shares = [shape(m.shape, BF) for m in masters[:4]] + [shape((16, 128), F32)]
     many = shape((micro, rows, width), BF)
     outs = [shape((s.shape[0] * 8,) + s.shape[1:], s.dtype) for s in shares]
-    outs += [shape((rows, width), BF), many, many, shape(words.shape, words.dtype)]
+    outs += [shape((FIRST, rows, width), BF), many, many, shape((2 * micro, rows), segs.dtype)]
     return pl.pallas_call(
         functools.partial(gather_kernel, pieces, micro),
         out_shape=outs,
-        in_specs=[ANYWHERE] * 8,
+        in_specs=[ANYWHERE] * 4 + [IN_VMEM] + [ANYWHERE] * 2 + [IN_VMEM, IN_SMEM],
         out_specs=[ANYWHERE] * 9,
         scratch_shapes=[pltpu.VMEM(s.shape, s.dtype) for s in shares] + [pltpu.VMEM(m.shape, F32) for m in masters[:4]]
         + [pltpu.VMEM(s.shape, BF) for s in shares[:4]] + [pltpu.VMEM(g.shape, BF)] * 2
         + [pltpu.VMEM((micro, rows, width), BF)] * 2
-        + [DMA((9, len(pieces))), DMA((9, len(pieces))), DMA((len(pieces),)), DMA((2 + micro,)), DMA((2 + micro,)),
-           DMA((6,))],
+        + [pltpu.VMEM((2 * micro, rows), segs.dtype), pltpu.VMEM((16, 128), F32)]
+        + [DMA((9, len(pieces))), DMA((9, len(pieces))), DMA((len(pieces),)), DMA((1 + FIRST + micro,)),
+           DMA((1 + FIRST + micro,)), DMA((6,))],
         compiler_params=pltpu.CompilerParams(collective_id=2, has_side_effects=True, vmem_limit_bytes=VMEM_CAP),
         name="gather_layers",
-    )(*masters, inputs, g, words)
+    )(*masters, inputs, g, segs, classes)
 
 
 SCATTER_PIECES = ((3, 0, 128, 0, 768, "x"), (3, 128, 128, 0, 768, "x"), (3, 256, 128, 0, 768, "x"),
                   (2, 0, 96, 0, 1024, "x"), (2, 0, 96, 1024, 1024, "x"), (2, 0, 96, 2048, 1024, "x"),
                   (0, 0, 96, 0, 768, "x"), (0, 0, 96, 768, 768, "x"), (0, 0, 96, 1536, 768, "x"),
                   (1, 0, 96, 0, 768, "x"), (4, 0, 16, 0, 128, "x"))
+
+
+SCATTER_LAGS = (1, 3, 4, 5)
 
 
 def scatter_kernel(pieces, micro, *refs):
@@ -921,6 +977,11 @@
     resting = (g_h, a2_h, a_h, o_h)
     rest_at = {3: 0, 2: 1, 0: 2, 1: 3}
 
+    openers = {}
+    for k in reversed(range(len(pieces))):
+        openers[pieces[k][0]] = k
+    opened = sorted((k, array) for array, k in openers.items() if array < 4)
+
     def streamed(k):
         array, first, size, column_at, columns, _ = pieces[k]
         slot = k % 2
@@ -939,11 +1000,11 @@
 
     for copy in streamed(0):
         copy.start()
-    rested(0).start()
+    rested(rest_at[opened[0][1]]).start()
     for copy in streamed(1):
         copy.start()
-    for i in range(1, 4):
-        rested(i).start()
+    for _, array in opened[1:]:
+        rested(rest_at[array]).start()
     for spot in slab + column:
         hail(spot)
 
@@ -963,9 +1024,9 @@
         for copy in streamed(k):
             copy.wait()
         if array == 4:
-            return
-        if array == 3:
-            if first == 0:
+            pass
+        elif array == 3:
+            if k == openers[3]:
                 rested(rest_at[3]).wait()
             share = totals[3].shape[0] // 8
             for p in range(0, 8, 2):
@@ -974,7 +1035,7 @@
                 for i in range(2):
                     totals[3][(p + i) * share + first : (p + i) * share + first + size, :] = both[i * size : (i + 1) * size]
         else:
-            if column_at == 0:
+            if k == openers[array]:
                 rested(rest_at[array]).wait()
                 flipped[...] = fixed[rest_at[array]].T
             for c in range(0, columns, 256):
@@ -1044,17 +1105,17 @@
     work(0)
     pl.semaphore_wait(pltpu.get_barrier_semaphore(), 10 + jnp.where(stays, 0, 2) + jnp.where(alone, 0, 2))
     for m in range(micro):
-        now = (me.z >= 2) | (m == micro - 1)
+        now = me.gives_down() | (m == micro - 1)
         pl.when(alone & now)(lambda: turn_stay(m).start())
         pl.when(pairs & now)(lambda: turn(m).start())
     tally = jnp.zeros((8, 128), F32)
-    for k in range(len(pieces) + 4):
+    for k in range(len(pieces) + SCATTER_LAGS[3]):
         if k < len(pieces):
             if k > 0:
                 work(k)
             for j in (3, 2, 1, 0):
                 crossed(k, j).start()
-        b = k - 1
+        b = k - SCATTER_LAGS[0]
         if 0 <= b < len(pieces):
             turn_x = (me.c == 0) if pieces[b][5] == "c" else (me.c < 0)
             for j in (3, 2, 1, 0):
@@ -1067,7 +1128,7 @@
                     pl.when(turn_x)(lambda: to_y(b).start())
                 if j == 1:
                     pl.when(jnp.logical_not(turn_x))(lambda: to_x(b).start())
-        b = k - 2
+        b = k - SCATTER_LAGS[1]
         if 0 <= b < len(pieces):
             to_diag(b, yn).wait_recv()
             turn_x = (me.c == 0) if pieces[b][5] == "c" else (me.c < 0)
@@ -1081,7 +1142,7 @@
             def _():
                 add(b, 2, of(diag, b)[...])
                 to_y(b).start()
-        b = k - 3
+        b = k - SCATTER_LAGS[2]
         if 0 <= b < len(pieces):
             to_x(b).wait_recv()
             to_y(b).wait_recv()
@@ -1094,7 +1155,7 @@
             pl.when(stays)(lambda: stay_home(b).start())
             pl.when(moves & jnp.logical_not(target_crosses))(lambda: to_home(b).start())
             pl.when(target_crosses)(lambda: to_swap(b).start())
-        b = k - 4
+        b = k - SCATTER_LAGS[3]
         if 0 <= b < len(pieces):
             @pl.when(crosses)
             def _():
@@ -1143,7 +1204,7 @@
         pl.when(moves)(lambda: to_home(k).wait_send())
         pl.when(crosses)(lambda: over(k).wait_send())
     for m in range(micro):
-        now, then = (me.z >= 2) | (m == micro - 1), (me.section() >= 2) | (m == micro - 1)
+        now, then = me.gives_down() | (m == micro - 1), me.takes_down() | (m == micro - 1)
         pl.when(alone & now)(lambda: turn_stay(m).wait())
         pl.when(pairs & now)(lambda: turn(m).wait_send())
         pl.when(pairs & then)(lambda: turn(m).wait_recv())
@@ -1177,11 +1238,13 @@
 
 
 def finish_kernel(order, micro, norm, *refs):
+    table, small_state, refs = refs[0], refs[1:4], refs[4:]
     shards_h, state_h, (acts_early, acts_late, gin_early, gin_late) = refs[:4], refs[4:16], refs[16:20]
+    norm_o, small_o, refs = refs[20], refs[21:25], refs[5:]
     state_o, acts_o, gin_o = refs[20:36], refs[36], refs[37]
-    shards, state, (acts, gin, acts_cut, gin_cut) = refs[38:42], refs[42:58], refs[58:62]
-    load_sem, pick_sem, out_sem = refs[62:]
-    upper = lax.axis_index("section") >= 2
+    shards, state, (acts, gin, acts_cut, gin_cut, row) = refs[38:42], refs[42:58], refs[58:63]
+    load_sem, pick_sem, out_sem = refs[63:]
+    upper = Spot.here().takes_down()
 
     def loads(array):
         copies = [pltpu.make_async_copy(shards_h[array], shards[array], load_sem.at[array, 0])]
@@ -1201,7 +1264,7 @@
     for i, (early, late, dst, is_early) in enumerate(
             ((acts_early, acts_late, acts, upper), (gin_early, gin_late, gin, jnp.logical_not(upper)))):
         for m in range(micro):
-            if m == micro - 1:
+            if m >= (EARLY if i == 0 else micro - 1):
                 pick(i, m, late, dst).start()
             else:
                 pl.when(is_early)(lambda: pick(i, m, early, dst).start())
@@ -1209,6 +1272,19 @@
     factor = 1.0 / jnp.maximum(norm[0:1, 0:1], 1.0)
     fix = 1.0 / (1.0 - 0.5**STEP)
     strip = 16
+    norm_o[0] = norm[0, 0]
+    share = row.shape[1] // 12
+    for i in range(8):
+        row[:, i * share : (i + 1) * share] = table[i : i + 1, 0:share]
+    for i in range(share // 32):
+        row[:, 8 * share + 128 * i : 8 * share + 128 * (i + 1)] = table[8 + i : 9 + i, :]
+    grad = row[...] * factor
+    first_new = 0.5 * small_state[1][...] + 0.5 * grad
+    second_new = 0.5 * small_state[2][...] + 0.5 * grad * grad
+    small_o[0][...] = grad
+    small_o[1][...] = small_state[0][...] - small_rate * ((first_new * fix) / (jnp.sqrt(second_new * fix) + adam_eps))
+    small_o[2][...] = first_new
+    small_o[3][...] = second_new
     for array in order:
         for copy in loads(array):
             copy.wait()
@@ -1243,21 +1319,22 @@
         pltpu.make_async_copy(cut, out, out_sem.at[4, i]).wait()
 
 
-def run_finish(norm, shards, states, tall, length):
+def run_finish(norm, table, small_states, shards, states, tall, length):
     micro, rows, width = tall[0].shape
     shape = jax.ShapeDtypeStruct
     return pl.pallas_call(
         functools.partial(finish_kernel, (1, 0, 2, 3), micro),
-        out_shape=[shape(s.shape, F32) for s in shards for _ in range(4)] + [shape((micro, length, width), BF)] * 2,
-        in_specs=[IN_VMEM] + [ANYWHERE] * 20,
-        out_specs=[ANYWHERE] * 18,
+        out_shape=[shape((1,), F32)] + [shape(small_states[0].shape, F32)] * 4
+        + [shape(s.shape, F32) for s in shards for _ in range(4)] + [shape((micro, length, width), BF)] * 2,
+        in_specs=[IN_VMEM] * 5 + [ANYWHERE] * 20,
+        out_specs=[IN_SMEM] + [IN_VMEM] * 4 + [ANYWHERE] * 18,
         scratch_shapes=[pltpu.VMEM(s.shape, BF) for s in shards]
         + [pltpu.VMEM(s.shape, F32) for _ in range(4) for s in shards]
         + [pltpu.VMEM((micro, rows, width), BF)] * 2 + [pltpu.VMEM((micro, length, width), BF)] * 2
-        + [DMA((4, 4)), DMA((2, micro)), DMA((5, 4))],
+        + [pltpu.VMEM(small_states[0].shape, F32)] + [DMA((4, 4)), DMA((2, micro)), DMA((5, 4))],
         compiler_params=pltpu.CompilerParams(vmem_limit_bytes=VMEM_CAP),
         name="finish",
-    )(norm, *shards, *states, *tall)
+    )(norm, table, *small_states, *shards, *states, *tall)
 
 
 def split_small(small, width, slices):
@@ -1303,21 +1380,16 @@
     share = masters[4].shape[1]
     total = share * slices
 
-    segs = jnp.pad(segment_ids, ((0, 0), (0, rows - length)), constant_values=-1)
-    words = jnp.concatenate([segs, jnp.broadcast_to(cls_index[:, None], (seq_dev, rows))], axis=0)
     if turned:
         line = Line("dp", 4, 2)
-        eighth = width // slices
-        flat = masters[4][0].astype(BF).astype(F32)
-        small = jnp.concatenate([
-            jnp.pad(flat[: 8 * eighth].reshape(8, eighth), ((0, 0), (0, 128 - eighth))),
-            flat[8 * eighth :].reshape(-1, 128), jnp.zeros((8 - (share - 8 * eighth) // 128, 128), F32)], axis=0)
         *weights, small, x_first, x_in, g_in, words = run_gather(
-            [m[0] for m in masters[:4]] + [small], inputs, out_grad, words, rows)
+            [m[0] for m in masters[:4]] + [masters[4]], inputs, out_grad, segment_ids, cls_index, rows)
     else:
         line = Line("section", stages, 1)
         extra = ((0, 0), (0, rows - length), (0, 0))
         x_in, g_in = jnp.pad(inputs, extra), jnp.pad(out_grad, extra)
+        segs = jnp.pad(segment_ids, ((0, 0), (0, rows - length)), constant_values=-1)
+        words = jnp.concatenate([segs, jnp.broadcast_to(cls_index[:, None], (seq_dev, rows))], axis=0)
         gathered = [lax.all_gather(m[0].astype(BF), "dp", axis=0, tiled=True) for m in masters]
         weights, x_first = gathered[:4], x_in[0]
         small = split_small(gathered[4].astype(F32), width, slices)
@@ -1330,13 +1402,10 @@
     if turned:
         matrix_states = [v[0] for group in (masters, firsts, seconds) for v in group[:4]]
         *shards, table, gin, norm = run_scatter([a, r, o, f, a2, dz, u, g], sums, gin)
-        *matrices, acts, gin = run_finish(norm, shards, matrix_states, [acts_early, acts, gin_early, gin], length)
-        results = [v[None] for v in matrices]
-        grad_norm = norm[0, 0]
-        ups = (share - 8 * eighth) // 128
-        small_share = jnp.concatenate([table[:8, :eighth].reshape(-1), table[8 : 8 + ups].reshape(-1)])[None]
-        factor = 1.0 / jnp.maximum(grad_norm, 1.0)
-        results += adam(small_share * factor, masters[4], firsts[4], seconds[4], small_rate, 0.0)
+        grad_norm, *rest = run_finish(norm, table, [masters[4], firsts[4], seconds[4]], shards, matrix_states,
+                                      [acts_early, acts, gin_early, gin], length)
+        acts, gin = rest[20:]
+        results = [v[None] for v in rest[4:20]] + rest[:4]
     else:
         acts, gin = acts[:, :length], gin[:, :length]
         totals = [weight_grad(a, r).astype(BF), weight_grad(o, f).astype(BF), weight_grad(a2, dz).astype(BF),

time: 436 us -> 422 us (0.968); the launches traced: 435 us -> 414 us
  Pallas kernels: 427 us -> 413 us
    pallas_call x1, Pallas kernels: 156 us -> 142 us  [run_backward(): pl.pallas_call(functools.partial(backward_kernel, line, length, turned),...]
where the time goes in v5:
time: 422 us; the launch traced here: 414 us
  Pallas kernels  413 us (98%)
    pallas_call x1, Pallas kernels, run_backward(): pl.pallas_call(functools.partial(backward_kernel, line, length, turned),...  142 us
    pallas_call x1, Pallas kernels, run_scatter(): pl.pallas_call(functools.partial(scatter_kernel, pieces, micro), out_shap...  116 us
    pallas_call x1, Pallas kernels, run_gather(): pl.pallas_call(functools.partial(gather_kernel, pieces, micro), out_shape...  94.8 us
    pallas_call x1, Pallas kernels, run_forward(): pl.pallas_call(functools.partial(forward_kernel, line, length, turned), o...  46.3 us
    pallas_call x1, Pallas kernels, run_finish(): pl.pallas_call(functools.partial(finish_kernel, (1, 0, 2, 3), micro), out...  13.6 us

profile of v5, /device:TPU:0, one launch (start us, length us, event | category | flops | bytes accessed | tf_op | source)
XLA Modules:
  0.0 414.1 jit_solution(11463707467702323325)
XLA Ops:
  0.7 94.8 %gather_layers.1 = (bf16[768,2304]{1,0:T(8,128)(2,1)}, bf16[768,768]{1,0:T(8,128)(2,1)}, bf16[768,3072]{1,0:T(8,128)(2,1)}, bf16[3072,768]{1,0:T(8,128)(2,1)}, f...) custom-call(f32[96,2304]{1,0:T(8,128)} %bitcast.45, ...), custom_call_target="tpu_custom_call" | custom-call | tf_op jit(solution)/shard_map/gather_layers/pallas_call | solution.py:935
  95.5 46.3 %forward_line.1 = (bf16[4,256,768]{2,1,0:T(8,128)(2,1)}, bf16[4,256,768]{2,1,0:T(8,128)(2,1)}, bf16[4,256,2304]{2,1,0:T(8,128)(2,1)}, f32[4,16,256]{2,1,0:T(8,12...) custom-call(bf16[2,256,768]{2,1,0:T(8,128)(2,1)} %get-tuple-element., ...), custom_call_target="tpu_custom_call" | custom-call | tf_op jit(solution)/shard_map/forward_line/pallas_call | solution.py:701
  141.8 141.7 %backward_line.1 = (bf16[4,256,768]{2,1,0:T(8,128)(2,1)}, bf16[4,256,768]{2,1,0:T(8,128)(2,1)}, bf16[4,256,768]{2,1,0:T(8,128)(2,1)}, bf16[4,256,3072]{2,1,0:T(8...) custom-call(bf16[4,256,768]{2,1,0:T(8,128)(2,1)} %get-tuple-element., ...), custom_call_target="tpu_custom_call" | custom-call | tf_op jit(solution)/shard_map/backward_line/pallas_call | solution.py:724
  283.5 116.4 %scatter_layers.1 = (bf16[96,2304]{1,0:T(8,128)(2,1)}, bf16[96,768]{1,0:T(8,128)(2,1)}, bf16[96,3072]{1,0:T(8,128)(2,1)}, bf16[384,768]{1,0:T(8,128)(2,1)}, f32[...) custom-call(bf16[1024,768]{1,0:T(8,128)(2,1)} %bitcast.47, bf16[1024,2304]{1,0:T(8,128)(2,1)} %bitcast.40, ...), custom_call_target="tpu_custom_call" | custom-call | tf_op jit(solution)/shard_map/scatter_layers/pallas_call | solution.py:1225
  400.0 13.6 %finish.1 = (f32[1]{0:T(128)}, f32[1,1152]{1,0:T(1,128)}, f32[1,1152]{1,0:T(1,128)}, f32[1,1152]{1,0:T(1,128)}, f32[1,1152]{1,0:T(1,128)}, /*index=5*/f32[96,230...) custom-call(f32[8,128]{1,0:T(8,128)} %get-tuple-element.106.norm, ...), custom_call_target="tpu_custom_call" | custom-call | tf_op jit(solution)/shard_map/finish/pallas_call | solution.py:1325

commit v6 on v5

--- a/solution.py
+++ b/solution.py
@@ -282,6 +282,24 @@
     def takes_down(self):
         return self.z < self.section()
 
+    def gives_near(self):
+        return (self.z >= 2) & (self.back().z == self.z - 1)
+
+    def takes_near(self):
+        return (self.section() >= 2) & (self.z == self.section() - 1)
+
+    def yields(self):
+        return (self.y == 0) & (self.z >= 2) & (self.back().z == 0)
+
+    def carries(self):
+        return self.flip(y=1).yields()
+
+    def carrier(self):
+        return Spot(self.x, 1, self.section(), 0)
+
+    def takes_carried(self):
+        return (self.z == 0) & (self.section() >= 2)
+
     def crosses(self):
         return (self.z + self.c) % 2 == 1
 
@@ -358,7 +376,9 @@
         if feeding:
             expected = expected + hail_feeding(me, 0, 0) + hail_stagger(me, 0, 1)
         else:
-            expected = expected + hail_stagger(me, line.count - 1, -1)
+            aside = me.yields() | me.carries()
+            pl.when(aside)(lambda: hail(me.flip(y=1)))
+            expected = expected + hail_stagger(me, line.count - 1, -1) + jnp.where(aside, 1, 0)
     pl.semaphore_wait(barrier, expected)
 
 
@@ -514,9 +534,9 @@
 
 def backward_kernel(line, length, turned, acts_h, g_in, x_h, qkv_h, lse_h, h_h, gp_h, words,
                     wqkv_h, wproj_h, wup_h, wdown_h, small_in,
-                    acts_o, home_o, g_o, dz_o, f_o, r_o, gin_o, sums_out,
+                    acts_o, home_o, side_o, g_o, dz_o, f_o, r_o, gin_o, sums_out,
                     wqkv, wproj, wup, wdown, gs, gins, x, qkv, lse, h, gp, dz, f, r, bias, do, dh, dqt, small, sums_o,
-                    w_sem, in_sem, g_sem, load_sem, save_sem, act_sem, send_sem, recv_sem, home_sem, back_sem, token):
+                    w_sem, in_sem, g_sem, load_sem, save_sem, act_sem, send_sem, recv_sem, home_sem, back_sem, side_sem, token):
     micro = gs.shape[0]
     stage = line.stage()
     loads = [
@@ -569,6 +589,13 @@
                 src_ref=gins.at[m], dst_ref=home_o.at[m], send_sem=back_sem.at[0, m], recv_sem=back_sem.at[1, m],
                 device_id=back.id(), device_id_type=MESH)
 
+        near, near_home = me.gives_near(), me.takes_near()
+
+        def aside(m):
+            return pltpu.make_async_remote_copy(
+                src_ref=gins.at[m], dst_ref=side_o.at[m], send_sem=side_sem.at[0, m], recv_sem=side_sem.at[1, m],
+                device_id=me.flip(y=1).id(), device_id_type=MESH)
+
         def settle_back(m):
             return pltpu.make_async_copy(gins.at[m], home_o.at[m], back_sem.at[0, m])
 
@@ -650,9 +677,21 @@
         if turned:
             pl.when(pairs & low & (m < micro - 1))(lambda: home_back(m).start())
             pl.when(alone & low & (m < micro - 1))(lambda: settle_back(m).start())
+            pl.when(me.yields())(lambda: aside(m).start())
         return carry
 
     lax.fori_loop(0, micro, step, 0)
+
+    @pl.when(stage > 0)
+    def _():
+        for m in range(micro):
+            hop(m).wait_send()
+
+    if turned:
+        @pl.when(near)
+        def _():
+            for m in range(micro):
+                home_back(m).start()
     if turned:
         share_small(sums_o, sums_out)
     else:
@@ -665,13 +704,12 @@
         pltpu.make_async_copy(gs.at[m], g_o.at[m], g_sem.at[m]).wait()
         pltpu.make_async_copy(gins.at[m], gin_o.at[m], act_sem.at[m]).wait()
 
-    @pl.when(stage > 0)
-    def _():
-        for m in range(micro):
-            hop(m).wait_send()
-
     for m in range(micro):
         if turned:
+            pl.when(near)(lambda: home_back(m).wait_send())
+            pl.when(near_home)(lambda: home_back(m).wait_recv())
+            pl.when(me.yields())(lambda: aside(m).wait_send())
+            pl.when(me.carries())(lambda: aside(m).wait_recv())
             now, then = low | (m >= EARLY), low_home | (m >= EARLY)
             pl.when(alone & now)(lambda: stay(m).wait())
             pl.when(pairs & now)(lambda: home(m).wait_send())
@@ -723,10 +761,10 @@
     wqkv, wproj, wup, wdown = weights
     return pl.pallas_call(
         functools.partial(backward_kernel, line, length, turned),
-        out_shape=[many, many, many, shape((micro, rows, hidden), BF), many, shape((micro, rows, 3 * width), BF), many,
+        out_shape=[many, many, many, many, shape((micro, rows, hidden), BF), many, shape((micro, rows, 3 * width), BF), many,
                    shape(small.shape, F32)],
         in_specs=[ANYWHERE] * 7 + [IN_VMEM] + [ANYWHERE] * 4 + [IN_VMEM],
-        out_specs=[ANYWHERE] * 7 + [IN_VMEM],
+        out_specs=[ANYWHERE] * 8 + [IN_VMEM],
         scratch_shapes=[pltpu.VMEM(w.shape, BF) for w in weights]
         + [pltpu.VMEM((micro, rows, width), BF)] * 2
         + [pltpu.VMEM((2, rows, width), BF), pltpu.VMEM((2, rows, 3 * width), BF), pltpu.VMEM((2, 16, rows), F32),
@@ -735,7 +773,8 @@
            pltpu.VMEM((rows, rows), F32), pltpu.VMEM((rows, width), BF), pltpu.VMEM((rows, width), F32),
            pltpu.VMEM((width, rows), BF), pltpu.VMEM((16, width), F32), pltpu.VMEM((16, width), F32)]
         + [DMA((4,)), DMA((micro,)), DMA((micro,)), DMA((2, 5)), DMA((2, 3)), DMA((micro,)), DMA((micro,)),
-           DMA((micro,)), DMA((2, micro)), DMA((2, micro)), pltpu.SemaphoreType.REGULAR],
+           DMA((micro,)), DMA((2, micro)), DMA((2, micro)), DMA((2, micro)),
+           pltpu.SemaphoreType.REGULAR],
         compiler_params=pltpu.CompilerParams(
             collective_id=1, has_side_effects=True, vmem_limit_bytes=VMEM_CAP),
         name="backward_line",
@@ -948,10 +987,10 @@
     )(*masters, inputs, g, segs, classes)
 
 
-SCATTER_PIECES = ((3, 0, 128, 0, 768, "x"), (3, 128, 128, 0, 768, "x"), (3, 256, 128, 0, 768, "x"),
-                  (2, 0, 96, 0, 1024, "x"), (2, 0, 96, 1024, 1024, "x"), (2, 0, 96, 2048, 1024, "x"),
-                  (0, 0, 96, 0, 768, "x"), (0, 0, 96, 768, 768, "x"), (0, 0, 96, 1536, 768, "x"),
-                  (1, 0, 96, 0, 768, "x"), (4, 0, 16, 0, 128, "x"))
+SCATTER_PIECES = ((3, 0, 128, 0, 768, "x"), (3, 128, 128, 0, 768, "c"), (3, 256, 128, 0, 768, "x"),
+                  (2, 0, 96, 0, 1024, "c"), (2, 0, 96, 1024, 1024, "x"), (2, 0, 96, 2048, 1024, "c"),
+                  (0, 0, 96, 0, 768, "x"), (0, 0, 96, 768, 768, "c"), (0, 0, 96, 1536, 768, "x"),
+                  (1, 0, 96, 0, 768, "c"), (4, 0, 16, 0, 128, "x"))
 
 
 SCATTER_LAGS = (1, 3, 4, 5)
@@ -959,9 +998,9 @@
 
 def scatter_kernel(pieces, micro, *refs):
     count = 5
-    a_h, r_h, o_h, f_h, a2_h, dz_h, u_h, g_h, small_h, gin_in = refs[:10]
-    outs, gin_o, norm_o = refs[10:15], refs[15], refs[16]
-    at = 17
+    a_h, r_h, o_h, f_h, a2_h, dz_h, u_h, g_h, small_h, gin_in, side_in = refs[:11]
+    outs, gin_o, norm_o = refs[11:16], refs[16], refs[17]
+    at = 18
     totals, beside, diag, from_x, from_y, done, swap, home = (refs[at + i * count : at + (i + 1) * count] for i in range(8))
     (stream, fixed, flipped, sums, tallies, stream_sem, fixed_sem, send, recv, local, turn_sem, note_send, note_recv,
      out_sem) = refs[at + 8 * count :]
@@ -1017,6 +1056,10 @@
     def _():
         hail(back)
         hail(ahead)
+
+    carried_to = Spot(me.x, 1, 0, me.z % 2)
+    pl.when(me.carries())(lambda: hail(carried_to))
+    pl.when(me.takes_carried())(lambda: hail(me.carrier()))
 
     def work(k):
         array, first, size, column_at, columns, _ = pieces[k]
@@ -1099,15 +1142,25 @@
             src_ref=gin_in.at[m], dst_ref=gin_o.at[m], send_sem=turn_sem.at[0, m], recv_sem=turn_sem.at[1, m],
             device_id=back.id(), device_id_type=MESH)
 
+    def carry(m):
+        return pltpu.make_async_remote_copy(
+            src_ref=side_in.at[m], dst_ref=gin_o.at[m], send_sem=turn_sem.at[2, m], recv_sem=turn_sem.at[1, m],
+            device_id=carried_to.id(), device_id_type=MESH)
+
+    gives_now = me.gives_down() & jnp.logical_not(me.gives_near() | me.yields())
+    takes_now = me.takes_down() & jnp.logical_not(me.takes_near())
+
     def turn_stay(m):
         return pltpu.make_async_copy(gin_in.at[m], gin_o.at[m], turn_sem.at[0, m])
 
     work(0)
-    pl.semaphore_wait(pltpu.get_barrier_semaphore(), 10 + jnp.where(stays, 0, 2) + jnp.where(alone, 0, 2))
+    pl.semaphore_wait(pltpu.get_barrier_semaphore(), 10 + jnp.where(stays, 0, 2) + jnp.where(alone, 0, 2)
+                      + jnp.where(me.carries(), 1, 0) + jnp.where(me.takes_carried(), 1, 0))
     for m in range(micro):
-        now = me.gives_down() | (m == micro - 1)
+        now = gives_now | (m == micro - 1) & jnp.logical_not(me.gives_down())
         pl.when(alone & now)(lambda: turn_stay(m).start())
         pl.when(pairs & now)(lambda: turn(m).start())
+        pl.when(me.carries())(lambda: carry(m).start())
     tally = jnp.zeros((8, 128), F32)
     for k in range(len(pieces) + SCATTER_LAGS[3]):
         if k < len(pieces):
@@ -1204,7 +1257,10 @@
         pl.when(moves)(lambda: to_home(k).wait_send())
         pl.when(crosses)(lambda: over(k).wait_send())
     for m in range(micro):
-        now, then = me.gives_down() | (m == micro - 1), me.takes_down() | (m == micro - 1)
+        last_one = m == micro - 1
+        now = gives_now | last_one & jnp.logical_not(me.gives_down())
+        then = takes_now | last_one & jnp.logical_not(me.takes_down())
+        pl.when(me.carries())(lambda: carry(m).wait_send())
         pl.when(alone & now)(lambda: turn_stay(m).wait())
         pl.when(pairs & now)(lambda: turn(m).wait_send())
         pl.when(pairs & then)(lambda: turn(m).wait_recv())
@@ -1212,7 +1268,7 @@
         pltpu.make_async_copy(home[array], outs[array], out_sem.at[array]).wait()
 
 
-def run_scatter(operands, small, gin):
+def run_scatter(operands, small, gin, side):
     pieces = SCATTER_PIECES
     micro = gin.shape[0]
     shape = jax.ShapeDtypeStruct
@@ -1225,16 +1281,16 @@
     return pl.pallas_call(
         functools.partial(scatter_kernel, pieces, micro),
         out_shape=[shape(s, t) for s, t in shares] + [shape(gin.shape, gin.dtype), shape((8, 128), F32)],
-        in_specs=[ANYWHERE] * 10,
+        in_specs=[ANYWHERE] * 11,
         out_specs=[ANYWHERE] * 6 + [IN_VMEM],
         scratch_shapes=[pltpu.VMEM(s, t) for s, t in sizes] + [pltpu.VMEM((4,) + s, t) for s, t in shares] + one * 6
         + [pltpu.VMEM((2, rows, 1024), BF), pltpu.VMEM((4, rows, a.shape[1]), BF), pltpu.VMEM((a.shape[1], rows), BF),
            pltpu.VMEM((2, 8, 128), F32), pltpu.VMEM((10, 8, 128), F32), DMA((2, 8)), DMA((4,)),
-           DMA((9, len(pieces))), DMA((9, len(pieces))), DMA((len(pieces),)), DMA((2, micro)), DMA((10,)), DMA((10,)),
+           DMA((9, len(pieces))), DMA((9, len(pieces))), DMA((len(pieces),)), DMA((3, micro)), DMA((10,)), DMA((10,)),
            DMA((5,))],
         compiler_params=pltpu.CompilerParams(collective_id=3, has_side_effects=True, vmem_limit_bytes=VMEM_CAP),
         name="scatter_layers",
-    )(*operands, small, gin)
+    )(*operands, small, gin, side)
 
 
 def finish_kernel(order, micro, norm, *refs):
@@ -1244,7 +1300,8 @@
     state_o, acts_o, gin_o = refs[20:36], refs[36], refs[37]
     shards, state, (acts, gin, acts_cut, gin_cut, row) = refs[38:42], refs[42:58], refs[58:63]
     load_sem, pick_sem, out_sem = refs[63:]
-    upper = Spot.here().takes_down()
+    me = Spot.here()
+    upper, near = me.takes_down(), me.takes_near()
 
     def loads(array):
         copies = [pltpu.make_async_copy(shards_h[array], shards[array], load_sem.at[array, 0])]
@@ -1261,14 +1318,11 @@
     for array in order:
         for copy in loads(array):
             copy.start()
-    for i, (early, late, dst, is_early) in enumerate(
-            ((acts_early, acts_late, acts, upper), (gin_early, gin_late, gin, jnp.logical_not(upper)))):
-        for m in range(micro):
-            if m >= (EARLY if i == 0 else micro - 1):
-                pick(i, m, late, dst).start()
-            else:
-                pl.when(is_early)(lambda: pick(i, m, early, dst).start())
-                pl.when(jnp.logical_not(is_early))(lambda: pick(i, m, late, dst).start())
+    for m in range(micro):
+        from_early = (upper & (m < EARLY), jnp.logical_not(upper) & (m < micro - 1) | near)
+        for i, (early, late, dst) in enumerate(((acts_early, acts_late, acts), (gin_early, gin_late, gin))):
+            pl.when(from_early[i])(lambda: pick(i, m, early, dst).start())
+            pl.when(jnp.logical_not(from_early[i]))(lambda: pick(i, m, late, dst).start())
     factor = 1.0 / jnp.maximum(norm[0:1, 0:1], 1.0)
     fix = 1.0 / (1.0 - 0.5**STEP)
     strip = 16
@@ -1396,12 +1450,12 @@
 
     x, a, qkv, lse, o, h, a2, gp, u, acts, acts_early = run_forward(
         line, length, turned, x_first, x_in, words, weights, small)
-    acts, gin_early, g, dz, f, r, gin, sums = run_backward(
+    acts, gin_early, side, g, dz, f, r, gin, sums = run_backward(
         line, length, turned, acts, g_in, x, qkv, lse, h, gp, words, weights, small)
     results = []
     if turned:
         matrix_states = [v[0] for group in (masters, firsts, seconds) for v in group[:4]]
-        *shards, table, gin, norm = run_scatter([a, r, o, f, a2, dz, u, g], sums, gin)
+        *shards, table, gin, norm = run_scatter([a, r, o, f, a2, dz, u, g], sums, gin, side)
         grad_norm, *rest = run_finish(norm, table, [masters[4], firsts[4], seconds[4]], shards, matrix_states,
                                       [acts_early, acts, gin_early, gin], length)
         acts, gin = rest[20:]

time: 422 us -> 414 us (0.981)
  Pallas kernels: 413 us -> 406 us
    pallas_call x1, Pallas kernels: 116 us -> 104 us  [run_scatter(): pl.pallas_call(functools.partial(scatter_kernel, pieces, micro), out_shap...]
    pallas_call x1, Pallas kernels: 142 us -> 147 us  [run_backward(): pl.pallas_call(functools.partial(backward_kernel, line, length, turned),...]
where the time goes in v6:
time: 414 us; the launch traced here: 407 us
  Pallas kernels  406 us (98%)
    pallas_call x1, Pallas kernels, run_backward(): pl.pallas_call(functools.partial(backward_kernel, line, length, turned),...  147 us
    pallas_call x1, Pallas kernels, run_scatter(): pl.pallas_call(functools.partial(scatter_kernel, pieces, micro), out_shap...  104 us
    pallas_call x1, Pallas kernels, run_gather(): pl.pallas_call(functools.partial(gather_kernel, pieces, micro), out_shape...  94.8 us
    pallas_call x1, Pallas kernels, run_forward(): pl.pallas_call(functools.partial(forward_kernel, line, length, turned), o...  46.3 us
    pallas_call x1, Pallas kernels, run_finish(): pl.pallas_call(functools.partial(finish_kernel, (1, 0, 2, 3), micro), out...  14.8 us

profile of v6, /device:TPU:0, one launch (start us, length us, event | category | flops | bytes accessed | tf_op | source)
XLA Modules:
  0.0 407.3 jit_solution(11385611242540294549)
XLA Ops:
  0.7 94.8 %gather_layers.1 = (bf16[768,2304]{1,0:T(8,128)(2,1)}, bf16[768,768]{1,0:T(8,128)(2,1)}, bf16[768,3072]{1,0:T(8,128)(2,1)}, bf16[3072,768]{1,0:T(8,128)(2,1)}, f...) custom-call(f32[96,2304]{1,0:T(8,128)} %bitcast.45, ...), custom_call_target="tpu_custom_call" | custom-call | tf_op jit(solution)/shard_map/gather_layers/pallas_call | solution.py:974
  95.5 46.3 %forward_line.1 = (bf16[4,256,768]{2,1,0:T(8,128)(2,1)}, bf16[4,256,768]{2,1,0:T(8,128)(2,1)}, bf16[4,256,2304]{2,1,0:T(8,128)(2,1)}, f32[4,16,256]{2,1,0:T(8,12...) custom-call(bf16[2,256,768]{2,1,0:T(8,128)(2,1)} %get-tuple-element., ...), custom_call_target="tpu_custom_call" | custom-call | tf_op jit(solution)/shard_map/forward_line/pallas_call | solution.py:739
  141.8 146.7 %backward_line.1 = (bf16[4,256,768]{2,1,0:T(8,128)(2,1)}, bf16[4,256,768]{2,1,0:T(8,128)(2,1)}, bf16[4,256,768]{2,1,0:T(8,128)(2,1)}, bf16[4,256,768]{2,1,0:T(8,...) custom-call(bf16[4,256,768]{2,1,0:T(8,128)(2,1)} %get-tuple-element., ...), custom_call_target="tpu_custom_call" | custom-call | tf_op jit(solution)/shard_map/backward_line/pallas_call | solution.py:762
  288.5 103.6 %scatter_layers.1 = (bf16[96,2304]{1,0:T(8,128)(2,1)}, bf16[96,768]{1,0:T(8,128)(2,1)}, bf16[96,3072]{1,0:T(8,128)(2,1)}, bf16[384,768]{1,0:T(8,128)(2,1)}, f32[...) custom-call(bf16[1024,768]{1,0:T(8,128)(2,1)} %bitcast.47, bf16[1024,2304]{1,0:T(8,128)(2,1)} %bitcast.40, ...), custom_call_target="tpu_custom_call" | custom-call | tf_op jit(solution)/shard_map/scatter_layers/pallas_call | solution.py:1281
  392.1 14.8 %finish.1 = (f32[1]{0:T(128)}, f32[1,1152]{1,0:T(1,128)}, f32[1,1152]{1,0:T(1,128)}, f32[1,1152]{1,0:T(1,128)}, f32[1,1152]{1,0:T(1,128)}, /*index=5*/f32[96,230...) custom-call(f32[8,128]{1,0:T(8,128)} %get-tuple-element.108.norm, ...), custom_call_target="tpu_custom_call" | custom-call | tf_op jit(solution)/shard_map/finish/pallas_call | solution.py:1379

commit v7 on v6

--- a/solution.py
+++ b/solution.py
@@ -1315,14 +1315,17 @@
     def saves(array):
         return [pltpu.make_async_copy(state[4 * i + array], state_o[4 * array + i], out_sem.at[array, i]) for i in range(4)]
 
-    for array in order:
+    for array in order[:2]:
         for copy in loads(array):
             copy.start()
-    for m in range(micro):
-        from_early = (upper & (m < EARLY), jnp.logical_not(upper) & (m < micro - 1) | near)
-        for i, (early, late, dst) in enumerate(((acts_early, acts_late, acts), (gin_early, gin_late, gin))):
-            pl.when(from_early[i])(lambda: pick(i, m, early, dst).start())
-            pl.when(jnp.logical_not(from_early[i]))(lambda: pick(i, m, late, dst).start())
+
+    def picks():
+        for m in range(micro):
+            from_early = (upper & (m < EARLY), jnp.logical_not(upper) & (m < micro - 1) | near)
+            for i, (early, late, dst) in enumerate(((acts_early, acts_late, acts), (gin_early, gin_late, gin))):
+                pl.when(from_early[i])(lambda: pick(i, m, early, dst).start())
+                pl.when(jnp.logical_not(from_early[i]))(lambda: pick(i, m, late, dst).start())
+
     factor = 1.0 / jnp.maximum(norm[0:1, 0:1], 1.0)
     fix = 1.0 / (1.0 - 0.5**STEP)
     strip = 16
@@ -1339,9 +1342,14 @@
     small_o[1][...] = small_state[0][...] - small_rate * ((first_new * fix) / (jnp.sqrt(second_new * fix) + adam_eps))
     small_o[2][...] = first_new
     small_o[3][...] = second_new
-    for array in order:
+    for at, array in enumerate(order):
         for copy in loads(array):
             copy.wait()
+        if at + 2 < len(order):
+            for copy in loads(order[at + 2]):
+                copy.start()
+        elif at + 2 == len(order):
+            picks()
         grads, master, first, second = state[array], state[4 + array], state[8 + array], state[12 + array]
 
         def update(i, carry):

time: 414 us -> 412 us (level)
  no operation moved by 1% of the time
where the time goes in v7:
time: 412 us; the launch traced here: 405 us
  Pallas kernels  404 us (98%)
    pallas_call x1, Pallas kernels, run_backward(): pl.pallas_call(functools.partial(backward_kernel, line, length, turned),...  147 us
    pallas_call x1, Pallas kernels, run_scatter(): pl.pallas_call(functools.partial(scatter_kernel, pieces, micro), out_shap...  104 us
    pallas_call x1, Pallas kernels, run_gather(): pl.pallas_call(functools.partial(gather_kernel, pieces, micro), out_shape...  94.8 us
    pallas_call x1, Pallas kernels, run_forward(): pl.pallas_call(functools.partial(forward_kernel, line, length, turned), o...  46.3 us
    pallas_call x1, Pallas kernels, run_finish(): pl.pallas_call(functools.partial(finish_kernel, (1, 0, 2, 3), micro), out...  12.8 us

profile of v7, /device:TPU:0, one launch (start us, length us, event | category | flops | bytes accessed | tf_op | source)
XLA Modules:
  0.0 405.4 jit_solution(15628620071427313494)
XLA Ops:
  0.7 94.8 %gather_layers.1 = (bf16[768,2304]{1,0:T(8,128)(2,1)}, bf16[768,768]{1,0:T(8,128)(2,1)}, bf16[768,3072]{1,0:T(8,128)(2,1)}, bf16[3072,768]{1,0:T(8,128)(2,1)}, f...) custom-call(f32[96,2304]{1,0:T(8,128)} %bitcast.45, ...), custom_call_target="tpu_custom_call" | custom-call | tf_op jit(solution)/shard_map/gather_layers/pallas_call | solution.py:974
  95.5 46.3 %forward_line.1 = (bf16[4,256,768]{2,1,0:T(8,128)(2,1)}, bf16[4,256,768]{2,1,0:T(8,128)(2,1)}, bf16[4,256,2304]{2,1,0:T(8,128)(2,1)}, f32[4,16,256]{2,1,0:T(8,12...) custom-call(bf16[2,256,768]{2,1,0:T(8,128)(2,1)} %get-tuple-element., ...), custom_call_target="tpu_custom_call" | custom-call | tf_op jit(solution)/shard_map/forward_line/pallas_call | solution.py:739
  141.8 146.7 %backward_line.1 = (bf16[4,256,768]{2,1,0:T(8,128)(2,1)}, bf16[4,256,768]{2,1,0:T(8,128)(2,1)}, bf16[4,256,768]{2,1,0:T(8,128)(2,1)}, bf16[4,256,768]{2,1,0:T(8,...) custom-call(bf16[4,256,768]{2,1,0:T(8,128)(2,1)} %get-tuple-element., ...), custom_call_target="tpu_custom_call" | custom-call | tf_op jit(solution)/shard_map/backward_line/pallas_call | solution.py:762
  288.5 103.6 %scatter_layers.1 = (bf16[96,2304]{1,0:T(8,128)(2,1)}, bf16[96,768]{1,0:T(8,128)(2,1)}, bf16[96,3072]{1,0:T(8,128)(2,1)}, bf16[384,768]{1,0:T(8,128)(2,1)}, f32[...) custom-call(bf16[1024,768]{1,0:T(8,128)(2,1)} %bitcast.47, bf16[1024,2304]{1,0:T(8,128)(2,1)} %bitcast.40, ...), custom_call_target="tpu_custom_call" | custom-call | tf_op jit(solution)/shard_map/scatter_layers/pallas_call | solution.py:1281
  392.1 12.8 %finish.1 = (f32[1]{0:T(128)}, f32[1,1152]{1,0:T(1,128)}, f32[1,1152]{1,0:T(1,128)}, f32[1,1152]{1,0:T(1,128)}, f32[1,1152]{1,0:T(1,128)}, /*index=5*/f32[96,230...) custom-call(f32[8,128]{1,0:T(8,128)} %get-tuple-element.108.norm, ...), custom_call_target="tpu_custom_call" | custom-call | tf_op jit(solution)/shard_map/finish/pallas_call | solution.py:1387
